TPU v7x, 32 devices: a whole 2x2x4 slice. The times are simulated.
32 devices in a mesh: dp: 4 (over y, core), seq: 8 (over z, x).
Axes of the slice: x: 2, y: 2, z: 4, core: 2. Of those that a mesh axis runs over, the one named last changes fastest.
Arguments:
- embedding: bfloat16 [8, 512, 1024], P('dp', 'seq'), may hold values from -6 to 6
- latent: bfloat16 [8, 512, 1024], P('dp', 'seq'), may hold values from -6 to 6
- segment_ids: int32 [8, 512], P('dp', 'seq'), may hold values from 0 to 5, as said below
- cotangent: bfloat16 [8, 512, 1024], P('dp', 'seq'), may hold values from -6 to 6
- weight_adapt: float32 [2048, 1024], P(('dp', 'seq')), may hold values from -0.125 to 0.125
- weight_attn: float32 [4, 1024, 1024], P(None, ('dp', 'seq')), may hold values from -0.1875 to 0.1875
- weight_gateup: float32 [2, 1024, 2816], P(None, ('dp', 'seq')), may hold values from -0.1875 to 0.1875
- weight_down: float32 [2816, 1024], P(('dp', 'seq')), may hold values from -0.109375 to 0.109375
- norm_gains: float32 [4, 1024], P(None, ('dp', 'seq')), may hold values from 0.5 to 1.5
- left_adapt: float32 [2048, 2048], P(('dp', 'seq')), may hold values from 0 to 4
- right_adapt: float32 [1024, 1024], P(('dp', 'seq')), may hold values from 0 to 4
- left_attn: float32 [4, 1024, 1024], P(None, ('dp', 'seq')), may hold values from 0 to 4
- right_attn: float32 [4, 1024, 1024], P(None, ('dp', 'seq')), may hold values from 0 to 4
- left_gateup: float32 [2, 1024, 1024], P(None, ('dp', 'seq')), may hold values from 0 to 4
- right_gateup: float32 [2, 2816, 2816], P(None, ('dp', 'seq')), may hold values from 0 to 4
- left_down: float32 [2816, 2816], P(('dp', 'seq')), may hold values from 0 to 4
- right_down: float32 [1024, 1024], P(('dp', 'seq')), may hold values from 0 to 4
- left_root_adapt: float32 [2048, 2048], P(('dp', 'seq')), may hold values from -1 to 2, as said below
- right_root_adapt: float32 [1024, 1024], P(('dp', 'seq')), may hold values from -1 to 2, as said below
- left_root_attn: float32 [4, 1024, 1024], P(None, ('dp', 'seq')), may hold values from -1 to 2, as said below
- right_root_attn: float32 [4, 1024, 1024], P(None, ('dp', 'seq')), may hold values from -1 to 2, as said below
- left_root_gateup: float32 [2, 1024, 1024], P(None, ('dp', 'seq')), may hold values from -1 to 2, as said below
- right_root_gateup: float32 [2, 2816, 2816], P(None, ('dp', 'seq')), may hold values from -1 to 2, as said below
- left_root_down: float32 [2816, 2816], P(('dp', 'seq')), may hold values from -1 to 2, as said below
- right_root_down: float32 [1024, 1024], P(('dp', 'seq')), may hold values from -1 to 2, as said below
- gain_moment: float32 [4, 1024], P(None, ('dp', 'seq')), may hold values from 1 to 4
Outputs:
- latent_out: bfloat16 [8, 512, 1024], P('dp', 'seq')
- grad_embedding: float32 [8, 512, 1024], P('dp', 'seq')
- grad_adapt: float32 [2048, 1024], P(('dp', 'seq'))
- grad_attn: float32 [4, 1024, 1024], P(None, ('dp', 'seq'))
- grad_gateup: float32 [2, 1024, 2816], P(None, ('dp', 'seq'))
- grad_down: float32 [2816, 1024], P(('dp', 'seq'))
- grad_gains: float32 [4, 1024], P(None, ('dp', 'seq'))
- new_left_adapt: float32 [2048, 2048], P(('dp', 'seq'))
- new_right_adapt: float32 [1024, 1024], P(('dp', 'seq'))
- new_left_attn: float32 [4, 1024, 1024], P(None, ('dp', 'seq'))
- new_right_attn: float32 [4, 1024, 1024], P(None, ('dp', 'seq'))
- new_left_gateup: float32 [2, 1024, 1024], P(None, ('dp', 'seq'))
- new_right_gateup: float32 [2, 2816, 2816], P(None, ('dp', 'seq'))
- new_left_down: float32 [2816, 2816], P(('dp', 'seq'))
- new_right_down: float32 [1024, 1024], P(('dp', 'seq'))
- new_adapt: float32 [2048, 1024], P(('dp', 'seq'))
- new_attn: float32 [4, 1024, 1024], P(None, ('dp', 'seq'))
- new_gateup: float32 [2, 1024, 2816], P(None, ('dp', 'seq'))
- new_down: float32 [2816, 1024], P(('dp', 'seq'))
- new_gain_moment: float32 [4, 1024], P(None, ('dp', 'seq'))
- new_norm_gains: float32 [4, 1024], P(None, ('dp', 'seq'))
Inputs may be any that keep to these rules, and one draw needn't show every extreme that they name: `segment_ids`: along each sequence the ids never fall and start at 0. Among the 2 sequences of each index of dp, one is a single document. `left_root_adapt`: Symmetric. `right_root_adapt`: Symmetric. `left_root_attn`: Symmetric. `right_root_attn`: Symmetric. `left_root_gateup`: Symmetric. `right_root_gateup`: Symmetric. `left_root_down`: Symmetric. `right_root_down`: Symmetric.
All inputs are finite; a program needn't handle non-finite values.
Results may differ from a plain program's by a relative error of at most 0.028.
Values may be sent and summed in bfloat16 or wider, within the bound.
No kernel may reach another device: no remote copies, remote signals or barrier semaphores. Data moves between devices by JAX's collectives and lax.ppermute only.
A program may use at most 320 MiB of HBM per device.

v0:
```python
import math

import jax
import jax.numpy as jnp
from jax import lax
from jax.sharding import PartitionSpec as P

HEADS = 8
HEAD_DIM = 128


EPSILON = 1e-06
THETA = 50000.0
HIGHEST = lax.Precision.HIGHEST


def product(left_side, right_side):
    return jnp.dot(left_side, right_side, preferred_element_type=jnp.float32)


def across(left_side, right_side):
    return lax.dot_general(
        left_side, right_side, (((0,), (0,)), ((), ())), preferred_element_type=jnp.float32
    )


def against(left_side, right_side):
    return lax.dot_general(
        left_side, right_side, (((1,), (1,)), ((), ())), preferred_element_type=jnp.float32
    )


def precise(left_side, right_side):
    return jnp.dot(left_side, right_side, precision=HIGHEST, preferred_element_type=jnp.float32)


def precise_across(left_side, right_side):
    return lax.dot_general(
        left_side,
        right_side,
        (((0,), (0,)), ((), ())),
        precision=HIGHEST,
        preferred_element_type=jnp.float32,
    )


def precise_against(left_side, right_side):
    return lax.dot_general(
        left_side,
        right_side,
        (((1,), (1,)), ((), ())),
        precision=HIGHEST,
        preferred_element_type=jnp.float32,
    )


def norm_scale(values):
    return lax.rsqrt(jnp.mean(values * values, axis=-1, keepdims=True) + EPSILON)


def norm_back(values, scaling, gain_row, gradient):
    unit_rows = values * scaling
    weighted = gradient * gain_row
    moved = scaling * (
        weighted - unit_rows * jnp.mean(unit_rows * weighted, axis=-1, keepdims=True)
    )
    return (moved, jnp.sum(gradient * unit_rows, axis=0))


def rotate(values, cosine, sine_table):
    half_dim = values.shape[-1] // 2
    first_half = values[..., :half_dim]
    second_half = values[..., half_dim:]
    return jnp.concatenate(
        [
            first_half * cosine - second_half * sine_table,
            second_half * cosine + first_half * sine_table,
        ],
        axis=-1,
    )


def silu_grad(values):
    sigmoid_value = jax.nn.sigmoid(values)
    return sigmoid_value * (1.0 + values * (1.0 - sigmoid_value))


def masked_scores(queries, keys_whole, query_places, segment_query, segment_keys):
    length = keys_whole.shape[0]
    scores = jnp.einsum("chd,rhd->hcr", queries, keys_whole, preferred_element_type=jnp.float32) * (
        1.0 / math.sqrt(queries.shape[-1])
    )
    key_places = jnp.arange(length, dtype=jnp.int32)
    allowed = (key_places[None, :] <= query_places[:, None]) & (
        segment_keys[None, :] == segment_query[:, None]
    )
    return jnp.where(allowed[None], scores, -1e30)


def body(
    embedding,
    latent,
    segment_ids,
    cotangent,
    weight_adapt,
    weight_attn,
    weight_gateup,
    weight_down,
    norm_gains,
    left_adapt,
    right_adapt,
    left_attn,
    right_attn,
    left_gateup,
    right_gateup,
    left_down,
    right_down,
    left_root_adapt,
    right_root_adapt,
    left_root_attn,
    right_root_attn,
    left_root_gateup,
    right_root_gateup,
    left_root_down,
    right_root_down,
    gain_moment,
):
    adapt_full, attn_full, gateup_full, down_full, gain_full = (
        lax.all_gather(weight_adapt.astype(jnp.bfloat16), ("dp", "seq"), axis=0, tiled=True),
        lax.all_gather(weight_attn.astype(jnp.bfloat16), ("dp", "seq"), axis=1, tiled=True),
        lax.all_gather(weight_gateup.astype(jnp.bfloat16), ("dp", "seq"), axis=1, tiled=True),
        lax.all_gather(weight_down.astype(jnp.bfloat16), ("dp", "seq"), axis=0, tiled=True),
        lax.all_gather(norm_gains.astype(jnp.bfloat16), ("dp", "seq"), axis=1, tiled=True),
    )
    gain_values = gain_full.astype(jnp.float32)
    seq_count, group_len, model_width = embedding.shape
    tokens = seq_count * group_len
    head_shape = (seq_count, group_len, HEADS, HEAD_DIM)
    segment_whole = lax.all_gather(segment_ids, "seq", axis=1, tiled=True)
    length = segment_whole.shape[1]
    query_places = lax.axis_index("seq") * group_len + jnp.arange(group_len, dtype=jnp.int32)
    doc_starts = jnp.sum(
        (segment_whole[:, None, :] < segment_ids[:, :, None]).astype(jnp.int32), axis=2
    )
    places = query_places[None, :] - doc_starts
    half_dim = HEAD_DIM // 2
    frequency = THETA ** (-jnp.arange(half_dim, dtype=jnp.float32) / half_dim)
    angles = places.astype(jnp.float32)[..., None] * frequency
    cosine = jnp.cos(angles)[:, :, None, :]
    sine_table = jnp.sin(angles)[:, :, None, :]
    embed_flat = embedding.reshape(tokens, model_width)

    def one_sequence(seq_items):
        query_seq, key_seq, value_seq, segment_query, segment_keys = seq_items
        keys_whole, values_whole = (
            lax.all_gather(key_seq, "seq", axis=0, tiled=True),
            lax.all_gather(value_seq, "seq", axis=0, tiled=True),
        )
        scores = masked_scores(query_seq, keys_whole, query_places, segment_query, segment_keys)
        row_top = jnp.max(scores, axis=-1)
        exponent = jnp.exp(scores - row_top[..., None])
        row_total = jnp.sum(exponent, axis=-1)
        soft_weights = (exponent / row_total[..., None]).astype(jnp.bfloat16)
        mixed_seq = jnp.einsum(
            "hcr,rhd->chd", soft_weights, values_whole, preferred_element_type=jnp.float32
        ).astype(jnp.bfloat16)
        return (mixed_seq, row_top, row_total)

    def forward(latent_state):
        joined = jnp.concatenate([latent_state.astype(jnp.bfloat16), embed_flat], axis=1)
        start_sum = product(joined, adapt_full)
        scale_one = norm_scale(start_sum)
        normed_one = (start_sum * scale_one * gain_values[0]).astype(jnp.bfloat16)
        queries = rotate(
            product(normed_one, attn_full[0]).reshape(head_shape), cosine, sine_table
        ).astype(jnp.bfloat16)
        keys_local = rotate(
            product(normed_one, attn_full[1]).reshape(head_shape), cosine, sine_table
        ).astype(jnp.bfloat16)
        values_local = product(normed_one, attn_full[2]).astype(jnp.bfloat16).reshape(head_shape)
        attended = lax.map(
            one_sequence, (queries, keys_local, values_local, segment_ids, segment_whole)
        )
        mixed_heads = attended[0].reshape(tokens, model_width)
        branch = product(mixed_heads, attn_full[3])
        scale_two = norm_scale(branch)
        middle = start_sum + branch * scale_two * gain_values[1]
        scale_three = norm_scale(middle)
        normed_three = (middle * scale_three * gain_values[2]).astype(jnp.bfloat16)
        gate_value = product(normed_three, gateup_full[0])
        upward = product(normed_three, gateup_full[1])
        hidden = (jax.nn.silu(gate_value) * upward).astype(jnp.bfloat16)
        feed_out = product(hidden, down_full)
        scale_four = norm_scale(feed_out)
        result = middle + feed_out * scale_four * gain_values[3]
        saved_values = (
            joined,
            start_sum,
            scale_one,
            normed_one,
            queries,
            keys_local,
            values_local,
            attended,
            mixed_heads,
            branch,
            scale_two,
            middle,
            scale_three,
            normed_three,
            gate_value,
            upward,
            hidden,
            feed_out,
            scale_four,
        )
        return (result, saved_values)

    latent_state = latent.astype(jnp.float32).reshape(tokens, model_width)
    latent_state, unused_saved = forward(latent_state)
    final_state, saved_values = forward(latent_state)
    (
        joined,
        start_sum,
        scale_one,
        normed_one,
        queries,
        keys_local,
        values_local,
        attended,
        mixed_heads,
        branch,
        scale_two,
        middle,
        scale_three,
        normed_three,
        gate_value,
        upward,
        hidden,
        feed_out,
        scale_four,
    ) = saved_values
    incoming = cotangent.astype(jnp.float32).reshape(tokens, model_width)
    feed_grad, gain_four = norm_back(feed_out, scale_four, gain_values[3], incoming)
    feed_grad = feed_grad.astype(jnp.bfloat16)
    grad_down = across(hidden, feed_grad)
    hidden_grad = against(feed_grad, down_full)
    gate_grad = (hidden_grad * upward * silu_grad(gate_value)).astype(jnp.bfloat16)
    up_grad = (hidden_grad * jax.nn.silu(gate_value)).astype(jnp.bfloat16)
    grad_gateup = jnp.stack([across(normed_three, gate_grad), across(normed_three, up_grad)])
    normed_three_grad = against(gate_grad, gateup_full[0]) + against(up_grad, gateup_full[1])
    middle_grad, gain_three = norm_back(middle, scale_three, gain_values[2], normed_three_grad)
    middle_grad = middle_grad + incoming
    branch_grad, gain_two = norm_back(branch, scale_two, gain_values[1], middle_grad)
    branch_grad = branch_grad.astype(jnp.bfloat16)
    grad_output_proj = across(mixed_heads, branch_grad)
    mixed_grad = against(branch_grad, attn_full[3]).astype(jnp.bfloat16).reshape(head_shape)

    def back_sequence(seq_items):
        query_seq, grad_seq, row_top, row_total, segment_query, segment_keys, key_seq, value_seq = (
            seq_items
        )
        keys_whole, values_whole = (
            lax.all_gather(key_seq, "seq", axis=0, tiled=True),
            lax.all_gather(value_seq, "seq", axis=0, tiled=True),
        )
        scores = masked_scores(query_seq, keys_whole, query_places, segment_query, segment_keys)
        soft_full = jnp.exp(scores - row_top[..., None]) / row_total[..., None]
        soft_low = soft_full.astype(jnp.bfloat16)
        soft_grad = jnp.einsum(
            "chd,rhd->hcr", grad_seq, values_whole, preferred_element_type=jnp.float32
        )
        inner_sum = jnp.sum(soft_full * soft_grad, axis=-1, keepdims=True)
        score_grad = (soft_full * (soft_grad - inner_sum)).astype(jnp.bfloat16)
        scaling = 1.0 / math.sqrt(query_seq.shape[-1])
        query_grad = (
            jnp.einsum("hcr,rhd->chd", score_grad, keys_whole, preferred_element_type=jnp.float32)
            * scaling
        )
        key_term = (
            jnp.einsum("hcr,chd->rhd", score_grad, query_seq, preferred_element_type=jnp.float32)
            * scaling
        )
        value_term = jnp.einsum(
            "hcr,chd->rhd", soft_low, grad_seq, preferred_element_type=jnp.float32
        )
        key_grad, value_grad = (
            lax.psum_scatter(
                key_term.astype(jnp.bfloat16), "seq", scatter_dimension=0, tiled=True
            ).astype(jnp.float32),
            lax.psum_scatter(
                value_term.astype(jnp.bfloat16), "seq", scatter_dimension=0, tiled=True
            ).astype(jnp.float32),
        )
        return (query_grad, key_grad, value_grad)

    back_items = (
        queries,
        mixed_grad,
        attended[1],
        attended[2],
        segment_ids,
        segment_whole,
        keys_local,
        values_local,
    )
    query_grad, key_grad, value_grad = lax.map(back_sequence, back_items)
    query_pre = (
        rotate(query_grad, cosine, -sine_table).astype(jnp.bfloat16).reshape(tokens, model_width)
    )
    key_pre = (
        rotate(key_grad, cosine, -sine_table).astype(jnp.bfloat16).reshape(tokens, model_width)
    )
    value_pre = value_grad.astype(jnp.bfloat16).reshape(tokens, model_width)
    grad_attn = jnp.stack(
        [
            across(normed_one, query_pre),
            across(normed_one, key_pre),
            across(normed_one, value_pre),
            grad_output_proj,
        ]
    )
    normed_one_grad = (
        against(query_pre, attn_full[0])
        + against(key_pre, attn_full[1])
        + against(value_pre, attn_full[2])
    )
    start_grad, gain_one = norm_back(start_sum, scale_one, gain_values[0], normed_one_grad)
    start_grad = (start_grad + middle_grad).astype(jnp.bfloat16)
    grad_adapt = across(joined, start_grad)
    grad_embedding = against(start_grad, adapt_full[model_width:]).reshape(
        seq_count, group_len, model_width
    )
    grad_gains = jnp.stack([gain_one, gain_two, gain_three, gain_four])
    reduced_adapt, reduced_attn, reduced_gateup, reduced_down, reduced_gains = (
        lax.psum_scatter(grad_adapt, ("dp", "seq"), scatter_dimension=0, tiled=True),
        lax.psum_scatter(grad_attn, ("dp", "seq"), scatter_dimension=1, tiled=True),
        lax.psum_scatter(grad_gateup, ("dp", "seq"), scatter_dimension=1, tiled=True),
        lax.psum_scatter(grad_down, ("dp", "seq"), scatter_dimension=0, tiled=True),
        lax.psum_scatter(grad_gains, ("dp", "seq"), scatter_dimension=1, tiled=True),
    )
    factor = 1.0 / math.sqrt(seq_count * lax.axis_size("dp") * length)
    reduced_adapt = reduced_adapt * factor
    reduced_attn = reduced_attn * factor
    reduced_gateup = reduced_gateup * factor
    reduced_down = reduced_down * factor
    reduced_gains = reduced_gains * factor
    position = lax.axis_index(("dp", "seq"))
    full_adapt, full_attn, full_gateup, full_down = (
        lax.all_gather(
            reduced_adapt.astype(jnp.bfloat16), ("dp", "seq"), axis=0, tiled=True
        ).astype(reduced_adapt.dtype),
        lax.all_gather(reduced_attn.astype(jnp.bfloat16), ("dp", "seq"), axis=1, tiled=True).astype(
            reduced_attn.dtype
        ),
        lax.all_gather(
            reduced_gateup.astype(jnp.bfloat16), ("dp", "seq"), axis=1, tiled=True
        ).astype(reduced_gateup.dtype),
        lax.all_gather(reduced_down.astype(jnp.bfloat16), ("dp", "seq"), axis=0, tiled=True).astype(
            reduced_down.dtype
        ),
    )

    def refresh(shard, whole_grad, left_stat, right_stat, left_root):
        row_count, col_count = whole_grad.shape
        new_left = 0.5 * left_stat + 0.5 * precise_against(shard, whole_grad) / col_count
        count = right_stat.shape[0]
        columns = lax.dynamic_slice_in_dim(whole_grad, position * count, count, 1)
        new_right = 0.5 * right_stat + 0.5 * precise_across(columns, whole_grad) / row_count
        return (new_left, new_right, precise(left_root, whole_grad))

    new_left_adapt, new_right_adapt, left_adapt_part = refresh(
        reduced_adapt, full_adapt, left_adapt, right_adapt, left_root_adapt
    )
    attn_parts = [
        refresh(
            reduced_attn[index],
            full_attn[index],
            left_attn[index],
            right_attn[index],
            left_root_attn[index],
        )
        for index in range(4)
    ]
    gateup_parts = [
        refresh(
            reduced_gateup[index],
            full_gateup[index],
            left_gateup[index],
            right_gateup[index],
            left_root_gateup[index],
        )
        for index in range(2)
    ]
    new_left_down, new_right_down, left_down_part = refresh(
        reduced_down, full_down, left_down, right_down, left_root_down
    )
    new_left_attn = jnp.stack([member[0] for member in attn_parts])
    new_right_attn = jnp.stack([member[1] for member in attn_parts])
    left_attn_part = jnp.stack([member[2] for member in attn_parts])
    new_left_gateup = jnp.stack([member[0] for member in gateup_parts])
    new_right_gateup = jnp.stack([member[1] for member in gateup_parts])
    left_gateup_part = jnp.stack([member[2] for member in gateup_parts])
    root_stack = jnp.concatenate(
        [right_root_adapt[None], right_root_attn, right_root_down[None]], axis=0
    )
    piece = lax.all_gather(
        root_stack.astype(jnp.bfloat16), ("dp", "seq"), axis=1, tiled=True
    ).astype(jnp.float32)
    count = piece.shape[1]
    sum_adapt = precise(left_adapt_part, piece[0])
    sum_attn = jnp.einsum(
        "mik,mkj->mij",
        left_attn_part,
        piece[1:5],
        precision=HIGHEST,
        preferred_element_type=jnp.float32,
    )
    sum_down = precise(left_down_part, piece[5])
    piece = lax.all_gather(
        right_root_gateup.astype(jnp.bfloat16), ("dp", "seq"), axis=1, tiled=True
    ).astype(jnp.float32)
    count = piece.shape[1]
    step_gateup = jnp.einsum(
        "mik,mkj->mij",
        left_gateup_part,
        piece,
        precision=HIGHEST,
        preferred_element_type=jnp.float32,
    )
    new_adapt = weight_adapt - sum_adapt / math.sqrt(full_adapt.shape[0])
    new_attn = weight_attn - sum_attn / math.sqrt(full_attn.shape[1])
    new_gateup = weight_gateup - step_gateup / math.sqrt(full_gateup.shape[1])
    new_down = weight_down - sum_down / math.sqrt(full_down.shape[0])
    new_gain_moment = 0.5 * gain_moment + 0.5 * reduced_gains * reduced_gains
    new_norm_gains = norm_gains - 0.5 * reduced_gains / (jnp.sqrt(new_gain_moment) + 1e-08)
    latent_out = final_state.reshape(seq_count, group_len, model_width).astype(jnp.bfloat16)
    return (
        latent_out,
        grad_embedding,
        reduced_adapt,
        reduced_attn,
        reduced_gateup,
        reduced_down,
        reduced_gains,
        new_left_adapt,
        new_right_adapt,
        new_left_attn,
        new_right_attn,
        new_left_gateup,
        new_right_gateup,
        new_left_down,
        new_right_down,
        new_adapt,
        new_attn,
        new_gateup,
        new_down,
        new_gain_moment,
        new_norm_gains,
    )


def solution(mesh):
    return jax.shard_map(
        body,
        mesh=mesh,
        in_specs=(
            P("dp", "seq", None),
            P("dp", "seq", None),
            P("dp", "seq"),
            P("dp", "seq", None),
            P(("dp", "seq"), None),
            P(None, ("dp", "seq"), None),
            P(None, ("dp", "seq"), None),
            P(("dp", "seq"), None),
            P(None, ("dp", "seq")),
            P(("dp", "seq"), None),
            P(("dp", "seq"), None),
            P(None, ("dp", "seq"), None),
            P(None, ("dp", "seq"), None),
            P(None, ("dp", "seq"), None),
            P(None, ("dp", "seq"), None),
            P(("dp", "seq"), None),
            P(("dp", "seq"), None),
            P(("dp", "seq"), None),
            P(("dp", "seq"), None),
            P(None, ("dp", "seq"), None),
            P(None, ("dp", "seq"), None),
            P(None, ("dp", "seq"), None),
            P(None, ("dp", "seq"), None),
            P(("dp", "seq"), None),
            P(("dp", "seq"), None),
            P(None, ("dp", "seq")),
        ),
        out_specs=(
            P("dp", "seq", None),
            P("dp", "seq", None),
            P(("dp", "seq"), None),
            P(None, ("dp", "seq"), None),
            P(None, ("dp", "seq"), None),
            P(("dp", "seq"), None),
            P(None, ("dp", "seq")),
            P(("dp", "seq"), None),
            P(("dp", "seq"), None),
            P(None, ("dp", "seq"), None),
            P(None, ("dp", "seq"), None),
            P(None, ("dp", "seq"), None),
            P(None, ("dp", "seq"), None),
            P(("dp", "seq"), None),
            P(("dp", "seq"), None),
            P(("dp", "seq"), None),
            P(None, ("dp", "seq"), None),
            P(None, ("dp", "seq"), None),
            P(("dp", "seq"), None),
            P(None, ("dp", "seq")),
            P(None, ("dp", "seq")),
        ),
        check_vma=False,
    )
```

profile of v0, /device:TPU:0, one launch (start us, length us, event | category | flops | bytes accessed | tf_op | source)
XLA Modules:
  0.0 3241.5 jit_solution(12555690918134397765)
XLA Ops:
  11.5 69.8 %all-gather.6 = bf16[32,32,4]{1,2,0:T(4,128)(2,1)S(1)} all-gather(bf16[1,32,4]{1,2,0:T(4,128)(2,1)S(1)} %convert_bitcast_fusion.2), channel_id=1, replica_groups=mesh['dp'=4,'seq'=8] {'dp','seq'}, dimensions={0}, use_global_device_ids=true | all-gather | bytes 8448 | tf_op jit(solution)/shard_map/all_gather | solution.py:133
  106.6 49.8 %all-gather.45.cloned.1.call-done = bf16[4,1024,1024]{2,1,0:T(8,128)(2,1)} async-done(((bf16[4,32,1024]{2,1,0:T(8,128)(2,1)}), bf16[4,1024,1024]{2,1,0:T(8,128)(2,1)}) %all-gather.45.cloned.1.call-update) | async-done | bytes 8388624 | tf_op jit(solution)/shard_map/all_gather | solution.py:130
  176.4 174.8 %while.41 = (s32[]{:T(128)}, bf16[2,64,8,128]{3,2,1,0:T(8,128)(2,1)}, bf16[2,64,8,128]{3,2,1,0:T(8,128)(2,1)S(1)}, s32[2,512]{1,0:T(2,128)}, s32[2,64]{1,0:T(2,1...) while((s32[]{:T(128)}, ...), condition=%wide.region_5.6_spmd.clone, body=%wide.region_2.5_spmd.clone.sunk | while | flops 136218176 | bytes 13708753 | solution.py:181
  355.4 90.1 %all-gather.47.cloned.1.call-done = bf16[2,1024,2816]{2,1,0:T(8,128)(2,1)} async-done(((bf16[2,32,2816]{2,1,0:T(8,128)(2,1)}), bf16[2,1024,2816]{2,1,0:T(8,128)(2,1)}) %all-gather.47.cloned.1.call-update) | async-done | bytes 11534352 | tf_op jit(solution)/shard_map/all_gather | solution.py:131
  450.2 64.5 %all-gather.49.cloned.1.call-done = bf16[2816,1024]{1,0:T(8,128)(2,1)} async-done(((bf16[88,1024]{1,0:T(8,128)(2,1)}), bf16[2816,1024]{1,0:T(8,128)(2,1)}) %all-gather.49.cloned.1.call-update) | async-done | bytes 5767184 | tf_op jit(solution)/shard_map/all_gather | solution.py:132
  530.5 174.8 %while.42 = (s32[]{:T(128)}, bf16[2,64,8,128]{3,2,1,0:T(8,128)(2,1)}, f32[2,8,64]{2,1,0:T(8,128)}, f32[2,8,64]{2,1,0:T(8,128)}, bf16[2,64,8,128]{3,1,2,0:T(8,128...) while((s32[]{:T(128)}, ...), condition=%wide.region_13.14_spmd.clone, body=%wide.region_10.13_spmd.clone.sunk | while | flops 136477760 | bytes 15562269 | solution.py:181
  533.8 40.0 %all-gather.69.cloned.1.call-done = bf16[1,512,8,128]{3,1,2,0:T(8,128)(2,1)} async-done(((bf16[1,64,8,128]{3,1,2,0:T(8,128)(2,1)}), bf16[1,512,8,128]{3,1,2,0:T(8,128)(2,1)}) %all-gather.69.cloned.1.call-update) | async-done | bytes 1048592 | tf_op jit(solution)/shard_map/while/body/eval_jaxpr/all_gather | solution.py:156
  621.1 39.8 %all-gather.69.cloned.1.call-done = bf16[1,512,8,128]{3,1,2,0:T(8,128)(2,1)} async-done(((bf16[1,64,8,128]{3,1,2,0:T(8,128)(2,1)}), bf16[1,512,8,128]{3,1,2,0:T(8,128)(2,1)}) %all-gather.69.cloned.1.call-update) | async-done | bytes 1048592 | tf_op jit(solution)/shard_map/while/body/eval_jaxpr/all_gather | solution.py:156
  732.0 452.7 %while.43 = (s32[]{:T(128)}, f32[2,64,8,128]{3,1,2,0:T(8,128)}, f32[2,64,8,128]{3,1,2,0:T(8,128)}, bf16[2,64,8,128]{3,2,1,0:T(8,128)(2,1)}, bf16[2,64,8,128]{3,1...) while((s32[]{:T(128)}, f32[2,64,8,128]{3,1,2,0:T(8,128)}, ...), condition=%wide.region_24.25_spmd.clone, body=%wide.region_20.24_spmd.clone.sunk | while | flops 340033088 | bytes 44920552 | solution.py:307
  840.5 56.1 %reduce-scatter.20.cloned.1.call-done = bf16[64,8,128]{2,1,0:T(8,128)(2,1)} async-done(((bf16[512,8,128]{2,1,0:T(8,128)(2,1)}), bf16[64,8,128]{2,1,0:T(8,128)(2,1)}) %reduce-scatter.20.cloned.1.call-update) | async-done | bytes 131088 | tf_op jit(solution)/shard_map/while/body/eval_jaxpr/reduce_scatter | solution.py:288
  897.7 64.8 %reduce-scatter.22.cloned.1.call-done = bf16[64,8,128]{2,1,0:T(8,128)(2,1)} async-done(((bf16[512,8,128]{2,1,0:T(8,128)(2,1)}), bf16[64,8,128]{2,1,0:T(8,128)(2,1)}) %reduce-scatter.22.cloned.1.call-update) | async-done | bytes 131088 | tf_op jit(solution)/shard_map/while/body/eval_jaxpr/reduce_scatter | solution.py:291
  1061.4 56.1 %reduce-scatter.20.cloned.1.call-done = bf16[64,8,128]{2,1,0:T(8,128)(2,1)} async-done(((bf16[512,8,128]{2,1,0:T(8,128)(2,1)}), bf16[64,8,128]{2,1,0:T(8,128)(2,1)}) %reduce-scatter.20.cloned.1.call-update) | async-done | bytes 131088 | tf_op jit(solution)/shard_map/while/body/eval_jaxpr/reduce_scatter | solution.py:288
  1118.5 64.7 %reduce-scatter.22.cloned.1.call-done = bf16[64,8,128]{2,1,0:T(8,128)(2,1)} async-done(((bf16[512,8,128]{2,1,0:T(8,128)(2,1)}), bf16[64,8,128]{2,1,0:T(8,128)(2,1)}) %reduce-scatter.22.cloned.1.call-update) | async-done | bytes 131088 | tf_op jit(solution)/shard_map/while/body/eval_jaxpr/reduce_scatter | solution.py:291
  1232.5 152.2 %reduce-scatter.10.cloned.1.call-done = f32[64,1024]{1,0:T(8,128)} async-done(((f32[2048,1024]{1,0:T(8,128)}), f32[64,1024]{1,0:T(8,128)}) %reduce-scatter.10.cloned.1.call-update) | async-done | bytes 262160 | tf_op jit(solution)/shard_map/reduce_scatter | solution.py:336
  1387.4 248.2 %reduce-scatter.16.cloned.1.call-done = f32[88,1024]{1,0:T(8,128)} async-done(((f32[2816,1024]{1,0:T(8,128)}), f32[88,1024]{1,0:T(8,128)}) %reduce-scatter.16.cloned.1.call-update) | async-done | bytes 360464 | tf_op jit(solution)/shard_map/reduce_scatter | solution.py:339
  1637.5 357.5 %reduce-scatter.12.cloned.1.call-done = f32[4,32,1024]{2,1,0:T(8,128)} async-done(((f32[4,1024,1024]{2,1,0:T(8,128)}), f32[4,32,1024]{2,1,0:T(8,128)}) %reduce-scatter.12.cloned.1.call-update) | async-done | bytes 524304 | tf_op jit(solution)/shard_map/reduce_scatter | solution.py:337
  1996.9 487.6 %reduce-scatter.14.cloned.1.call-done = f32[2,32,2816]{2,1,0:T(8,128)} async-done(((f32[2,1024,2816]{2,1,0:T(8,128)}), f32[2,32,2816]{2,1,0:T(8,128)}) %reduce-scatter.14.cloned.1.call-update) | async-done | bytes 720912 | tf_op jit(solution)/shard_map/reduce_scatter | solution.py:338
  2492.8 128.5 %reduce-scatter.18.cloned.1.call-done = f32[32,4]{1,0:T(8,128)} async-done(((f32[1024,4]{1,0:T(8,128)}), f32[32,4]{1,0:T(8,128)}) %reduce-scatter.18.cloned.1.call-update) | async-done | bytes 528
  2622.8 60.7 %all-gather.51.cloned.1.call-done = bf16[2048,1024]{1,0:T(8,128)(2,1)} async-done(((bf16[64,1024]{1,0:T(8,128)(2,1)}), bf16[2048,1024]{1,0:T(8,128)(2,1)}) %all-gather.51.cloned.1.call-update) | async-done | bytes 4194320 | tf_op jit(solution)/shard_map/all_gather | solution.py:350
  2688.1 93.5 %all-gather.59.cloned.1.call-done = bf16[6,1024,1024]{2,1,0:T(8,128)(2,1)} async-done(((bf16[6,32,1024]{2,1,0:T(8,128)(2,1)}), bf16[6,1024,1024]{2,1,0:T(8,128)(2,1)}) %all-gather.59.cloned.1.call-update) | async-done | bytes 12582928 | tf_op jit(solution)/shard_map/all_gather | solution.py:407
  2794.2 57.0 %all-gather.57.cloned.1.call-done = bf16[2816,1024]{1,0:T(8,128)(2,1)} async-done(((bf16[88,1024]{1,0:T(8,128)(2,1)}), bf16[2816,1024]{1,0:T(8,128)(2,1)}) %all-gather.57.cloned.1.call-update) | async-done | bytes 5767184 | tf_op jit(solution)/shard_map/all_gather | solution.py:359
  2869.2 62.5 %all-gather.53.cloned.1.call-done = bf16[4,1024,1024]{2,1,0:T(8,128)(2,1)} async-done(((bf16[4,32,1024]{2,1,0:T(8,128)(2,1)}), bf16[4,1024,1024]{2,1,0:T(8,128)(2,1)}) %all-gather.53.cloned.1.call-update) | async-done | bytes 8388624 | tf_op jit(solution)/shard_map/all_gather | solution.py:353
  2960.8 64.5 %all-gather.55.cloned.1.call-done = bf16[2,1024,2816]{2,1,0:T(8,128)(2,1)} async-done(((bf16[2,32,2816]{2,1,0:T(8,128)(2,1)}), bf16[2,1024,2816]{2,1,0:T(8,128)(2,1)}) %all-gather.55.cloned.1.call-update) | async-done | bytes 11534352 | tf_op jit(solution)/shard_map/all_gather | solution.py:356
  3067.5 145.6 %all-gather.61.cloned.1.call-done = bf16[2,2816,2816]{2,1,0:T(8,128)(2,1)} async-done(((bf16[2,88,2816]{2,1,0:T(8,128)(2,1)}), bf16[2,2816,2816]{2,1,0:T(8,128)(2,1)}) %all-gather.61.cloned.1.call-update) | async-done | bytes 31719440 | tf_op jit(solution)/shard_map/all_gather | solution.py:420
  (507 shorter events, 759.8 us)
Async XLA Ops:
  7.2 95.3 %all-gather.43.cloned.1.call-start = ((), (), s32[]{:S(2)}) async-start(), calls=%async_computation.7 | async-start | bytes 4325376 | tf_op jit(solution)/shard_map/all_gather | solution.py:129
  9.0 147.4 %all-gather.45.cloned.1.call-start = ((), (), s32[]{:S(2)}) async-start(), calls=%async_computation.8 | async-start | bytes 8650752 | tf_op jit(solution)/shard_map/all_gather | solution.py:130
  177.1 83.7 %all-gather.63.cloned.1.call-start = ((), (), s32[]{:S(2)}) async-start(), calls=%async_computation.22 | async-start | bytes 1179648 | tf_op jit(solution)/shard_map/while/body/eval_jaxpr/all_gather | solution.py:157
  351.1 94.4 %all-gather.47.cloned.1.call-start = ((), (), s32[]{:S(2)}) async-start(), calls=%async_computation.9 | async-start | bytes 11894784 | tf_op jit(solution)/shard_map/all_gather | solution.py:131
  351.9 162.8 %all-gather.49.cloned.1.call-start = ((), (), s32[]{:S(2)}) async-start(), calls=%async_computation.10 | async-start | bytes 5947392 | tf_op jit(solution)/shard_map/all_gather | solution.py:132
  531.6 84.1 %all-gather.67.cloned.1.call-start = ((), (), s32[]{:S(2)}) async-start(), calls=%async_computation.24 | async-start | bytes 1179648 | tf_op jit(solution)/shard_map/while/body/eval_jaxpr/all_gather | solution.py:157
  618.9 83.9 %all-gather.67.cloned.1.call-start = ((), (), s32[]{:S(2)}) async-start(), calls=%async_computation.24 | async-start | bytes 1179648 | tf_op jit(solution)/shard_map/while/body/eval_jaxpr/all_gather | solution.py:157
  743.9 83.9 %all-gather.73.cloned.1.call-start = ((), (), s32[]{:S(2)}) async-start(), calls=%async_computation.27 | async-start | bytes 1179648 | tf_op jit(solution)/shard_map/while/body/eval_jaxpr/all_gather | solution.py:264
  744.7 152.0 %reduce-scatter.20.cloned.1.call-start = ((), (), s32[]{:S(2)}) async-start(), calls=%async_computation.28 | async-start | bytes 1179648 | tf_op jit(solution)/shard_map/while/body/eval_jaxpr/reduce_scatter | solution.py:288
  834.2 128.2 %reduce-scatter.22.cloned.1.call-start = ((), (), s32[]{:S(2)}) async-start(), calls=%async_computation.29 | async-start | bytes 1179648 | tf_op jit(solution)/shard_map/while/body/eval_jaxpr/reduce_scatter | solution.py:291
  964.8 83.9 %all-gather.73.cloned.1.call-start = ((), (), s32[]{:S(2)}) async-start(), calls=%async_computation.27 | async-start | bytes 1179648 | tf_op jit(solution)/shard_map/while/body/eval_jaxpr/all_gather | solution.py:264
  965.5 151.9 %reduce-scatter.20.cloned.1.call-start = ((), (), s32[]{:S(2)}) async-start(), calls=%async_computation.28 | async-start | bytes 1179648 | tf_op jit(solution)/shard_map/while/body/eval_jaxpr/reduce_scatter | solution.py:288
  1055.1 128.1 %reduce-scatter.22.cloned.1.call-start = ((), (), s32[]{:S(2)}) async-start(), calls=%async_computation.29 | async-start | bytes 1179648 | tf_op jit(solution)/shard_map/while/body/eval_jaxpr/reduce_scatter | solution.py:291
  1184.8 199.9 %reduce-scatter.10.cloned.1.call-start = ((), (), s32[]{:S(2)}) async-start(), calls=%async_computation.11 | async-start | bytes 8650752 | tf_op jit(solution)/shard_map/reduce_scatter | solution.py:336
  1200.7 435.0 %reduce-scatter.16.cloned.1.call-start = ((), (), s32[]{:S(2)}) async-start(), calls=%async_computation.14 | async-start | bytes 11894784 | tf_op jit(solution)/shard_map/reduce_scatter | solution.py:339
  1207.7 787.3 %reduce-scatter.12.cloned.1.call-start = ((), (), s32[]{:S(2)}) async-start(), calls=%async_computation.12 | async-start | bytes 17301504 | tf_op jit(solution)/shard_map/reduce_scatter | solution.py:337
  1217.8 1266.8 %reduce-scatter.14.cloned.1.call-start = ((), (), s32[]{:S(2)}) async-start(), calls=%async_computation.13 | async-start | bytes 23789568 | tf_op jit(solution)/shard_map/reduce_scatter | solution.py:338
  1230.7 1390.6 %reduce-scatter.18.cloned.1.call-start = ((), (), s32[]{:S(2)}) async-start(), calls=%async_computation.21 | async-start | bytes 540672
  1232.4 1451.1 %all-gather.51.cloned.1.call-start = ((), (), s32[]{:S(2)}) async-start(), calls=%async_computation.15 | async-start | bytes 4325376 | tf_op jit(solution)/shard_map/all_gather | solution.py:350
  1386.4 1395.2 %all-gather.59.cloned.1.call-start = ((), (), s32[]{:S(2)}) async-start(), calls=%async_computation.19 | async-start | bytes 12976128 | tf_op jit(solution)/shard_map/all_gather | solution.py:407
  1387.4 1463.8 %all-gather.57.cloned.1.call-start = ((), (), s32[]{:S(2)}) async-start(), calls=%async_computation.18 | async-start | bytes 5947392 | tf_op jit(solution)/shard_map/all_gather | solution.py:359
  1637.4 1294.3 %all-gather.53.cloned.1.call-start = ((), (), s32[]{:S(2)}) async-start(), calls=%async_computation.16 | async-start | bytes 8650752 | tf_op jit(solution)/shard_map/all_gather | solution.py:353
  1996.9 1028.5 %all-gather.55.cloned.1.call-start = ((), (), s32[]{:S(2)}) async-start(), calls=%async_computation.17 | async-start | bytes 11894784 | tf_op jit(solution)/shard_map/all_gather | solution.py:356
  2486.5 726.6 %all-gather.61.cloned.1.call-start = ((), (), s32[]{:S(2)}) async-start(), calls=%async_computation.20 | async-start | bytes 32710656 | tf_op jit(solution)/shard_map/all_gather | solution.py:420
  (110 other events, 12441.7 us)
Sparse Core Ops, SparseCore 0:
  11.6 64.9 all-gather.42
  80.3 76.0 all-gather.44
  221.8 38.9 all-gather.62
  355.4 90.0 all-gather.46
  449.0 65.6 all-gather.48
  534.7 39.1 all-gather.68
  622.0 38.9 all-gather.68
  747.0 38.9 all-gather.70
  834.4 62.2 reduce-scatter.19
  899.9 62.4 reduce-scatter.21
  967.6 39.1 all-gather.70
  1055.2 62.2 reduce-scatter.19
  1120.7 62.3 reduce-scatter.21
  1200.8 183.8 reduce-scatter.9
  1387.0 248.6 reduce-scatter.15
  1638.0 356.9 reduce-scatter.11
  1997.2 487.3 reduce-scatter.13
  2487.4 133.9 reduce-scatter.17
  2625.2 58.2 all-gather.50
  2687.4 94.1 all-gather.58
  2785.5 65.5 all-gather.56
  2855.3 76.4 all-gather.52
  2935.4 89.8 all-gather.54
  3028.7 184.3 all-gather.60
  (7 shorter events, 272.0 us)
where the time goes:
time: 3250 us; the launch traced here: 3240 us
  waiting for transfers between devices  2780 us (86%)
  matrix products  225 us (7%)
  blocking collectives  86.4 us (3%)
  local copies, waits for them, and re-layouts  69.7 us (2%)
  other arithmetic  52.8 us (2%)
    reduce_scatter x1, waiting for transfers between devices, body(): lax.psum_scatter(grad_gateup, ('dp', 'seq'), scatter_dimension=1, tiled=T...  488 us
    reduce_scatter x1, waiting for transfers between devices, body(): lax.psum_scatter(grad_attn, ('dp', 'seq'), scatter_dimension=1, tiled=True)  358 us
    reduce_scatter x1, waiting for transfers between devices, body(): lax.psum_scatter(grad_down, ('dp', 'seq'), scatter_dimension=0, tiled=True)  248 us
    all_gather x4, waiting for transfers between devices, one_sequence(): lax.all_gather(key_seq, 'seq', axis=0, tiled=True)  159 us
    all_gather x4, waiting for transfers between devices, one_sequence(): lax.all_gather(value_seq, 'seq', axis=0, tiled=True)  159 us
    reduce_scatter x1, waiting for transfers between devices, body(): lax.psum_scatter(grad_adapt, ('dp', 'seq'), scatter_dimension=0, tiled=True)  152 us
    all_gather x1, waiting for transfers between devices, body(): lax.all_gather(right_root_gateup.astype(jnp.bfloat16), ('dp', 'seq'), axi...  146 us
    unnamed x16, waiting for transfers between devices  129 us
  transfers between devices with their start and end apart: 31, of which 30 were waited for; matrix products, arithmetic and copies ran while one was open for 7% of the time, Pallas kernels for 0%

commit v1 on v0

v1 whole, which is shorter than its diff:
```python
import math

import jax
import jax.numpy as jnp
from jax import lax
from jax.sharding import PartitionSpec as P

HEADS = 8
HEAD_DIM = 128
EPSILON = 1e-06
THETA = 50000.0
AXES = ("dp", "seq")
BF16 = jnp.bfloat16
F32 = jnp.float32


def product(left_side, right_side):
    return jnp.dot(left_side, right_side, preferred_element_type=F32)


def across(left_side, right_side):
    return lax.dot_general(
        left_side, right_side, (((0,), (0,)), ((), ())), preferred_element_type=F32
    )


def against(left_side, right_side):
    return lax.dot_general(
        left_side, right_side, (((1,), (1,)), ((), ())), preferred_element_type=F32
    )


def norm_scale(values):
    return lax.rsqrt(jnp.mean(values * values, axis=-1, keepdims=True) + EPSILON)


def norm_back(values, scaling, gain_row, gradient):
    unit_rows = values * scaling
    weighted = gradient * gain_row
    moved = scaling * (
        weighted - unit_rows * jnp.mean(unit_rows * weighted, axis=-1, keepdims=True)
    )
    return (moved, jnp.sum(gradient * unit_rows, axis=0))


def rotate(values, cosine, sine_table):
    half_dim = values.shape[-1] // 2
    first_half = values[..., :half_dim]
    second_half = values[..., half_dim:]
    return jnp.concatenate(
        [
            first_half * cosine - second_half * sine_table,
            second_half * cosine + first_half * sine_table,
        ],
        axis=-1,
    )


def silu_grad(values):
    sigmoid_value = jax.nn.sigmoid(values)
    return sigmoid_value * (1.0 + values * (1.0 - sigmoid_value))


class Links:
    def __init__(self, n_dp, n_seq):
        self.n_dp, self.n_seq = n_dp, n_seq
        self.sizes = (n_dp // 2, 2, n_seq // 2, 2)
        self.count = n_dp * n_seq
        dp, seq = lax.axis_index("dp"), lax.axis_index("seq")
        self.place = (dp // 2, dp % 2, seq // 2, seq % 2)
        self.index = dp * n_seq + seq
        self.seq_index = seq

    def digits(self, index):
        out = []
        for size in reversed(self.sizes):
            out.append(index % size)
            index //= size
        return out[::-1]

    def number(self, digits):
        index = 0
        for digit, size in zip(digits, self.sizes):
            index = index * size + digit
        return index

    def move(self, values, digit, step):
        pairs = []
        for source in range(self.count):
            target = self.digits(source)
            target[digit] = (target[digit] + step) % self.sizes[digit]
            pairs.append((source, self.number(target)))
        return lax.ppermute(values, AXES, pairs)

    def total(self, values, digits):
        for digit in digits:
            size = self.sizes[digit]
            bit = 1
            while bit < size:
                pairs = []
                for source in range(self.count):
                    target = self.digits(source)
                    target[digit] ^= bit
                    pairs.append((source, self.number(target)))
                values = values + lax.ppermute(values, AXES, pairs)
                bit *= 2
        return values

    def _put(self, whole, part, axis, where, column):
        starts = [0] * whole.ndim
        starts[axis] = where
        starts[-1] = column
        return lax.dynamic_update_slice(whole, jnp.expand_dims(part, axis), tuple(starts))

    def gather(self, shard):
        rows, columns = shard.shape
        half = columns // 2
        whole = jnp.zeros(self.sizes + (rows, columns), shard.dtype)
        for start, order in ((0, (2, 3, 0)), (half, (2, 0, 3))):
            part = shard[:, start : start + half]
            known = []
            for digit in order:
                axis = sum(1 for other in known if other < digit)
                size = self.sizes[digit]
                shape = part.shape[:axis] + (size,) + part.shape[axis:]
                wider = jnp.zeros(shape, part.dtype)
                wider = self._put(wider, part, axis, self.place[digit], 0)
                for step in range(1, size):
                    came = self.move(part, digit, step)
                    wider = self._put(wider, came, axis, (self.place[digit] - step) % size, 0)
                part = wider
                known.append(digit)
            came = self.move(part, 1, 1)
            whole = self._put(whole, part, 1, self.place[1], start)
            whole = self._put(whole, came, 1, 1 - self.place[1], start)
        return whole.reshape(self.count * rows, columns)

    def reduce(self, left_side, right_side):
        tokens, height = left_side.shape
        columns = right_side.shape[1]
        rows = height // self.count
        first, second, third, fourth = self.sizes
        sides = left_side.reshape(tokens, first, 2, third * fourth * rows)
        shape = (first, third, fourth, rows, columns)

        def term(which):
            side = lax.dynamic_index_in_dim(sides, which, 2, False).reshape(tokens, -1)
            return across(side, right_side)

        away = term(1 - self.place[1]).astype(BF16)
        came = self.move(away, 1, 1)
        total = (term(self.place[1]) + came.astype(F32)).astype(BF16).reshape(shape)
        half = columns // 2
        parts = []
        for start, order in ((0, (0, 3, 2)), (half, (3, 0, 2))):
            part = total[..., start : start + half]
            left = [0, 2, 3]
            for digit in order:
                axis, size = left.index(digit), self.sizes[digit]
                place = self.place[digit]
                summed = lax.dynamic_index_in_dim(part, place, axis, False).astype(F32)
                for step in range(1, size):
                    away = lax.dynamic_index_in_dim(part, (place + step) % size, axis, False)
                    summed = summed + self.move(away, digit, step).astype(F32)
                left.remove(digit)
                part = summed.astype(BF16) if left else summed
            parts.append(part)
        return jnp.concatenate(parts, axis=1)


def body(
    embedding,
    latent,
    segment_ids,
    cotangent,
    weight_adapt,
    weight_attn,
    weight_gateup,
    weight_down,
    norm_gains,
    left_adapt,
    right_adapt,
    left_attn,
    right_attn,
    left_gateup,
    right_gateup,
    left_down,
    right_down,
    left_root_adapt,
    right_root_adapt,
    left_root_attn,
    right_root_attn,
    left_root_gateup,
    right_root_gateup,
    left_root_down,
    right_root_down,
    gain_moment,
):
    n_dp, n_seq = lax.axis_size("dp"), lax.axis_size("seq")
    links = Links(n_dp, n_seq)
    seq_count, group_len, width = embedding.shape
    tokens = seq_count * group_len
    length = group_len * n_seq
    hidden_width = weight_gateup.shape[2]
    by_heads = HEADS % n_seq == 0

    adapt_full = links.gather(weight_adapt.astype(BF16))
    attn_rows = weight_attn.astype(BF16)
    qkv_full = links.gather(jnp.concatenate([attn_rows[0], attn_rows[1], attn_rows[2]], axis=1))
    out_full = links.gather(attn_rows[3])
    gateup_rows = weight_gateup.astype(BF16)
    gateup_full = links.gather(jnp.concatenate([gateup_rows[0], gateup_rows[1]], axis=1))
    down_full = links.gather(weight_down.astype(BF16))

    gain_share = norm_gains.shape[1]
    gain_values = lax.dynamic_update_slice(
        jnp.zeros((4, width), F32),
        norm_gains.astype(BF16).astype(F32),
        (0, links.index * gain_share),
    )
    gain_values = links.total(gain_values, (0, 1, 2, 3))
    segment_whole = lax.dynamic_update_slice(
        jnp.zeros((seq_count, length), jnp.int32), segment_ids, (0, links.seq_index * group_len)
    )
    segment_whole = links.total(segment_whole, (2, 3))

    all_places = jnp.arange(length, dtype=jnp.int32)
    doc_starts = jnp.sum(
        (segment_whole[:, None, :] < segment_whole[:, :, None]).astype(jnp.int32), axis=2
    )
    places = all_places[None, :] - doc_starts
    half_dim = HEAD_DIM // 2
    frequency = THETA ** (-jnp.arange(half_dim, dtype=F32) / half_dim)
    angles = places.astype(F32)[..., None] * frequency
    cosine_all, sine_all = jnp.cos(angles), jnp.sin(angles)
    own_start = links.seq_index * group_len
    cosine = lax.dynamic_slice_in_dim(cosine_all, own_start, group_len, 1)
    sine_table = lax.dynamic_slice_in_dim(sine_all, own_start, group_len, 1)
    if by_heads:
        query_places, segment_query = all_places, segment_whole
        cosine_back, sine_back = cosine_all[:, None], sine_all[:, None]
    else:
        query_places, segment_query = own_start + jnp.arange(group_len), segment_ids
        cosine_back, sine_back = cosine[:, None], sine_table[:, None]
    allowed = (all_places[None, None, :] <= query_places[None, :, None]) & (
        segment_whole[:, None, :] == segment_query[:, :, None]
    )

    def to_heads(values):
        parts = values.shape[2]
        values = values.transpose(3, 2, 0, 1, 4)
        came = lax.all_to_all(values, "seq", 0, 0, tiled=True)
        came = came.reshape(n_seq, HEADS // n_seq, parts, seq_count, group_len, HEAD_DIM)
        came = came.transpose(2, 3, 1, 0, 4, 5)
        return came.reshape(parts, seq_count, HEADS // n_seq, length, HEAD_DIM)

    def to_tokens(values):
        parts = values.shape[0]
        own = HEADS // n_seq
        values = values.reshape(parts, seq_count, own, n_seq, group_len, HEAD_DIM)
        values = values.transpose(3, 2, 0, 1, 4, 5)
        came = lax.all_to_all(values, "seq", 0, 0, tiled=True)
        came = came.reshape(HEADS, parts, seq_count, group_len, HEAD_DIM)
        return came.transpose(1, 2, 3, 0, 4)

    scaling = 1.0 / math.sqrt(HEAD_DIM)

    def attention(queries, keys, values):
        if by_heads:
            queries, keys, values = to_heads(jnp.stack([queries, keys, values], axis=2))
        else:
            queries = queries.transpose(0, 2, 1, 3)
            keys, values = (
                lax.all_gather(item, "seq", axis=1, tiled=True).transpose(0, 2, 1, 3)
                for item in (keys, values)
            )
        scores = jnp.einsum("shqd,shkd->shqk", queries, keys, preferred_element_type=F32)
        scores = jnp.where(allowed[:, None], scores * scaling, -1e30)
        exponent = jnp.exp(scores - jnp.max(scores, axis=-1, keepdims=True))
        soft_full = exponent / jnp.sum(exponent, axis=-1, keepdims=True)
        mixed = jnp.einsum(
            "shqk,shkd->shqd", soft_full.astype(BF16), values, preferred_element_type=F32
        ).astype(BF16)
        if by_heads:
            mixed = to_tokens(mixed[None])[0]
        else:
            mixed = mixed.transpose(0, 2, 1, 3)
        return mixed.reshape(tokens, width), (queries, keys, values, soft_full)

    def attention_back(mixed_grad, saved):
        queries, keys, values, soft_full = saved
        mixed_grad = mixed_grad.reshape(seq_count, group_len, HEADS, HEAD_DIM)
        if by_heads:
            mixed_grad = to_heads(mixed_grad[:, :, None])[0]
        else:
            mixed_grad = mixed_grad.transpose(0, 2, 1, 3)
        soft_grad = jnp.einsum("shqd,shkd->shqk", mixed_grad, values, preferred_element_type=F32)
        inner_sum = jnp.sum(soft_full * soft_grad, axis=-1, keepdims=True)
        score_grad = (soft_full * (soft_grad - inner_sum)).astype(BF16)
        query_grad = (
            jnp.einsum("shqk,shkd->shqd", score_grad, keys, preferred_element_type=F32) * scaling
        )
        key_grad = (
            jnp.einsum("shqk,shqd->shkd", score_grad, queries, preferred_element_type=F32)
            * scaling
        )
        value_grad = jnp.einsum(
            "shqk,shqd->shkd", soft_full.astype(BF16), mixed_grad, preferred_element_type=F32
        )
        if by_heads:
            query_grad = rotate(query_grad, cosine_back, -sine_back).astype(BF16)
            key_grad = rotate(key_grad, cosine_back, -sine_back).astype(BF16)
            value_grad = value_grad.astype(BF16)
            grads = to_tokens(jnp.stack([query_grad, key_grad, value_grad]))
        else:
            key_grad, value_grad = (
                lax.psum_scatter(
                    item.astype(BF16), "seq", scatter_dimension=2, tiled=True
                ).astype(F32)
                for item in (key_grad, value_grad)
            )
            query_grad = rotate(query_grad, cosine_back, -sine_back).astype(BF16)
            key_grad = rotate(key_grad, cosine_back, -sine_back).astype(BF16)
            grads = jnp.stack([query_grad, key_grad, value_grad.astype(BF16)])
            grads = grads.transpose(0, 1, 3, 2, 4)
        return grads.reshape(3, tokens, width)

    embed_flat = embedding.reshape(tokens, width)
    embed_part = product(embed_flat, adapt_full[width:])

    def forward(latent_low):
        start_sum = product(latent_low, adapt_full[:width]) + embed_part
        scale_one = norm_scale(start_sum)
        normed_one = (start_sum * scale_one * gain_values[0]).astype(BF16)
        qkv = product(normed_one, qkv_full).reshape(seq_count, group_len, 3, HEADS, HEAD_DIM)
        turn_cos, turn_sin = cosine[:, :, None, :], sine_table[:, :, None, :]
        queries = rotate(qkv[:, :, 0], turn_cos, turn_sin).astype(BF16)
        keys = rotate(qkv[:, :, 1], turn_cos, turn_sin).astype(BF16)
        mixed_heads, attended = attention(queries, keys, qkv[:, :, 2].astype(BF16))
        branch = product(mixed_heads, out_full)
        scale_two = norm_scale(branch)
        middle = start_sum + branch * scale_two * gain_values[1]
        scale_three = norm_scale(middle)
        normed_three = (middle * scale_three * gain_values[2]).astype(BF16)
        both = product(normed_three, gateup_full)
        gate_value, upward = both[:, :hidden_width], both[:, hidden_width:]
        hidden = (jax.nn.silu(gate_value) * upward).astype(BF16)
        feed_out = product(hidden, down_full)
        scale_four = norm_scale(feed_out)
        result = middle + feed_out * scale_four * gain_values[3]
        saved_values = (
            start_sum,
            scale_one,
            normed_one,
            attended,
            mixed_heads,
            branch,
            scale_two,
            middle,
            scale_three,
            normed_three,
            gate_value,
            upward,
            hidden,
            feed_out,
            scale_four,
        )
        return (result, saved_values)

    latent_low = latent.reshape(tokens, width)
    latent_state, unused_saved = forward(latent_low)
    latent_low = latent_state.astype(BF16)
    final_state, saved_values = forward(latent_low)
    (
        start_sum,
        scale_one,
        normed_one,
        attended,
        mixed_heads,
        branch,
        scale_two,
        middle,
        scale_three,
        normed_three,
        gate_value,
        upward,
        hidden,
        feed_out,
        scale_four,
    ) = saved_values
    factor = 1.0 / math.sqrt(seq_count * n_dp * length)
    incoming = cotangent.astype(F32).reshape(tokens, width)
    feed_grad, gain_four = norm_back(feed_out, scale_four, gain_values[3], incoming)
    feed_grad = feed_grad.astype(BF16)
    reduced_down = links.reduce(hidden, feed_grad) * factor
    full_down = links.gather(reduced_down.astype(BF16))
    hidden_grad = against(feed_grad, down_full)
    gate_grad = (hidden_grad * upward * silu_grad(gate_value)).astype(BF16)
    up_grad = (hidden_grad * jax.nn.silu(gate_value)).astype(BF16)
    both_grad = jnp.concatenate([gate_grad, up_grad], axis=1)
    reduced_both = links.reduce(normed_three, both_grad) * factor
    full_both = links.gather(reduced_both.astype(BF16))
    normed_three_grad = against(both_grad, gateup_full)
    middle_grad, gain_three = norm_back(middle, scale_three, gain_values[2], normed_three_grad)
    middle_grad = middle_grad + incoming
    branch_grad, gain_two = norm_back(branch, scale_two, gain_values[1], middle_grad)
    branch_grad = branch_grad.astype(BF16)
    reduced_out = links.reduce(mixed_heads, branch_grad) * factor
    full_out = links.gather(reduced_out.astype(BF16))
    mixed_grad = against(branch_grad, out_full).astype(BF16)
    query_pre, key_pre, value_pre = attention_back(mixed_grad, attended)
    qkv_grad = jnp.concatenate([query_pre, key_pre, value_pre], axis=1)
    reduced_qkv = links.reduce(normed_one, qkv_grad) * factor
    full_qkv = links.gather(reduced_qkv.astype(BF16))
    normed_one_grad = against(qkv_grad, qkv_full)
    start_grad, gain_one = norm_back(start_sum, scale_one, gain_values[0], normed_one_grad)
    start_grad = (start_grad + middle_grad).astype(BF16)
    joined = jnp.concatenate([latent_low, embed_flat], axis=1)
    reduced_adapt = links.reduce(joined, start_grad) * factor
    full_adapt = links.gather(reduced_adapt.astype(BF16))
    grad_embedding = against(start_grad, adapt_full[width:]).reshape(
        seq_count, group_len, width
    )
    gain_sums = links.total(jnp.stack([gain_one, gain_two, gain_three, gain_four]), (0, 1, 2, 3))
    reduced_gains = (
        lax.dynamic_slice_in_dim(gain_sums, links.index * gain_share, gain_share, 1) * factor
    )

    root_stack = jnp.concatenate(
        [
            right_root_adapt.astype(BF16)[:, None],
            right_root_attn.astype(BF16).transpose(1, 0, 2),
            right_root_down.astype(BF16)[:, None],
            left_root_gateup.astype(BF16).transpose(1, 0, 2),
        ],
        axis=1,
    )
    share = root_stack.shape[0]
    roots = lax.all_gather(root_stack.reshape(share, 8 * width), AXES, axis=0, tiled=True)

    def statistics(shard, whole, left_stat, right_stat, left_root):
        rows, columns = whole.shape
        new_left = 0.5 * left_stat + (0.5 / columns) * against(shard.astype(BF16), whole)
        count = right_stat.shape[0]
        own = lax.dynamic_slice_in_dim(whole, links.index * count, count, 1).T
        if left_root is None:
            return (new_left, 0.5 * right_stat + (0.5 / rows) * product(own, whole), None)
        own_count = left_root.shape[0]
        both = product(jnp.concatenate([left_root.astype(BF16), own], axis=0), whole)
        return (new_left, 0.5 * right_stat + (0.5 / rows) * both[own_count:], both[:own_count])

    def step(part, which, rows):
        root = roots[:, which * width : (which + 1) * width]
        return product(part.astype(BF16), root) * (1.0 / math.sqrt(rows))

    whole_gates = [full_both[:, :hidden_width], full_both[:, hidden_width:]]
    gate_shards = [reduced_both[:, :hidden_width], reduced_both[:, hidden_width:]]
    gateup_parts = [
        statistics(gate_shards[i], whole_gates[i], left_gateup[i], right_gateup[i], None)
        for i in range(2)
    ]
    step_columns = []
    for i in range(2):
        turned = against(whole_gates[i], right_root_gateup[i].astype(BF16)).astype(BF16)
        root = roots[:, (6 + i) * width : (7 + i) * width]
        step_columns.append(product(root, turned).astype(BF16))
    step_columns = jnp.stack(step_columns)
    ff_share = step_columns.shape[2]
    row_share = width // links.count
    step_columns = step_columns.reshape(2, links.count, row_share, ff_share).transpose(1, 0, 2, 3)
    step_rows = lax.all_to_all(step_columns, AXES, 0, 0, tiled=True)
    step_gateup = step_rows.transpose(1, 2, 0, 3).reshape(2, row_share, hidden_width)
    new_gateup = weight_gateup - step_gateup.astype(F32) * (1.0 / math.sqrt(width))

    new_left_down, new_right_down, down_part = statistics(
        reduced_down, full_down, left_down, right_down, left_root_down
    )
    new_down = weight_down - step(down_part, 5, hidden_width)
    attn_shards = [reduced_qkv[:, i * width : (i + 1) * width] for i in range(3)] + [reduced_out]
    attn_wholes = [full_qkv[:, i * width : (i + 1) * width] for i in range(3)] + [full_out]
    attn_parts = [
        statistics(attn_shards[i], attn_wholes[i], left_attn[i], right_attn[i], left_root_attn[i])
        for i in range(4)
    ]
    new_attn = weight_attn - jnp.stack([step(attn_parts[i][2], 1 + i, width) for i in range(4)])
    new_left_adapt, new_right_adapt, adapt_part = statistics(
        reduced_adapt, full_adapt, left_adapt, right_adapt, left_root_adapt
    )
    new_adapt = weight_adapt - step(adapt_part, 0, 2 * width)
    new_gain_moment = 0.5 * gain_moment + 0.5 * reduced_gains * reduced_gains
    new_norm_gains = norm_gains - 0.5 * reduced_gains / (jnp.sqrt(new_gain_moment) + 1e-08)
    latent_out = final_state.reshape(seq_count, group_len, width).astype(BF16)
    return (
        latent_out,
        grad_embedding,
        reduced_adapt,
        jnp.stack(attn_shards),
        jnp.stack(gate_shards),
        reduced_down,
        reduced_gains,
        new_left_adapt,
        new_right_adapt,
        jnp.stack([member[0] for member in attn_parts]),
        jnp.stack([member[1] for member in attn_parts]),
        jnp.stack([member[0] for member in gateup_parts]),
        jnp.stack([member[1] for member in gateup_parts]),
        new_left_down,
        new_right_down,
        new_adapt,
        new_attn,
        new_gateup,
        new_down,
        new_gain_moment,
        new_norm_gains,
    )

def solution(mesh):
    return jax.shard_map(
        body,
        mesh=mesh,
        in_specs=(
            P("dp", "seq", None),
            P("dp", "seq", None),
            P("dp", "seq"),
            P("dp", "seq", None),
            P(("dp", "seq"), None),
            P(None, ("dp", "seq"), None),
            P(None, ("dp", "seq"), None),
            P(("dp", "seq"), None),
            P(None, ("dp", "seq")),
            P(("dp", "seq"), None),
            P(("dp", "seq"), None),
            P(None, ("dp", "seq"), None),
            P(None, ("dp", "seq"), None),
            P(None, ("dp", "seq"), None),
            P(None, ("dp", "seq"), None),
            P(("dp", "seq"), None),
            P(("dp", "seq"), None),
            P(("dp", "seq"), None),
            P(("dp", "seq"), None),
            P(None, ("dp", "seq"), None),
            P(None, ("dp", "seq"), None),
            P(None, ("dp", "seq"), None),
            P(None, ("dp", "seq"), None),
            P(("dp", "seq"), None),
            P(("dp", "seq"), None),
            P(None, ("dp", "seq")),
        ),
        out_specs=(
            P("dp", "seq", None),
            P("dp", "seq", None),
            P(("dp", "seq"), None),
            P(None, ("dp", "seq"), None),
            P(None, ("dp", "seq"), None),
            P(("dp", "seq"), None),
            P(None, ("dp", "seq")),
            P(("dp", "seq"), None),
            P(("dp", "seq"), None),
            P(None, ("dp", "seq"), None),
            P(None, ("dp", "seq"), None),
            P(None, ("dp", "seq"), None),
            P(None, ("dp", "seq"), None),
            P(("dp", "seq"), None),
            P(("dp", "seq"), None),
            P(("dp", "seq"), None),
            P(None, ("dp", "seq"), None),
            P(None, ("dp", "seq"), None),
            P(("dp", "seq"), None),
            P(None, ("dp", "seq")),
            P(None, ("dp", "seq")),
        ),
        check_vma=False,
    )
```

time: 3250 us -> 1130 us (0.35)
  waiting for transfers between devices: 2780 us -> 379 us
  starting transfers between devices: 1.71 us -> 262 us
  local copies, waits for them, and re-layouts: 69.7 us -> 256 us
  blocking collectives: 86.4 us -> 0 us
  matrix products: 225 us -> 155 us
    reduce_scatter x8 -> x0, waiting for transfers between devices: 1490 us -> none  [the longest x1 488 us: body(): lax.psum_scatter(grad_gateup, ('dp', 'seq'), scatter_dimension=1, tiled=T...]
    all_gather x22 -> x1, waiting for transfers between devices: 1160 us -> 0.01 us  [body(): lax.all_gather(root_stack.reshape(share, 8 * width), AXES, axis=0, tiled=...]
    ppermute x0 -> x188, waiting for transfers between devices: none -> 341 us  [the longest x175 316 us: move(): return lax.ppermute(values, AXES, pairs)]
    ppermute x0 -> x188, starting transfers between devices: none -> 231 us  [the longest x175 218 us: move(): return lax.ppermute(values, AXES, pairs)]
    unnamed x16 -> x1, waiting for transfers between devices: 129 us -> 0.02 us
    dynamic_update_slice x8 -> x199, local copies, waits for them, and re-layouts: 3.18 us -> 108 us  [the longest x197 107 us: _put(): lax.dynamic_update_slice(whole, jnp.expand_dims(part, axis), tuple(starts))]
    dot_general x61 -> x33, matrix products: 188 us -> 85.2 us  [the longest x27 73 us: product(): return jnp.dot(left_side, right_side, preferred_element_type=F32)]
    all_gather x2 -> x0, blocking collectives: 86.4 us -> none  [the longest x1 69.8 us: body(): lax.all_gather(norm_gains.astype(jnp.bfloat16), ('dp', 'seq'), axis=1, ti...]
  transfers between devices with their start and end apart: 31 -> 196, of which waited for: 30 -> 93; matrix products, arithmetic and copies ran while one was open for 7% -> 36% of each run, Pallas kernels for 0% -> 0%
where the time goes in v1:
time: 1130 us; the launch traced here: 1120 us
  waiting for transfers between devices  379 us (34%)
  starting transfers between devices  262 us (23%)
  local copies, waits for them, and re-layouts  256 us (23%)
  matrix products  155 us (14%)
  other arithmetic  52.2 us (5%)
  between operations  18.6 us (2%)
    ppermute x175, waiting for transfers between devices, move(): return lax.ppermute(values, AXES, pairs)  316 us
    ppermute x175, starting transfers between devices, move(): return lax.ppermute(values, AXES, pairs)  218 us
    dynamic_update_slice x197, local copies, waits for them, and re-layouts, _put(): lax.dynamic_update_slice(whole, jnp.expand_dims(part, axis), tuple(starts))  107 us
    dot_general x27, matrix products, product(): return jnp.dot(left_side, right_side, preferred_element_type=F32)  73 us
    dot_general x13, matrix products, against(): lax.dot_general(left_side, right_side, (((1,), (1,)), ((), ())), preferre...  41.5 us
    another operation x70, local copies, waits for them, and re-layouts  37.4 us
    all_to_all x3, waiting for transfers between devices, to_heads(): came = lax.all_to_all(values, 'seq', 0, 0, tiled=True)  33.1 us
    unnamed x262, local copies, waits for them, and re-layouts  25 us
  transfers between devices with their start and end apart: 196, of which 93 were waited for; matrix products, arithmetic and copies ran while one was open for 36% of the time, Pallas kernels for 0%

profile of v1, /device:TPU:0, one launch (start us, length us, event | category | flops | bytes accessed | tf_op | source)
XLA Modules:
  0.0 1122.2 jit_solution(17860836831819948472)
XLA Ops:
  124.6 6.9 collective-permute-start.51
  151.6 10.4 collective-permute-done.36
  181.4 6.5 collective-permute-done.4
  213.1 10.6 collective-permute-done.24
  236.6 17.8 %collective-permute-done.48 = bf16[4,2,32,2816]{3,2,1,0:T(8,128)(2,1)} collective-permute-done((bf16[4,2,32,2816]{3,2,1,0:T(8,128)(2,1)}, bf16[4,2,32,2816]{3,2,1,0:T(8,128)(2,1)}, u32[]{:S(2)}, u32[]{:S(2)}) %collective-permute-start.48) | collective-permute-done | bytes 1441824 | tf_op jit(solution)/shard_map/ppermute | solution.py:93
  262.9 7.3 copy.620
  270.2 9.6 copy.440
  304.6 8.0 all-to-all-done
  355.3 6.2 fusion.146
  383.0 23.9 %all-to-all-done.2 = bf16[8,3,2,64,128]{4,3,2,1,0:T(8,128)(2,1)} async-done(((bf16[8,3,2,64,128]{4,3,2,1,0:T(8,128)(2,1)}), bf16[8,3,2,64,128]{4,3,2,1,0:T(8,128)(2,1)}, u32[]{:S(2)}, u32[]{:S(2)}) %all-to-all-start.2) | async-done | bytes 786464 | tf_op jit(solution)/shard_map/all_to_all | solution.py:252
  473.3 6.7 multiply_reduce_fusion.2
  482.5 6.4 all-to-all-start.4
  618.6 11.8 %collective-permute-done.118 = bf16[2,4,88,512]{3,2,1,0:T(8,128)(2,1)S(1)} collective-permute-done((bf16[2,4,88,512]{3,2,1,0:T(8,128)(2,1)S(1)}, bf16[2,4,88,512]{3,2,1,0:T(8,128)(2,1)S(1)}, u32[]{:S(2)}, u32[]{:S(2)}) %collective-permute-start.118) | collective-permute-done | bytes 720928 | tf_op jit(solution)/shard_map/ppermute | solution.py:93
  661.6 6.9 collective-permute-done.176
  678.6 6.3 collective-permute-done.182
  730.3 6.2 collective-permute-done.129
  773.7 8.7 collective-permute-done.132
  909.8 11.1 collective-permute-done.144
  922.7 6.4 collective-permute-done.108
  942.2 7.5 collective-permute-done.110
  971.1 9.1 collective-permute-start.170
  1001.4 8.6 collective-permute-done.173
  1015.8 17.7 %collective-permute-done.168 = bf16[4,2,32,2816]{3,2,1,0:T(8,128)(2,1)S(1)} collective-permute-done((bf16[4,2,32,2816]{3,2,1,0:T(8,128)(2,1)S(1)}, bf16[4,2,32,2816]{3,2,1,0:T(8,128)(2,1)S(1)}, u32[]{:S(2)}, u32[]{:S(2)}) %collective-permute-start.168) | collective-permute-done | bytes 1441824 | tf_op jit(solution)/shard_map/ppermute | solution.py:93
  1062.9 9.5 fusion.269
  (1199 shorter events, 873.6 us)
Async XLA Ops:
  8.9 53.1 %collective-permute-start = (bf16[64,512]{1,0:T(8,128)(2,1)}, bf16[64,512]{1,0:T(8,128)(2,1)}, u32[]{:S(2)}, u32[]{:S(2)}) collective-permute-start(bf16[64,512]{1,0:T(8,128)(2,1)} %get-tuple-element.203), channel_id=1, source_target_pairs={{0,2},{1,3},{2,4},{3,5},{4,6},{5,7},{6,0},{7,1},{8,10},{9,11},{10,... | collective-permute-start | bytes 196616 | tf_op jit(solution)/shard_map/ppermute | solution.py:93
  11.9 52.8 %collective-permute-start.1 = (bf16[64,512]{1,0:T(8,128)(2,1)}, bf16[64,512]{1,0:T(8,128)(2,1)S(1)}, u32[]{:S(2)}, u32[]{:S(2)}) collective-permute-start(bf16[64,512]{1,0:T(8,128)(2,1)} %get-tuple-element.203), channel_id=1, source_target_pairs={{0,4},{1,5},{2,6},{3,7},{4,0},{5,1},{6,2},{7,3},{8,12},{9,13},{10,... | collective-permute-start | bytes 196616 | tf_op jit(solution)/shard_map/ppermute | solution.py:93
  14.5 50.5 %collective-permute-start.2 = (bf16[64,512]{1,0:T(8,128)(2,1)}, bf16[64,512]{1,0:T(8,128)(2,1)}, u32[]{:S(2)}, u32[]{:S(2)}) collective-permute-start(bf16[64,512]{1,0:T(8,128)(2,1)} %get-tuple-element.203), channel_id=1, source_target_pairs={{0,6},{1,7},{2,0},{3,1},{4,2},{5,3},{6,4},{7,5},{8,14},{9,15},{10,... | collective-permute-start | bytes 196616 | tf_op jit(solution)/shard_map/ppermute | solution.py:93
  209.1 45.3 %collective-permute-start.48 = (bf16[4,2,32,2816]{3,2,1,0:T(8,128)(2,1)}, bf16[4,2,32,2816]{3,2,1,0:T(8,128)(2,1)}, u32[]{:S(2)}, u32[]{:S(2)}) collective-permute-start(bf16[4,2,32,2816]{3,2,1,0:T(8,128)(2,1)} %bitcast_dynamic-update-slice_fusion.53), channel_id=1, source_target_pairs={{0,16},{1,17},{2,18},{3,19},{4,20},{5,21},{6,22},{7,23},{8,24},{9,... | collective-permute-start | bytes 4325384 | tf_op jit(solution)/shard_map/ppermute | solution.py:93
  223.8 75.6 %collective-permute-start.54 = (bf16[2,4,32,2816]{3,2,1,0:T(8,128)(2,1)}, bf16[2,4,32,2816]{3,2,1,0:T(8,128)(2,1)}, u32[]{:S(2)}, u32[]{:S(2)}) collective-permute-start(bf16[2,4,32,2816]{3,2,1,0:T(8,128)(2,1)} %bitcast_dynamic-update-slice_fusion.62), channel_id=1, source_target_pairs={{0,1},{1,0},{2,3},{3,2},{4,5},{5,4},{6,7},{7,6},{8,9},{9,8},{10,11... | collective-permute-start | bytes 4325384 | tf_op jit(solution)/shard_map/ppermute | solution.py:93
  228.4 73.6 %collective-permute-start.61 = (bf16[2,4,2,88,512]{4,3,2,1,0:T(8,128)(2,1)}, bf16[2,4,2,88,512]{4,3,2,1,0:T(8,128)(2,1)}, u32[]{:S(2)}, u32[]{:S(2)}) collective-permute-start(bf16[2,4,2,88,512]{4,3,2,1,0:T(8,128)(2,1)} %bitcast_dynamic-update-slice_fusion.60), channel_id=1, source_target_pairs={{0,8},{1,9},{2,10},{3,11},{4,12},{5,13},{6,14},{7,15},{8,0},{9,1},... | collective-permute-start | bytes 4325384 | tf_op jit(solution)/shard_map/ppermute | solution.py:93
  228.6 101.6 %collective-permute-start.67 = (bf16[2,4,2,88,512]{4,3,2,1,0:T(8,128)(2,1)}, bf16[2,4,2,88,512]{4,3,2,1,0:T(8,128)(2,1)}, u32[]{:S(2)}, u32[]{:S(2)}) collective-permute-start(bf16[2,4,2,88,512]{4,3,2,1,0:T(8,128)(2,1)} %bitcast_dynamic-update-slice_fusion.59), channel_id=1, source_target_pairs={{0,8},{1,9},{2,10},{3,11},{4,12},{5,13},{6,14},{7,15},{8,0},{9,1},... | collective-permute-start | bytes 4325384 | tf_op jit(solution)/shard_map/ppermute | solution.py:93
  257.0 87.2 %collective-permute-start.49 = (bf16[2,4,2,32,2816]{4,3,2,1,0:T(8,128)(2,1)}, bf16[2,4,2,32,2816]{4,3,2,1,0:T(8,128)(2,1)}, u32[]{:S(2)}, u32[]{:S(2)}) collective-permute-start(bf16[2,4,2,32,2816]{4,3,2,1,0:T(8,128)(2,1)} %bitcast_dynamic-update-slice_fusion.30), channel_id=1, source_target_pairs={{0,8},{1,9},{2,10},{3,11},{4,12},{5,13},{6,14},{7,15},{8,0},{9,1},... | collective-permute-start | bytes 8650760 | tf_op jit(solution)/shard_map/ppermute | solution.py:93
  302.0 49.6 %collective-permute-start.55 = (bf16[2,4,2,32,2816]{4,3,2,1,0:T(8,128)(2,1)}, bf16[2,4,2,32,2816]{4,3,2,1,0:T(8,128)(2,1)}, u32[]{:S(2)}, u32[]{:S(2)}) collective-permute-start(bf16[2,4,2,32,2816]{4,3,2,1,0:T(8,128)(2,1)} %bitcast_dynamic-update-slice_fusion.29), channel_id=1, source_target_pairs={{0,8},{1,9},{2,10},{3,11},{4,12},{5,13},{6,14},{7,15},{8,0},{9,1},... | collective-permute-start | bytes 8650760 | tf_op jit(solution)/shard_map/ppermute | solution.py:93
  380.0 699.8 %all-gather.2.cloned.1.call-start = ((), (), s32[]{:S(2)}) async-start(), calls=%async_computation.7 | async-start | bytes 17301504 | tf_op jit(solution)/shard_map/all_gather | solution.py:439
  498.6 293.9 %collective-permute-start.101 = (bf16[512,5632]{1,0:T(8,128)(2,1)}, bf16[512,5632]{1,0:T(8,128)(2,1)}, u32[]{:S(2)}, u32[]{:S(2)}) collective-permute-start(bf16[512,5632]{1,0:T(8,128)(2,1)} %convolution_convert_fusion), channel_id=1, source_target_pairs={{0,8},{1,9},{2,10},{3,11},{4,12},{5,13},{6,14},{7,15},{8,0},{9,1},... | collective-permute-start | bytes 17301512 | tf_op jit(solution)/shard_map/ppermute | solution.py:93
  502.8 106.2 %collective-permute-start.112 = (bf16[1408,1024]{1,0:T(8,128)(2,1)}, bf16[1408,1024]{1,0:T(8,128)(2,1)}, u32[]{:S(2)}, u32[]{:S(2)}) collective-permute-start(bf16[1408,1024]{1,0:T(8,128)(2,1)} %convolution_convert_fusion.2), channel_id=1, source_target_pairs={{0,8},{1,9},{2,10},{3,11},{4,12},{5,13},{6,14},{7,15},{8,0},{9,1},... | collective-permute-start | bytes 8650760 | tf_op jit(solution)/shard_map/ppermute | solution.py:93
  521.5 57.2 %all-to-all-start.5 = ((bf16[8,1,3,2,64,128]{5,4,3,2,1,0:T(8,128)(2,1)}), bf16[8,1,3,2,64,128]{5,4,3,2,1,0:T(8,128)(2,1)S(1)}, u32[]{:S(2)}, u32[]{:S(2)}) async-start(bf16[8,1,3,2,64,128]{5,4,3,2,1,0:T(8,128)(2,1)} %maximum_bitcast_fusion.2), calls=%async_computation.5 | async-start | bytes 1572864 | tf_op jit(solution)/shard_map/all_to_all | solution.py:262
  607.7 149.1 %collective-permute-start.79 = (bf16[512,3072]{1,0:T(8,128)(2,1)S(1)}, bf16[512,3072]{1,0:T(8,128)(2,1)S(1)}, u32[]{:S(2)}, u32[]{:S(2)}) collective-permute-start(bf16[512,3072]{1,0:T(8,128)(2,1)S(1)} %copy-done.18), channel_id=1, source_target_pairs={{0,8},{1,9},{2,10},{3,11},{4,12},{5,13},{6,14},{7,15},{8,0},{9,1},... | collective-permute-start | bytes 9437192 | tf_op jit(solution)/shard_map/ppermute | solution.py:93
  719.0 50.6 %collective-permute-start.180 = (bf16[4,2,88,512]{3,2,1,0:T(8,128)(2,1)S(1)}, bf16[4,2,88,512]{3,2,1,0:T(8,128)(2,1)S(1)}, u32[]{:S(2)}, u32[]{:S(2)}) collective-permute-start(bf16[4,2,88,512]{3,2,1,0:T(8,128)(2,1)S(1)} %bitcast_dynamic-update-slice_fusion.88), channel_id=1, source_target_pairs={{0,16},{1,17},{2,18},{3,19},{4,20},{5,21},{6,22},{7,23},{8,24},{9,... | collective-permute-start | bytes 2162696 | tf_op jit(solution)/shard_map/ppermute | solution.py:93
  722.1 49.6 %collective-permute-start.186 = (bf16[2,4,88,512]{3,2,1,0:T(8,128)(2,1)S(1)}, bf16[2,4,88,512]{3,2,1,0:T(8,128)(2,1)S(1)}, u32[]{:S(2)}, u32[]{:S(2)}) collective-permute-start(bf16[2,4,88,512]{3,2,1,0:T(8,128)(2,1)S(1)} %bitcast_dynamic-update-slice_fusion.92), channel_id=1, source_target_pairs={{0,1},{1,0},{2,3},{3,2},{4,5},{5,4},{6,7},{7,6},{8,9},{9,8},{10,11... | collective-permute-start | bytes 2162696 | tf_op jit(solution)/shard_map/ppermute | solution.py:93
  782.4 79.9 %collective-permute-start.181 = (bf16[2,4,2,88,512]{4,3,2,1,0:T(8,128)(2,1)S(1)}, bf16[2,4,2,88,512]{4,3,2,1,0:T(8,128)(2,1)S(1)}, u32[]{:S(2)}, u32[]{:S(2)}) collective-permute-start(bf16[2,4,2,88,512]{4,3,2,1,0:T(8,128)(2,1)S(1)} %bitcast_dynamic-update-slice_fusion.55), channel_id=1, source_target_pairs={{0,8},{1,9},{2,10},{3,11},{4,12},{5,13},{6,14},{7,15},{8,0},{9,1},... | collective-permute-start | bytes 4325384 | tf_op jit(solution)/shard_map/ppermute | solution.py:93
  788.1 75.9 %collective-permute-start.187 = (bf16[2,4,2,88,512]{4,3,2,1,0:T(8,128)(2,1)S(1)}, bf16[2,4,2,88,512]{4,3,2,1,0:T(8,128)(2,1)S(1)}, u32[]{:S(2)}, u32[]{:S(2)}) collective-permute-start(bf16[2,4,2,88,512]{4,3,2,1,0:T(8,128)(2,1)S(1)} %bitcast_dynamic-update-slice_fusion.48), channel_id=1, source_target_pairs={{0,8},{1,9},{2,10},{3,11},{4,12},{5,13},{6,14},{7,15},{8,0},{9,1},... | collective-permute-start | bytes 4325384 | tf_op jit(solution)/shard_map/ppermute | solution.py:93
  818.0 61.5 %collective-permute-start.133 = (bf16[2,4,2,64,512]{4,3,2,1,0:T(8,128)(2,1)}, bf16[2,4,2,64,512]{4,3,2,1,0:T(8,128)(2,1)}, u32[]{:S(2)}, u32[]{:S(2)}) collective-permute-start(bf16[2,4,2,64,512]{4,3,2,1,0:T(8,128)(2,1)} %bitcast_dynamic-update-slice_fusion.75), channel_id=1, source_target_pairs={{0,8},{1,9},{2,10},{3,11},{4,12},{5,13},{6,14},{7,15},{8,0},{9,1},... | collective-permute-start | bytes 3145736 | tf_op jit(solution)/shard_map/ppermute | solution.py:93
  820.3 64.3 %collective-permute-start.139 = (bf16[2,4,2,64,512]{4,3,2,1,0:T(8,128)(2,1)}, bf16[2,4,2,64,512]{4,3,2,1,0:T(8,128)(2,1)}, u32[]{:S(2)}, u32[]{:S(2)}) collective-permute-start(bf16[2,4,2,64,512]{4,3,2,1,0:T(8,128)(2,1)} %bitcast_dynamic-update-slice_fusion.74), channel_id=1, source_target_pairs={{0,8},{1,9},{2,10},{3,11},{4,12},{5,13},{6,14},{7,15},{8,0},{9,1},... | collective-permute-start | bytes 3145736 | tf_op jit(solution)/shard_map/ppermute | solution.py:93
  859.3 45.1 %collective-permute-start.107 = (bf16[2,4,32,2816]{3,2,1,0:T(8,128)(2,1)}, bf16[2,4,32,2816]{3,2,1,0:T(8,128)(2,1)}, u32[]{:S(2)}, u32[]{:S(2)}) collective-permute-start(bf16[2,4,32,2816]{3,2,1,0:T(8,128)(2,1)} %dynamic-slice_bitcast_fusion), channel_id=1, source_target_pairs={{0,1},{1,0},{2,3},{3,2},{4,5},{5,4},{6,7},{7,6},{8,9},{9,8},{10,11... | collective-permute-start | bytes 4325384 | tf_op jit(solution)/shard_map/ppermute | solution.py:93
  862.3 44.9 %collective-permute-start.102 = (bf16[4,2,32,2816]{3,2,0,1:T(8,128)(2,1)}, bf16[4,2,32,2816]{3,2,0,1:T(8,128)(2,1)}, u32[]{:S(2)}, u32[]{:S(2)}) collective-permute-start(bf16[4,2,32,2816]{3,2,0,1:T(8,128)(2,1)} %bitcast.1164), channel_id=1, source_target_pairs={{0,16},{1,17},{2,18},{3,19},{4,20},{5,21},{6,22},{7,23},{8,24},{9,... | collective-permute-start | bytes 4325384 | tf_op jit(solution)/shard_map/ppermute | solution.py:93
  921.0 90.8 %collective-permute-start.145 = (bf16[2,4,2,32,1536]{4,3,2,1,0:T(8,128)(2,1)S(1)}, bf16[2,4,2,32,1536]{4,3,2,1,0:T(8,128)(2,1)S(1)}, u32[]{:S(2)}, u32[]{:S(2)}) collective-permute-start(bf16[2,4,2,32,1536]{4,3,2,1,0:T(8,128)(2,1)S(1)} %bitcast_dynamic-update-slice_fusion.43), channel_id=1, source_target_pairs={{0,8},{1,9},{2,10},{3,11},{4,12},{5,13},{6,14},{7,15},{8,0},{9,1},... | collective-permute-start | bytes 4718600 | tf_op jit(solution)/shard_map/ppermute | solution.py:93
  921.5 90.7 %collective-permute-start.151 = (bf16[2,4,2,32,1536]{4,3,2,1,0:T(8,128)(2,1)S(1)}, bf16[2,4,2,32,1536]{4,3,2,1,0:T(8,128)(2,1)S(1)}, u32[]{:S(2)}, u32[]{:S(2)}) collective-permute-start(bf16[2,4,2,32,1536]{4,3,2,1,0:T(8,128)(2,1)S(1)} %bitcast_dynamic-update-slice_fusion.40), channel_id=1, source_target_pairs={{0,8},{1,9},{2,10},{3,11},{4,12},{5,13},{6,14},{7,15},{8,0},{9,1},... | collective-permute-start | bytes 4718600 | tf_op jit(solution)/shard_map/ppermute | solution.py:93
  (298 other events, 3275.2 us)
Sparse Core Ops, SparseCore 0:
  383.8 131.7 all-gather.1

commit v2 on v1

v2 whole, which is shorter than its diff:
```python
import math

import jax
import jax.numpy as jnp
from jax import lax
from jax.experimental import pallas as pl
from jax.experimental.pallas import tpu as pltpu
from jax.sharding import PartitionSpec as P

HEADS = 8
HEAD_DIM = 128
EPSILON = 1e-06
THETA = 50000.0
AXES = ("dp", "seq")
BF16 = jnp.bfloat16
F32 = jnp.float32


def product(left_side, right_side):
    return jnp.dot(left_side, right_side, preferred_element_type=F32)


def across(left_side, right_side):
    return lax.dot_general(
        left_side, right_side, (((0,), (0,)), ((), ())), preferred_element_type=F32
    )


def against(left_side, right_side):
    return lax.dot_general(
        left_side, right_side, (((1,), (1,)), ((), ())), preferred_element_type=F32
    )


def norm_scale(values):
    return lax.rsqrt(jnp.mean(values * values, axis=-1, keepdims=True) + EPSILON)


def norm_back(values, scaling, gain_row, gradient):
    unit_rows = values * scaling
    weighted = gradient * gain_row
    moved = scaling * (
        weighted - unit_rows * jnp.mean(unit_rows * weighted, axis=-1, keepdims=True)
    )
    return (moved, jnp.sum(gradient * unit_rows, axis=0))


def rotate(values, cosine, sine_table):
    half_dim = values.shape[-1] // 2
    first_half = values[..., :half_dim]
    second_half = values[..., half_dim:]
    return jnp.concatenate(
        [
            first_half * cosine - second_half * sine_table,
            second_half * cosine + first_half * sine_table,
        ],
        axis=-1,
    )


def silu_grad(values):
    sigmoid_value = jax.nn.sigmoid(values)
    return sigmoid_value * (1.0 + values * (1.0 - sigmoid_value))


def tie(*values):
    return lax.optimization_barrier(values)


def tick(works, *values):
    flat = [part for work in works for part in work.parts]
    tied = list(lax.optimization_barrier(tuple(flat) + values))
    for work in works:
        count = len(work.parts)
        work.parts, tied = tied[:count], tied[count:]
    return tied


class Links:
    def __init__(self, n_dp, n_seq):
        self.count = n_dp * n_seq
        self.bits = (self.count - 1).bit_length()
        self.core = (n_dp - 1).bit_length() - 1
        self.last = self.bits - 1
        self.upper = list(range(self.core))
        self.inner = list(range(self.core + 1, self.last))
        self.index = lax.axis_index("dp") * n_seq + lax.axis_index("seq")
        self.seq_index = lax.axis_index("seq")
        self.pairs = [
            [(i, i ^ (1 << (self.bits - 1 - bit))) for i in range(self.count)]
            for bit in range(self.bits)
        ]
        self.steps = len(self.upper) + 1

    def own(self, bit):
        return (self.index >> (self.bits - 1 - bit)) & 1

    def swap(self, values, bit):
        return lax.ppermute(values, AXES, self.pairs[bit])


class Gathering:
    def __init__(self, links, shards):
        self.links = links
        self.heights = [shard.shape[0] for shard in shards]
        self.rows = sum(self.heights)
        shard = shards[0] if len(shards) == 1 else jnp.concatenate(shards, axis=0)
        self.parts = [shard]
        self.known = [[]]

    def widen(self, i, bit):
        links, part, known = self.links, self.parts[i], self.known[i]
        came = links.swap(part, bit)
        columns = part.shape[1]
        before = 1 << sum(1 for other in known if other < bit)
        mine = part.reshape(before, 1, -1, columns)
        both = jnp.zeros((before, 2) + mine.shape[2:], part.dtype)
        both = lax.dynamic_update_slice(both, mine, (0, links.own(bit), 0, 0))
        both = lax.dynamic_update_slice(
            both, came.reshape(mine.shape), (0, 1 - links.own(bit), 0, 0)
        )
        self.parts[i] = both.reshape(-1, columns)
        self.known[i] = known + [bit]

    def inside(self, step):
        self.widen(0, self.links.inner[step])

    def cross(self, step):
        links = self.links
        if len(self.parts) == 1:
            half = self.parts[0].shape[1] // 2
            self.parts = [self.parts[0][:, :half], self.parts[0][:, half:]]
            self.known = [self.known[0], self.known[0]]
        orders = ([links.last] + links.upper, links.upper + [links.last])
        for i in range(2):
            self.widen(i, orders[i][step])

    def core(self):
        self.parts += [self.links.swap(part, self.links.core) for part in self.parts]

    def finish(self):
        links = self.links
        before, half = 1 << len(links.upper), self.parts[0].shape[1]
        four = [part.reshape(before, -1, self.rows, half) for part in self.parts]
        wholes, row = [], 0
        for height in self.heights:
            piece = [part[:, :, row : row + height] for part in four]
            own = links.own(links.core)
            whole = jnp.zeros((before, 2) + piece[0].shape[1:3] + (2 * half,), piece[0].dtype)
            for i in range(4):
                place = own if i < 2 else 1 - own
                whole = lax.dynamic_update_slice(
                    whole, piece[i][:, None], (0, place, 0, 0, (i % 2) * half)
                )
            wholes.append(whole.reshape(-1, 2 * half))
            row += height
        return wholes

    def sources(self):
        columns = 2 * self.parts[0].shape[1]
        befores = 1 << len(self.links.upper)
        if len(self.heights) == 1:
            arrays = [part.reshape(befores, -1, part.shape[1]) for part in self.parts]
            return [Source(arrays, 0, arrays[0].shape[1], columns)]
        arrays = [part.reshape(-1, self.rows, part.shape[1]) for part in self.parts]
        sources, row = [], 0
        for height in self.heights:
            sources.append(Source(arrays, row, height, columns))
            row += height
        return sources


class Reduction:
    def __init__(self, links, wide):
        self.links, self.wide = links, wide
        self.terms, self.came = [], []

    def sides(self, left_side, which):
        blocks = 2 << len(self.links.upper)
        wide = left_side.shape[1] // blocks
        chosen = []
        for block in range(0, blocks, 2):
            first = left_side[:, block * wide : (block + 1) * wide]
            second = left_side[:, (block + 1) * wide : (block + 2) * wide]
            chosen.append(jnp.where(which == 0, first, second))
        return jnp.concatenate(chosen, axis=1)

    def send(self, left_side, right_side):
        links = self.links
        away = across(self.sides(left_side, 1 - links.own(links.core)), right_side)
        kept = self.sides(left_side, links.own(links.core))
        self.terms.append(lambda: across(kept, right_side))
        self.came.append(links.swap(away.astype(BF16), links.core))

    def send_rows(self, values):
        links = self.links
        halves = values.reshape(1 << len(links.upper), 2, -1, values.shape[1])
        own = links.own(links.core)
        away = lax.dynamic_index_in_dim(halves, 1 - own, 1, False).reshape(-1, values.shape[1])
        kept = lax.dynamic_index_in_dim(halves, own, 1, False).reshape(-1, values.shape[1])
        self.terms.append(lambda: kept)
        self.came.append(links.swap(away.astype(BF16), links.core))

    def add(self):
        links = self.links
        owners = links.count // 2
        total = []
        for term, came in zip(self.terms, self.came):
            item = (term() + came.astype(F32)).astype(BF16)
            item = item.reshape(owners, -1, item.shape[1])
            for start in range(0, item.shape[2], self.wide):
                total.append(item[:, :, start : start + self.wide])
        total = total[0] if len(total) == 1 else jnp.concatenate(total, axis=1)
        total = total.reshape(-1, total.shape[2])
        half = total.shape[1] // 2
        self.parts = [total[:, :half], total[:, half:]]
        left = [bit for bit in range(links.bits) if bit != links.core]
        self.left = [list(left), list(left)]

    def halve(self, i, bit, out_type=BF16):
        links, part = self.links, self.parts[i]
        columns = part.shape[1]
        before = 1 << sum(1 for other in self.left[i] if other < bit)
        both = part.reshape(before, 2, -1, columns)
        own = links.own(bit)
        away = lax.dynamic_index_in_dim(both, 1 - own, 1, False)
        kept = lax.dynamic_index_in_dim(both, own, 1, False)
        came = links.swap(away.reshape(-1, columns), bit)
        kept = kept.reshape(-1, columns).astype(F32) + came.astype(F32)
        self.parts[i] = kept.astype(out_type)
        self.left[i].remove(bit)

    def cross(self, step):
        links = self.links
        orders = (links.upper + [links.last], [links.last] + links.upper)
        for i in range(2):
            self.halve(i, orders[i][step])

    def join(self, other):
        owners = 1 << len(self.left[0])
        for i in range(2):
            both = [part.reshape(owners, -1, part.shape[1]) for part in (self.parts[i], other.parts[i])]
            self.parts[i] = jnp.concatenate(both, axis=1).reshape(-1, both[0].shape[2])

    def inside(self, step):
        if len(self.parts) == 2:
            self.parts = [jnp.concatenate(self.parts, axis=1)]
        final = step == len(self.links.inner) - 1
        self.halve(0, self.links.inner[-1 - step], F32 if final else BF16)


class Source:
    def __init__(self, arrays, start, height, columns):
        self.arrays, self.start, self.height, self.columns = arrays, start, height, columns


def shampoo(links, matrices, roots):
    side = roots.shape[0]
    big = [roots]
    for source, *_ in matrices:
        for array in source.arrays:
            if not any(array is other for other in big):
                big.append(array)
    place = {id(array): i for i, array in enumerate(big)}
    small, out_shape, scratch, copies = [], [], [], 0
    for source, shard, left_stat, right_stat, root, weight, which in matrices:
        rows, columns = left_stat.shape[1], right_stat.shape[1]
        small += [shard, left_stat, right_stat, root] + ([] if weight is None else [weight])
        out_shape += [
            jax.ShapeDtypeStruct(left_stat.shape, F32),
            jax.ShapeDtypeStruct(right_stat.shape, F32),
            jax.ShapeDtypeStruct(
                (right_stat.shape[0], rows) if weight is None else weight.shape,
                BF16 if weight is None else F32,
            ),
        ]
        if len(source.arrays) == 1:
            scratch.append(pltpu.VMEM((1, rows, columns), BF16))
            copies += 1
        else:
            blocks = 2 * source.arrays[0].shape[0]
            scratch.append(pltpu.VMEM((blocks, rows // blocks, columns), BF16))
            copies += 4 << len(links.upper)
        scratch.append(pltpu.VMEM((side, side), BF16))
        copies += 1
    bits = jnp.stack([links.index, links.own(links.core)]).astype(jnp.int32)

    def kernel(*refs):
        place_ref, refs = refs[0], list(refs[1:])
        bigs, refs = refs[: len(big)], refs[len(big) :]
        smalls, refs = refs[: len(small)], refs[len(small) :]
        outs, refs = refs[: len(out_shape)], refs[len(out_shape) :]
        scratches, done = refs[: len(scratch)], refs[-1]
        index, own = place_ref[0], place_ref[1]
        started, used = [], 0
        for i, (source, *_, which) in enumerate(matrices):
            whole, root = scratches[2 * i], scratches[2 * i + 1]
            mine = []
            if len(source.arrays) == 1:
                ref = bigs[place[id(source.arrays[0])]]
                mine.append((ref.at[:, pl.ds(source.start, source.columns)], whole.at[0]))
            else:
                befores = 1 << len(links.upper)
                deep = source.arrays[0].shape[0] // befores
                half = source.arrays[0].shape[2]
                for part in range(4):
                    ref = bigs[place[id(source.arrays[part])]]
                    core = own if part < 2 else 1 - own
                    for before in range(befores):
                        mine.append(
                            (
                                ref.at[
                                    pl.ds(before * deep, deep), pl.ds(source.start, source.height)
                                ],
                                whole.at[
                                    pl.ds((2 * before + core) * deep, deep),
                                    :,
                                    pl.ds((part % 2) * half, half),
                                ],
                            )
                        )
            mine.append((bigs[0].at[:, pl.ds(which * side, side)], root))
            group = []
            for from_ref, to_ref in mine:
                copy = pltpu.make_async_copy(from_ref, to_ref, done.at[used])
                copy.start()
                group.append(copy)
                used += 1
            started.append(group)
        for i, (source, shard, left_stat, right_stat, root, weight, which) in enumerate(matrices):
            for copy in started[i]:
                copy.wait()
            rows, columns = left_stat.shape[1], right_stat.shape[1]
            high, wide = left_stat.shape[0], right_stat.shape[0]
            whole = scratches[2 * i][...].reshape(rows, columns)
            shard_ref, left_ref, right_ref, root_ref = smalls[:4]
            lane = lax.broadcasted_iota(jnp.int32, (wide, columns), 1)
            row = lax.broadcasted_iota(jnp.int32, (wide, columns), 0)
            pick = (lane == row + index * wide).astype(F32)
            stacked = [shard_ref[...], pick] + ([root_ref[...]] if weight is None else [])
            first = against(jnp.concatenate(stacked, axis=0).astype(BF16), whole)
            outs[3 * i][...] = 0.5 * left_ref[...] + (0.5 / columns) * first[:high]
            picked = first[high : high + wide]
            other = scratches[2 * i + 1][...]
            if weight is None:
                second = product(picked.astype(BF16), whole)
                outs[3 * i + 1][...] = 0.5 * right_ref[...] + (0.5 / rows) * second
                turned = first[high + wide :].astype(BF16)
                outs[3 * i + 2][...] = product(turned, other).astype(BF16)
                smalls = smalls[4:]
            else:
                second = product(
                    jnp.concatenate([root_ref[...], picked], axis=0).astype(BF16), whole
                )
                outs[3 * i + 1][...] = 0.5 * right_ref[...] + (0.5 / rows) * second[high:]
                step = product(second[:high].astype(BF16), other)
                outs[3 * i + 2][...] = smalls[4][...] - step * (1.0 / math.sqrt(rows))
                smalls = smalls[5:]

    vmem = pl.BlockSpec(memory_space=pltpu.VMEM)
    results = pl.pallas_call(
        kernel,
        out_shape=out_shape,
        in_specs=[pl.BlockSpec(memory_space=pltpu.SMEM)]
        + [pl.BlockSpec(memory_space=pl.ANY)] * len(big)
        + [vmem] * len(small),
        out_specs=[vmem] * len(out_shape),
        scratch_shapes=scratch + [pltpu.SemaphoreType.DMA((copies,))],
        compiler_params=pltpu.CompilerParams(vmem_limit_bytes=56 << 20),
    )(bits, *big, *small)
    return [results[3 * i : 3 * i + 3] for i in range(len(matrices))]


def body(
    embedding,
    latent,
    segment_ids,
    cotangent,
    weight_adapt,
    weight_attn,
    weight_gateup,
    weight_down,
    norm_gains,
    left_adapt,
    right_adapt,
    left_attn,
    right_attn,
    left_gateup,
    right_gateup,
    left_down,
    right_down,
    left_root_adapt,
    right_root_adapt,
    left_root_attn,
    right_root_attn,
    left_root_gateup,
    right_root_gateup,
    left_root_down,
    right_root_down,
    gain_moment,
):
    n_dp, n_seq = lax.axis_size("dp"), lax.axis_size("seq")
    links = Links(n_dp, n_seq)
    seq_count, group_len, width = embedding.shape
    tokens = seq_count * group_len
    length = group_len * n_seq
    hidden_width = weight_gateup.shape[2]
    by_heads = HEADS % n_seq == 0

    gateup_rows = weight_gateup.astype(BF16)
    down_rows = weight_down.astype(BF16).reshape(-1, hidden_width)
    feed_full = lax.all_gather(
        jnp.concatenate([gateup_rows[0], gateup_rows[1], down_rows], axis=1),
        AXES,
        axis=0,
        tiled=True,
    )
    gain_share = norm_gains.shape[1]
    small = jnp.concatenate(
        [norm_gains.astype(BF16).reshape(-1), segment_ids.astype(BF16).reshape(-1)]
    )
    small = jnp.pad(small[None], ((0, 7), (0, width - small.shape[0])))
    attn_rows = weight_attn.astype(BF16)
    first = Gathering(links, [weight_adapt.astype(BF16), small])
    second = Gathering(links, [attn_rows[i] for i in range(4)])
    inner_steps, cross_steps = range(len(links.inner)), range(links.steps)
    for step in inner_steps:
        first.inside(step)
    tick([first, second])
    for step in inner_steps:
        second.inside(step)
    for step in cross_steps:
        first.cross(step)
    tick([first, second])
    first.core()
    adapt_full, small = first.finish()
    for step in cross_steps:
        second.cross(step)
    second.core()
    query_full, key_full, value_full, out_full = second.finish()

    small = small.reshape(links.count, 8, width)[:, 0]
    gain_values = small[:, : 4 * gain_share].reshape(links.count, 4, gain_share)
    gain_values = gain_values.transpose(1, 0, 2).reshape(4, width).astype(F32)
    ids = small[:, 4 * gain_share : 4 * gain_share + tokens].reshape(n_dp, n_seq, seq_count, -1)
    ids = lax.dynamic_index_in_dim(ids, lax.axis_index("dp"), 0, False)
    segment_whole = ids.transpose(1, 0, 2).reshape(seq_count, length).astype(jnp.int32)

    all_places = jnp.arange(length, dtype=jnp.int32)
    doc_starts = jnp.sum(
        (segment_whole[:, None, :] < segment_whole[:, :, None]).astype(jnp.int32), axis=2
    )
    places = all_places[None, :] - doc_starts
    half_dim = HEAD_DIM // 2
    frequency = THETA ** (-jnp.arange(half_dim, dtype=F32) / half_dim)
    angles = places.astype(F32)[..., None] * frequency
    cosine_all, sine_all = jnp.cos(angles), jnp.sin(angles)
    own_start = links.seq_index * group_len
    cosine = lax.dynamic_slice_in_dim(cosine_all, own_start, group_len, 1)
    sine_table = lax.dynamic_slice_in_dim(sine_all, own_start, group_len, 1)
    if by_heads:
        query_places, segment_query = all_places, segment_whole
        cosine_back, sine_back = cosine_all[:, None], sine_all[:, None]
    else:
        query_places, segment_query = own_start + jnp.arange(group_len), segment_ids
        cosine_back, sine_back = cosine[:, None], sine_table[:, None]
    allowed = (all_places[None, None, :] <= query_places[None, :, None]) & (
        segment_whole[:, None, :] == segment_query[:, :, None]
    )

    def to_heads(values):
        parts = values.shape[2]
        values = values.transpose(3, 2, 0, 1, 4)
        came = lax.all_to_all(values, "seq", 0, 0, tiled=True)
        came = came.reshape(n_seq, HEADS // n_seq, parts, seq_count, group_len, HEAD_DIM)
        came = came.transpose(2, 3, 1, 0, 4, 5)
        return came.reshape(parts, seq_count, HEADS // n_seq, length, HEAD_DIM)

    def to_tokens(values):
        parts = values.shape[0]
        own = HEADS // n_seq
        values = values.reshape(parts, seq_count, own, n_seq, group_len, HEAD_DIM)
        values = values.transpose(3, 2, 0, 1, 4, 5)
        came = lax.all_to_all(values, "seq", 0, 0, tiled=True)
        came = came.reshape(HEADS, parts, seq_count, group_len, HEAD_DIM)
        return came.transpose(1, 2, 3, 0, 4)

    scaling = 1.0 / math.sqrt(HEAD_DIM)

    def attention(queries, keys, values, with_feed):
        if by_heads:
            queries, keys, values = to_heads(jnp.stack([queries, keys, values], axis=2))
        else:
            queries = queries.transpose(0, 2, 1, 3)
            keys, values = (
                lax.all_gather(item, "seq", axis=1, tiled=True).transpose(0, 2, 1, 3)
                for item in (keys, values)
            )
        if with_feed:
            queries, feed[0], feed[1] = tie(queries, feed[0], feed[1])
        scores = jnp.einsum("shqd,shkd->shqk", queries, keys, preferred_element_type=F32)
        scores = jnp.where(allowed[:, None], scores * scaling, -1e30)
        exponent = jnp.exp(scores - jnp.max(scores, axis=-1, keepdims=True))
        soft_full = exponent / jnp.sum(exponent, axis=-1, keepdims=True)
        mixed = jnp.einsum(
            "shqk,shkd->shqd", soft_full.astype(BF16), values, preferred_element_type=F32
        ).astype(BF16)
        if by_heads:
            mixed = to_tokens(mixed[None])[0]
        else:
            mixed = mixed.transpose(0, 2, 1, 3)
        return mixed.reshape(tokens, width), (queries, keys, values, soft_full)

    def attention_back(mixed_grad, saved):
        queries, keys, values, soft_full = saved
        soft_grad = jnp.einsum("shqd,shkd->shqk", mixed_grad, values, preferred_element_type=F32)
        inner_sum = jnp.sum(soft_full * soft_grad, axis=-1, keepdims=True)
        score_grad = (soft_full * (soft_grad - inner_sum)).astype(BF16)
        query_grad = (
            jnp.einsum("shqk,shkd->shqd", score_grad, keys, preferred_element_type=F32) * scaling
        )
        key_grad = (
            jnp.einsum("shqk,shqd->shkd", score_grad, queries, preferred_element_type=F32)
            * scaling
        )
        value_grad = jnp.einsum(
            "shqk,shqd->shkd", soft_full.astype(BF16), mixed_grad, preferred_element_type=F32
        )
        if by_heads:
            query_grad = rotate(query_grad, cosine_back, -sine_back).astype(BF16)
            key_grad = rotate(key_grad, cosine_back, -sine_back).astype(BF16)
            value_grad = value_grad.astype(BF16)
            return jnp.stack([query_grad, key_grad, value_grad])
        key_grad, value_grad = (
            lax.psum_scatter(item.astype(BF16), "seq", scatter_dimension=2, tiled=True).astype(F32)
            for item in (key_grad, value_grad)
        )
        query_grad = rotate(query_grad, cosine_back, -sine_back).astype(BF16)
        key_grad = rotate(key_grad, cosine_back, -sine_back).astype(BF16)
        grads = jnp.stack([query_grad, key_grad, value_grad.astype(BF16)])
        return grads.transpose(0, 1, 3, 2, 4)

    embed_flat = embedding.reshape(tokens, width)
    embed_part = product(embed_flat, adapt_full[width:])
    embed_part, feed_full = tie(embed_part, feed_full)
    feed = [
        feed_full[:, : 2 * hidden_width],
        feed_full[:, 2 * hidden_width :].reshape(hidden_width, width),
    ]

    roots = []

    def forward(latent_low, with_roots=False):
        start_sum = product(latent_low, adapt_full[:width]) + embed_part
        scale_one = norm_scale(start_sum)
        normed_one = (start_sum * scale_one * gain_values[0]).astype(BF16)
        head_shape = (seq_count, group_len, HEADS, HEAD_DIM)
        turn_cos, turn_sin = cosine[:, :, None, :], sine_table[:, :, None, :]
        queries = product(normed_one, query_full).reshape(head_shape)
        queries = rotate(queries, turn_cos, turn_sin).astype(BF16)
        keys = product(normed_one, key_full).reshape(head_shape)
        keys = rotate(keys, turn_cos, turn_sin).astype(BF16)
        values = product(normed_one, value_full).astype(BF16).reshape(head_shape)
        mixed_heads, attended = attention(queries, keys, values, with_roots)
        if with_roots:
            root_stack = jnp.concatenate(
                [
                    right_root_adapt.astype(BF16)[:, None],
                    right_root_attn.astype(BF16).transpose(1, 0, 2),
                    right_root_down.astype(BF16)[:, None],
                    left_root_gateup.astype(BF16).transpose(1, 0, 2),
                ],
                axis=1,
            )
            share = root_stack.shape[0]
            root_stack, mixed_heads = tie(root_stack.reshape(share, 8 * width), mixed_heads)
            roots.append(lax.all_gather(root_stack, AXES, axis=0, tiled=True))
        branch = product(mixed_heads, out_full)
        scale_two = norm_scale(branch)
        middle = start_sum + branch * scale_two * gain_values[1]
        scale_three = norm_scale(middle)
        normed_three = (middle * scale_three * gain_values[2]).astype(BF16)
        gateup_full, down_full = feed
        both = product(normed_three, gateup_full)
        gate_value, upward = both[:, :hidden_width], both[:, hidden_width:]
        hidden = (jax.nn.silu(gate_value) * upward).astype(BF16)
        feed_out = product(hidden, down_full)
        scale_four = norm_scale(feed_out)
        result = middle + feed_out * scale_four * gain_values[3]
        saved_values = (
            start_sum,
            scale_one,
            normed_one,
            attended,
            mixed_heads,
            branch,
            scale_two,
            middle,
            scale_three,
            normed_three,
            gate_value,
            upward,
            hidden,
            feed_out,
            scale_four,
        )
        return (result, saved_values)

    latent_low = latent.reshape(tokens, width)
    latent_state, unused_saved = forward(latent_low, True)
    latent_low = latent_state.astype(BF16)
    final_state, saved_values = forward(latent_low)
    (
        start_sum,
        scale_one,
        normed_one,
        attended,
        mixed_heads,
        branch,
        scale_two,
        middle,
        scale_three,
        normed_three,
        gate_value,
        upward,
        hidden,
        feed_out,
        scale_four,
    ) = saved_values
    factor = 1.0 / math.sqrt(seq_count * n_dp * length)
    incoming = cotangent.astype(F32).reshape(tokens, width)
    feed_grad, gain_four = norm_back(feed_out, scale_four, gain_values[3], incoming)
    feed_grad = feed_grad.astype(BF16)
    down_sum = Reduction(links, width)
    down_sum.send(hidden, feed_grad)
    gateup_full, down_full = feed
    hidden_grad = against(feed_grad, down_full)
    gate_grad = (hidden_grad * upward * silu_grad(gate_value)).astype(BF16)
    up_grad = (hidden_grad * jax.nn.silu(gate_value)).astype(BF16)
    gateup_sum = Reduction(links, hidden_width)
    gateup_sum.send(normed_three, gate_grad)
    gateup_sum.send(normed_three, up_grad)
    both_grad = jnp.concatenate([gate_grad, up_grad], axis=1)
    normed_three_grad = against(both_grad, gateup_full)
    middle_grad, gain_three = norm_back(middle, scale_three, gain_values[2], normed_three_grad)
    middle_grad = middle_grad + incoming
    branch_grad, gain_two = norm_back(branch, scale_two, gain_values[1], middle_grad)
    branch_grad = branch_grad.astype(BF16)
    mixed_grad = against(branch_grad, out_full).astype(BF16)
    rest_sum = Reduction(links, width)
    rest_sum.send(mixed_heads, branch_grad)
    down_sum.add()
    (mixed_grad,) = tick([down_sum], mixed_grad)
    mixed_grad = mixed_grad.reshape(seq_count, group_len, HEADS, HEAD_DIM)
    if by_heads:
        mixed_grad = to_heads(mixed_grad[:, :, None])[0]
    else:
        mixed_grad = mixed_grad.transpose(0, 2, 1, 3)
    down_sum.cross(0)
    gateup_sum.add()
    (mixed_grad,) = tick([down_sum, gateup_sum], mixed_grad)
    grads = attention_back(mixed_grad, attended)
    for step in cross_steps[1:]:
        down_sum.cross(step)
    gateup_sum.cross(0)
    if by_heads:
        grads = to_tokens(grads)
    query_pre, key_pre, value_pre = grads.reshape(3, tokens, width)
    query_pre, key_pre, value_pre = tick([down_sum, gateup_sum], query_pre, key_pre, value_pre)
    for step in cross_steps[1:]:
        gateup_sum.cross(step)
    rest_sum.send(normed_one, jnp.concatenate([query_pre, key_pre, value_pre], axis=1))
    normed_one_grad = (
        against(query_pre, query_full) + against(key_pre, key_full) + against(value_pre, value_full)
    )
    start_grad, gain_one = norm_back(start_sum, scale_one, gain_values[0], normed_one_grad)
    start_grad = (start_grad + middle_grad).astype(BF16)
    joined = jnp.concatenate([latent_low, embed_flat], axis=1)
    rest_sum.send(joined, start_grad)
    gain_sums = jnp.stack([gain_one, gain_two, gain_three, gain_four])
    gain_sums = gain_sums.reshape(4, links.count, gain_share).transpose(1, 0, 2)
    gain_sums = gain_sums.reshape(links.count, 1, 4 * gain_share)
    gain_sums = jnp.pad(gain_sums, ((0, 0), (0, 7), (0, width - 4 * gain_share)))
    rest_sum.send_rows(gain_sums.reshape(-1, width))
    rest_sum.add()
    start_grad, root_rows = tick([gateup_sum, down_sum, rest_sum], start_grad, roots[0])
    rest_sum.cross(0)
    for step in inner_steps:
        down_sum.inside(step)
    for step in inner_steps:
        gateup_sum.inside(step)
    tick([rest_sum, gateup_sum, down_sum])
    reduced_down = down_sum.parts[0] * factor
    first = Gathering(links, [reduced_down.astype(BF16)])
    left_root_adapt, left_root_attn, left_root_down, right_root_gateup, reduced_down = tie(
        left_root_adapt, left_root_attn, left_root_down, right_root_gateup, reduced_down
    )
    for step in cross_steps[1:]:
        rest_sum.cross(step)
    gate_shards = (gateup_sum.parts[0] * factor).reshape(2, -1, hidden_width)
    full_both = lax.all_gather(
        jnp.concatenate([gate_shards[0], gate_shards[1]], axis=1).astype(BF16),
        AXES,
        axis=0,
        tiled=True,
    )
    first.inside(0)
    tick([rest_sum, first])
    rest_sum.inside(0)
    for step in inner_steps[1:]:
        first.inside(step)
    tick([rest_sum, first])
    for step in inner_steps[1:]:
        rest_sum.inside(step)
    first.cross(0)
    tick([rest_sum, first])
    reduced_rest = rest_sum.parts[0] * factor
    row_share = width // links.count
    attn_shards = reduced_rest[: 4 * row_share].reshape(4, row_share, width)
    attn_shards = jnp.concatenate([attn_shards[1:], attn_shards[:1]], axis=0)
    reduced_adapt = reduced_rest[4 * row_share : 6 * row_share]
    reduced_gains = reduced_rest[6 * row_share, : 4 * gain_share].reshape(4, gain_share)
    third = Gathering(
        links, [attn_shards[i].astype(BF16) for i in range(4)] + [reduced_adapt.astype(BF16)]
    )
    third.inside(0)
    for step in cross_steps[1:]:
        first.cross(step)
    tick([third, first])
    for step in inner_steps[1:]:
        third.inside(step)
    first.core()
    tick([third, first])
    third.cross(0)
    tick([third])
    for step in cross_steps[1:]:
        third.cross(step)
    tick([third])
    third.core()
    tick([third])
    grad_embedding = against(start_grad, adapt_full[width:]).reshape(
        seq_count, group_len, width
    )
    def statistics(shard, whole, left_stat, right_stat, left_root):
        rows, columns = whole.shape
        new_left = 0.5 * left_stat + (0.5 / columns) * against(shard.astype(BF16), whole)
        count = right_stat.shape[0]
        own = lax.dynamic_slice_in_dim(whole, links.index * count, count, 1).T
        if left_root is None:
            return (new_left, 0.5 * right_stat + (0.5 / rows) * product(own, whole), None)
        own_count = left_root.shape[0]
        both = product(jnp.concatenate([left_root.astype(BF16), own], axis=0), whole)
        return (new_left, 0.5 * right_stat + (0.5 / rows) * both[own_count:], both[:own_count])

    def step(part, which, rows):
        root = root_rows[:, which * width : (which + 1) * width]
        return product(part.astype(BF16), root) * (1.0 / math.sqrt(rows))

    fits = row_share % 16 == 0
    if fits:
        gateup_parts = shampoo(
            links,
            [
                (
                    Source([full_both], i * hidden_width, width, hidden_width),
                    gate_shards[i],
                    left_gateup[i],
                    right_gateup[i],
                    right_root_gateup[i],
                    None,
                    6 + i,
                )
                for i in range(2)
            ],
            root_rows,
        )
        step_columns = jnp.stack([member[2].T for member in gateup_parts])
    else:
        whole_gates = [full_both[:, :hidden_width], full_both[:, hidden_width:]]
        gateup_parts = [
            statistics(gate_shards[i], whole_gates[i], left_gateup[i], right_gateup[i], None)
            for i in range(2)
        ]
        step_columns = []
        for i in range(2):
            turned = against(whole_gates[i], right_root_gateup[i].astype(BF16)).astype(BF16)
            root = root_rows[:, (6 + i) * width : (7 + i) * width]
            step_columns.append(product(root, turned).astype(BF16))
        step_columns = jnp.stack(step_columns)
    ff_share = step_columns.shape[2]
    step_columns = step_columns.reshape(2, links.count, row_share, ff_share).transpose(1, 0, 2, 3)
    step_rows = lax.all_to_all(step_columns, AXES, 0, 0, tiled=True)
    step_gateup = step_rows.transpose(1, 2, 0, 3).reshape(2, row_share, hidden_width)
    new_gateup = weight_gateup - step_gateup.astype(F32) * (1.0 / math.sqrt(width))

    if fits:
        ((new_left_down, new_right_down, new_down),) = shampoo(
            links,
            [
                (
                    first.sources()[0],
                    reduced_down,
                    left_down,
                    right_down,
                    left_root_down,
                    weight_down,
                    5,
                )
            ],
            root_rows,
        )
        sources = third.sources()
        attn_parts = [
            (
                sources[i],
                attn_shards[i],
                left_attn[i],
                right_attn[i],
                left_root_attn[i],
                weight_attn[i],
                1 + i,
            )
            for i in range(4)
        ]
        adapt_part = (
            sources[4],
            reduced_adapt,
            left_adapt,
            right_adapt,
            left_root_adapt,
            weight_adapt,
            0,
        )
        *attn_parts, (new_left_adapt, new_right_adapt, new_adapt) = shampoo(
            links, attn_parts + [adapt_part], root_rows
        )
        new_attn = jnp.stack([member[2] for member in attn_parts])
    else:
        (full_down,) = first.finish()
        *attn_wholes, full_adapt = third.finish()
        new_left_down, new_right_down, down_part = statistics(
            reduced_down, full_down, left_down, right_down, left_root_down
        )
        new_down = weight_down - step(down_part, 5, hidden_width)
        attn_parts = [
            statistics(
                attn_shards[i], attn_wholes[i], left_attn[i], right_attn[i], left_root_attn[i]
            )
            for i in range(4)
        ]
        new_attn = weight_attn - jnp.stack(
            [step(attn_parts[i][2], 1 + i, width) for i in range(4)]
        )
        new_left_adapt, new_right_adapt, adapt_part = statistics(
            reduced_adapt, full_adapt, left_adapt, right_adapt, left_root_adapt
        )
        new_adapt = weight_adapt - step(adapt_part, 0, 2 * width)
    new_gain_moment = 0.5 * gain_moment + 0.5 * reduced_gains * reduced_gains
    new_norm_gains = norm_gains - 0.5 * reduced_gains / (jnp.sqrt(new_gain_moment) + 1e-08)
    latent_out = final_state.reshape(seq_count, group_len, width).astype(BF16)
    return (
        latent_out,
        grad_embedding,
        reduced_adapt,
        attn_shards,
        gate_shards,
        reduced_down,
        reduced_gains,
        new_left_adapt,
        new_right_adapt,
        jnp.stack([member[0] for member in attn_parts]),
        jnp.stack([member[1] for member in attn_parts]),
        jnp.stack([member[0] for member in gateup_parts]),
        jnp.stack([member[1] for member in gateup_parts]),
        new_left_down,
        new_right_down,
        new_adapt,
        new_attn,
        new_gateup,
        new_down,
        new_gain_moment,
        new_norm_gains,
    )

def solution(mesh):
    return jax.shard_map(
        body,
        mesh=mesh,
        in_specs=(
            P("dp", "seq", None),
            P("dp", "seq", None),
            P("dp", "seq"),
            P("dp", "seq", None),
            P(("dp", "seq"), None),
            P(None, ("dp", "seq"), None),
            P(None, ("dp", "seq"), None),
            P(("dp", "seq"), None),
            P(None, ("dp", "seq")),
            P(("dp", "seq"), None),
            P(("dp", "seq"), None),
            P(None, ("dp", "seq"), None),
            P(None, ("dp", "seq"), None),
            P(None, ("dp", "seq"), None),
            P(None, ("dp", "seq"), None),
            P(("dp", "seq"), None),
            P(("dp", "seq"), None),
            P(("dp", "seq"), None),
            P(("dp", "seq"), None),
            P(None, ("dp", "seq"), None),
            P(None, ("dp", "seq"), None),
            P(None, ("dp", "seq"), None),
            P(None, ("dp", "seq"), None),
            P(("dp", "seq"), None),
            P(("dp", "seq"), None),
            P(None, ("dp", "seq")),
        ),
        out_specs=(
            P("dp", "seq", None),
            P("dp", "seq", None),
            P(("dp", "seq"), None),
            P(None, ("dp", "seq"), None),
            P(None, ("dp", "seq"), None),
            P(("dp", "seq"), None),
            P(None, ("dp", "seq")),
            P(("dp", "seq"), None),
            P(("dp", "seq"), None),
            P(None, ("dp", "seq"), None),
            P(None, ("dp", "seq"), None),
            P(None, ("dp", "seq"), None),
            P(None, ("dp", "seq"), None),
            P(("dp", "seq"), None),
            P(("dp", "seq"), None),
            P(("dp", "seq"), None),
            P(None, ("dp", "seq"), None),
            P(None, ("dp", "seq"), None),
            P(("dp", "seq"), None),
            P(None, ("dp", "seq")),
            P(None, ("dp", "seq")),
        ),
        check_vma=False,
    )
```

time: 1130 us -> 870 us (0.77)
  starting transfers between devices: 262 us -> 92.6 us
  local copies, waits for them, and re-layouts: 256 us -> 144 us
  matrix products: 155 us -> 81.1 us
  waiting for transfers between devices: 379 us -> 429 us
  Pallas kernels: 0 us -> 36.4 us
    ppermute x188 -> x57, starting transfers between devices: 231 us -> 61.5 us  [swap(): return lax.ppermute(values, AXES, self.pairs[bit])]
    dynamic_update_slice x199 -> x63, local copies, waits for them, and re-layouts: 108 us -> 28.4 us  [the longest x15 14.1 us: finish(): lax.dynamic_update_slice(whole, piece[i][:, None], (0, place, 0, 0, i % 2...]
    dot_general x27 -> x15, matrix products: 73 us -> 24.1 us  [product(): return jnp.dot(left_side, right_side, preferred_element_type=F32)]
    another operation x78 -> x14, local copies, waits for them, and re-layouts: 39.7 us -> 2.8 us
    pallas_call x0 -> x3, Pallas kernels: none -> 36.4 us  [shampoo(): pl.pallas_call(kernel, out_shape=out_shape, in_specs=[pl.BlockSpec(memory...]
    dot_general x13 -> x7, matrix products: 41.5 us -> 12 us  [against(): lax.dot_general(left_side, right_side, (((1,), (1,)), ((), ())), preferre...]
    ppermute x188 -> x57, waiting for transfers between devices: 341 us -> 367 us  [swap(): return lax.ppermute(values, AXES, self.pairs[bit])]
    reshape x2 -> x16, local copies, waits for them, and re-layouts: 2.1 us -> 18.6 us  [the longest x1 11.7 us: body(): feed_full[:, 2 * hidden_width:].reshape(hidden_width, width)]
  transfers between devices with their start and end apart: 196 -> 67, of which waited for: 93 -> 30; matrix products, arithmetic and copies ran while one was open for 36% -> 28% of each run, Pallas kernels for 0% -> 3%
where the time goes in v2:
time: 870 us; the launch traced here: 858 us
  waiting for transfers between devices  429 us (49%)
  local copies, waits for them, and re-layouts  144 us (17%)
  starting transfers between devices  92.6 us (11%)
  matrix products  81.1 us (9%)
  other arithmetic  57.3 us (7%)
  Pallas kernels  36.4 us (4%)
  between operations  17.2 us (2%)
    ppermute x57, waiting for transfers between devices, swap(): return lax.ppermute(values, AXES, self.pairs[bit])  367 us
    ppermute x57, starting transfers between devices, swap(): return lax.ppermute(values, AXES, self.pairs[bit])  61.5 us
    all_to_all x3, waiting for transfers between devices, to_heads(): came = lax.all_to_all(values, 'seq', 0, 0, tiled=True)  36.6 us
    pallas_call x3, Pallas kernels, shampoo(): pl.pallas_call(kernel, out_shape=out_shape, in_specs=[pl.BlockSpec(memory...  36.4 us
    dot_general x12, matrix products, across(): lax.dot_general(left_side, right_side, (((0,), (0,)), ((), ())), preferre...  29.4 us
    dot_general x15, matrix products, product(): return jnp.dot(left_side, right_side, preferred_element_type=F32)  24.1 us
    convert_element_type x15, other arithmetic, halve(): self.parts[i] = kept.astype(out_type)  18.7 us
  transfers between devices with their start and end apart: 67, of which 30 were waited for; matrix products, arithmetic and copies ran while one was open for 28% of the time, Pallas kernels for 3%

profile of v2, /device:TPU:0, one launch (start us, length us, event | category | flops | bytes accessed | tf_op | source)
XLA Modules:
  0.0 858.3 jit_solution(15183132288210788906)
XLA Ops:
  23.0 14.7 %collective-permute-done.1 = bf16[144,1024]{1,0:T(8,128)(2,1)S(1)} collective-permute-done((bf16[144,1024]{1,0:T(8,128)(2,1)S(1)}, bf16[144,1024]{1,0:T(8,128)(2,1)S(1)}, u32[]{:S(2)}, u32[]{:S(2)}) %collective-permute-start.1) | collective-permute-done | bytes 294944 | tf_op jit(solution)/shard_map/ppermute | solution.py:99
  47.8 19.3 %collective-permute-done.6 = bf16[128,1024]{1,0:T(8,128)(2,1)S(1)} collective-permute-done((bf16[128,1024]{1,0:T(8,128)(2,1)S(1)}, bf16[128,1024]{1,0:T(8,128)(2,1)S(1)}, u32[]{:S(2)}, u32[]{:S(2)}) %collective-permute-start.6) | collective-permute-done | bytes 262176 | tf_op jit(solution)/shard_map/ppermute | solution.py:99
  74.5 16.3 %collective-permute-done.7 = bf16[256,1024]{1,0:T(8,128)(2,1)S(1)} collective-permute-done((bf16[256,1024]{1,0:T(8,128)(2,1)S(1)}, bf16[256,1024]{1,0:T(8,128)(2,1)S(1)}, u32[]{:S(2)}, u32[]{:S(2)}) %collective-permute-start.7) | collective-permute-done | bytes 524320 | tf_op jit(solution)/shard_map/ppermute | solution.py:99
  98.1 18.2 %collective-permute-done.12 = bf16[512,512]{1,0:T(8,128)(2,1)S(1)} collective-permute-done((bf16[512,512]{1,0:T(8,128)(2,1)S(1)}, bf16[512,512]{1,0:T(8,128)(2,1)S(1)}, u32[]{:S(2)}, u32[]{:S(2)}) %collective-permute-start.12) | collective-permute-done | bytes 524320 | tf_op jit(solution)/shard_map/ppermute | solution.py:99
  137.0 21.4 %collective-permute-done.11 = bf16[1024,512]{1,0:T(8,128)(2,1)} collective-permute-done((bf16[1024,512]{1,0:T(8,128)(2,1)}, bf16[1024,512]{1,0:T(8,128)(2,1)}, u32[]{:S(2)}, u32[]{:S(2)}) %collective-permute-start.11) | collective-permute-done | bytes 1048608 | tf_op jit(solution)/shard_map/ppermute | solution.py:99
  210.8 9.9 %slice.496 = bf16[1024,5632]{1,0:T(8,128)(2,1)} slice(bf16[1024,8448]{1,0:T(8,128)(2,1)} %all-gather.4.cloned.1.call-done), slice={[0:1024], [0:5632]} | slice | bytes 23068672 | tf_op jit(solution)/shard_map/slice | solution.py:547
  220.7 11.7 %reshape.1166 = bf16[2816,1024]{1,0:T(8,128)(2,1)} reshape(bf16[1024,2816]{1,0:T(8,128)(2,1)} %slice.497) | data formatting | bytes 11534336 | tf_op jit(solution)/shard_map/reshape | solution.py:548
  276.3 31.5 %all-to-all-done.2 = bf16[8,3,2,64,128]{4,3,2,1,0:T(8,128)(2,1)} async-done(((bf16[8,3,2,64,128]{4,3,2,1,0:T(8,128)(2,1)}), bf16[8,3,2,64,128]{4,3,2,1,0:T(8,128)(2,1)}, u32[]{:S(2)}, u32[]{:S(2)}) %all-to-all-start.2) | async-done | bytes 786464 | tf_op jit(solution)/shard_map/all_to_all | solution.py:474
  323.2 12.7 %all-to-all-done.3 = bf16[8,1,1,2,64,128]{5,4,3,2,1,0:T(8,128)(2,1)S(1)} async-done(((bf16[8,1,1,2,64,128]{5,4,3,2,1,0:T(8,128)(2,1)}), bf16[8,1,1,2,64,128]{5,4,3,2,1,0:T(8,128)(2,1)S(1)}, u32[]{:S(2)}, u32[]{:S(2)}) %all-to-all-start.3) | async-done | bytes 262176 | tf_op jit(solution)/shard_map/all_to_all | solution.py:484
  423.0 30.0 %collective-permute-done.22 = bf16[352,512]{1,0:T(8,128)(2,1)} collective-permute-done((bf16[352,512]{1,0:T(8,128)(2,1)}, bf16[352,512]{1,0:T(8,128)(2,1)}, u32[]{:S(2)}, u32[]{:S(2)}) %collective-permute-start.22) | collective-permute-done | bytes 360480 | tf_op jit(solution)/shard_map/ppermute | solution.py:99
  483.1 15.2 %collective-permute-done.26 = bf16[256,1408]{1,0:T(8,128)(2,1)} collective-permute-done((bf16[256,1408]{1,0:T(8,128)(2,1)}, bf16[256,1408]{1,0:T(8,128)(2,1)}, u32[]{:S(2)}, u32[]{:S(2)}) %collective-permute-start.26) | collective-permute-done | bytes 720928 | tf_op jit(solution)/shard_map/ppermute | solution.py:99
  526.0 15.2 %collective-permute-done.33 = bf16[128,2816]{1,0:T(8,128)(2,1)S(1)} collective-permute-done((bf16[128,2816]{1,0:T(8,128)(2,1)S(1)}, bf16[128,2816]{1,0:T(8,128)(2,1)S(1)}, u32[]{:S(2)}, u32[]{:S(2)}) %collective-permute-start.33) | collective-permute-done | bytes 720928 | tf_op jit(solution)/shard_map/ppermute | solution.py:99
  542.5 15.8 %collective-permute-done.34 = bf16[64,2816]{1,0:T(8,128)(2,1)S(1)} collective-permute-done((bf16[64,2816]{1,0:T(8,128)(2,1)S(1)}, bf16[64,2816]{1,0:T(8,128)(2,1)S(1)}, u32[]{:S(2)}, u32[]{:S(2)}) %collective-permute-start.34) | collective-permute-done | bytes 360480 | tf_op jit(solution)/shard_map/ppermute | solution.py:99
  564.7 12.7 %collective-permute-done.39 = bf16[88,1024]{1,0:T(8,128)(2,1)S(1)} collective-permute-done((bf16[88,1024]{1,0:T(8,128)(2,1)S(1)}, bf16[88,1024]{1,0:T(8,128)(2,1)S(1)}, u32[]{:S(2)}, u32[]{:S(2)}) %collective-permute-start.39) | collective-permute-done | bytes 180256 | tf_op jit(solution)/shard_map/ppermute | solution.py:99
  589.1 40.0 %collective-permute-done.41 = bf16[176,1024]{1,0:T(8,128)(2,1)S(1)} collective-permute-done((bf16[176,1024]{1,0:T(8,128)(2,1)S(1)}, bf16[176,1024]{1,0:T(8,128)(2,1)S(1)}, u32[]{:S(2)}, u32[]{:S(2)}) %collective-permute-start.41) | collective-permute-done | bytes 360480 | tf_op jit(solution)/shard_map/ppermute | solution.py:99
  632.8 13.7 %collective-permute-done.43 = bf16[352,512]{1,0:T(8,128)(2,1)S(1)} collective-permute-done((bf16[352,512]{1,0:T(8,128)(2,1)S(1)}, bf16[352,512]{1,0:T(8,128)(2,1)S(1)}, u32[]{:S(2)}, u32[]{:S(2)}) %collective-permute-start.43) | collective-permute-done | bytes 360480 | tf_op jit(solution)/shard_map/ppermute | solution.py:99
  646.9 26.3 %collective-permute-done.42 = bf16[200,1024]{1,0:T(8,128)(2,1)S(1)} collective-permute-done((bf16[200,1024]{1,0:T(8,128)(2,1)S(1)}, bf16[200,1024]{1,0:T(8,128)(2,1)S(1)}, u32[]{:S(2)}, u32[]{:S(2)}) %collective-permute-start.42) | collective-permute-done | bytes 409632 | tf_op jit(solution)/shard_map/ppermute | solution.py:99
  676.9 21.2 %collective-permute-done.45 = bf16[192,1024]{1,0:T(8,128)(2,1)S(1)} collective-permute-done((bf16[192,1024]{1,0:T(8,128)(2,1)S(1)}, bf16[192,1024]{1,0:T(8,128)(2,1)S(1)}, u32[]{:S(2)}, u32[]{:S(2)}) %collective-permute-start.45) | collective-permute-done | bytes 393248 | tf_op jit(solution)/shard_map/ppermute | solution.py:99
  699.3 19.1 %collective-permute-done.48 = bf16[384,1024]{1,0:T(8,128)(2,1)S(1)} collective-permute-done((bf16[384,1024]{1,0:T(8,128)(2,1)S(1)}, bf16[384,1024]{1,0:T(8,128)(2,1)S(1)}, u32[]{:S(2)}, u32[]{:S(2)}) %collective-permute-start.48) | collective-permute-done | bytes 786464 | tf_op jit(solution)/shard_map/ppermute | solution.py:99
  723.6 14.3 %collective-permute-done.51 = bf16[768,512]{1,0:T(8,128)(2,1)S(1)} collective-permute-done((bf16[768,512]{1,0:T(8,128)(2,1)S(1)}, bf16[768,512]{1,0:T(8,128)(2,1)S(1)}, u32[]{:S(2)}, u32[]{:S(2)}) %collective-permute-start.51) | collective-permute-done | bytes 786464 | tf_op jit(solution)/shard_map/ppermute | solution.py:99
  746.9 25.6 %collective-permute-done.54 = bf16[1536,512]{1,0:T(8,128)(2,1)S(1)} collective-permute-done((bf16[1536,512]{1,0:T(8,128)(2,1)S(1)}, bf16[1536,512]{1,0:T(8,128)(2,1)S(1)}, u32[]{:S(2)}, u32[]{:S(2)}) %collective-permute-start.54) | collective-permute-done | bytes 1572896 | tf_op jit(solution)/shard_map/ppermute | solution.py:99
  796.6 14.0 %shard_map.409 = (f32[32,1024]{1,0:T(8,128)}, f32[32,1024]{1,0:T(8,128)}, f32[32,1024]{1,0:T(8,128)}, f32[32,1024]{1,0:T(8,128)}, f32[32,1024]{1,0:T(8,128)}, /*...) custom-call(s32[2]{0:T(128)} %pad_add_fusion.refs_0_, ...), custom_call_target="tpu_custom_call" | custom-call | tf_op jit(solution)/shard_map/pallas_call | solution.py:361
  812.6 12.9 %shard_map.410 = (f32[32,1024]{1,0:T(8,128)}, f32[88,2816]{1,0:T(8,128)}, bf16[88,1024]{1,0:T(8,128)(2,1)}, f32[32,1024]{1,0:T(8,128)}, f32[88,2816]{1,0:T(8,128)}, /*index=5*/bf16[88,1024]{1,0:T(8,128)(2,1)}) custom-call(s32[2]{0:T(128)} %pad_add_fusion.refs_0_, bf16[1024,8192]{1,0:T(8,128)(2,1)} %all-gather.6.cloned.1.call-done.refs_1_, ...), custom_call_target="tpu_custom_call" | custom-call | tf_op jit(solution)/shard_map/pallas_call | solution.py:361
  837.7 11.4 %all-to-all-done.6 = bf16[32,2,32,88]{3,2,1,0:T(8,128)(2,1)S(1)} async-done(((bf16[32,2,32,88]{3,2,1,0:T(8,128)(2,1)}), bf16[32,2,32,88]{3,2,1,0:T(8,128)(2,1)S(1)}, u32[]{:S(2)}, u32[]{:S(2)}) %all-to-all-start.6) | async-done | bytes 360480 | tf_op jit(solution)/shard_map/all_to_all | solution.py:792
  (728 shorter events, 397.8 us)
Async XLA Ops:
  7.2 183.4 %all-gather.4.cloned.1.call-start = ((), (), s32[]{:S(2)}) async-start(), calls=%async_computation.7 | async-start | bytes 17842176 | tf_op jit(solution)/shard_map/all_gather | solution.py:412
  37.8 29.4 %collective-permute-start.6 = (bf16[128,1024]{1,0:T(8,128)(2,1)S(1)}, bf16[128,1024]{1,0:T(8,128)(2,1)S(1)}, u32[]{:S(2)}, u32[]{:S(2)}) collective-permute-start(bf16[128,1024]{1,0:T(8,128)(2,1)S(1)} %pad_maximum_fusion.11), channel_id=1, source_target_pairs={{0,4},{1,5},{2,6},{3,7},{4,0},{5,1},{6,2},{7,3},{8,12},{9,13},{10,... | collective-permute-start | bytes 786440 | tf_op jit(solution)/shard_map/ppermute | solution.py:99
  94.6 33.0 %collective-permute-start.8 = (bf16[1152,512]{1,0:T(8,128)(2,1)S(1)}, bf16[1152,512]{1,0:T(8,128)(2,1)S(1)}, u32[]{:S(2)}, u32[]{:S(2)}) collective-permute-start(bf16[1152,512]{1,0:T(8,128)(2,1)S(1)} %bitcast.817), channel_id=1, source_target_pairs={{0,8},{1,9},{2,10},{3,11},{4,12},{5,13},{6,14},{7,15},{8,0},{9,1},... | collective-permute-start | bytes 3538952 | tf_op jit(solution)/shard_map/ppermute | solution.py:99
  94.6 33.0 %collective-permute-start.9 = (bf16[1152,512]{1,0:T(8,128)(2,1)S(1)}, bf16[1152,512]{1,0:T(8,128)(2,1)S(1)}, u32[]{:S(2)}, u32[]{:S(2)}) collective-permute-start(bf16[1152,512]{1,0:T(8,128)(2,1)S(1)} %bitcast.814), channel_id=1, source_target_pairs={{0,8},{1,9},{2,10},{3,11},{4,12},{5,13},{6,14},{7,15},{8,0},{9,1},... | collective-permute-start | bytes 3538952 | tf_op jit(solution)/shard_map/ppermute | solution.py:99
  116.3 45.5 %collective-permute-start.13 = (bf16[1024,512]{1,0:T(8,128)(2,1)S(1)}, bf16[1024,512]{1,0:T(8,128)(2,1)}, u32[]{:S(2)}, u32[]{:S(2)}) collective-permute-start(bf16[1024,512]{1,0:T(8,128)(2,1)S(1)} %bitcast.823), channel_id=1, source_target_pairs={{0,1},{1,0},{2,3},{3,2},{4,5},{5,4},{6,7},{7,6},{8,9},{9,8},{10,11... | collective-permute-start | bytes 3145736 | tf_op jit(solution)/shard_map/ppermute | solution.py:99
  119.2 39.3 %collective-permute-start.11 = (bf16[1024,512]{1,0:T(8,128)(2,1)}, bf16[1024,512]{1,0:T(8,128)(2,1)}, u32[]{:S(2)}, u32[]{:S(2)}) collective-permute-start(bf16[1024,512]{1,0:T(8,128)(2,1)} %bitcast.70), channel_id=1, source_target_pairs={{0,16},{1,17},{2,18},{3,19},{4,20},{5,21},{6,22},{7,23},{8,24},{9,... | collective-permute-start | bytes 3145736 | tf_op jit(solution)/shard_map/ppermute | solution.py:99
  197.9 34.5 %all-to-all-start = ((bf16[8,3,2,64,128]{4,3,2,1,0:T(8,128)(2,1)}), bf16[8,3,2,64,128]{4,3,2,1,0:T(8,128)(2,1)}, u32[]{:S(2)}, u32[]{:S(2)}) async-start(bf16[8,3,2,64,128]{4,3,2,1,0:T(8,128)(2,1)} %copy.278), calls=%async_computation | async-start | bytes 1572864 | tf_op jit(solution)/shard_map/all_to_all | solution.py:474
  247.6 262.2 %all-gather.6.cloned.1.call-start = ((), (), s32[]{:S(2)}) async-start(), calls=%async_computation.8 | async-start | bytes 17301504 | tf_op jit(solution)/shard_map/all_gather | solution.py:577
  271.4 36.4 %all-to-all-start.2 = ((bf16[8,3,2,64,128]{4,3,2,1,0:T(8,128)(2,1)}), bf16[8,3,2,64,128]{4,3,2,1,0:T(8,128)(2,1)}, u32[]{:S(2)}, u32[]{:S(2)}) async-start(bf16[8,3,2,64,128]{4,3,2,1,0:T(8,128)(2,1)} %copy.290), calls=%async_computation.2 | async-start | bytes 1572864 | tf_op jit(solution)/shard_map/all_to_all | solution.py:474
  405.1 55.6 %all-to-all-start.5 = ((bf16[8,1,3,2,64,128]{5,4,3,2,1,0:T(8,128)(2,1)}), bf16[8,1,3,2,64,128]{5,4,3,2,1,0:T(8,128)(2,1)S(1)}, u32[]{:S(2)}, u32[]{:S(2)}) async-start(bf16[8,1,3,2,64,128]{5,4,3,2,1,0:T(8,128)(2,1)} %maximum_bitcast_fusion.2), calls=%async_computation.5 | async-start | bytes 1572864 | tf_op jit(solution)/shard_map/all_to_all | solution.py:484
  408.7 403.9 %all-gather.8.cloned.1.call-start = ((), (), s32[]{:S(2)}) async-start(), calls=%async_computation.9 | async-start | bytes 11894784 | tf_op jit(solution)/shard_map/all_gather | solution.py:701
  411.8 49.8 %collective-permute-start.23 = (bf16[512,1408]{1,0:T(8,128)(2,1)}, bf16[512,1408]{1,0:T(8,128)(2,1)}, u32[]{:S(2)}, u32[]{:S(2)}) collective-permute-start(bf16[512,1408]{1,0:T(8,128)(2,1)} %dynamic-slice_bitcast_fusion.1), channel_id=1, source_target_pairs={{0,16},{1,17},{2,18},{3,19},{4,20},{5,21},{6,22},{7,23},{8,24},{9,... | collective-permute-start | bytes 4325384 | tf_op jit(solution)/shard_map/ppermute | solution.py:99
  416.3 49.1 %collective-permute-start.24 = (bf16[512,1408]{1,0:T(8,128)(2,1)}, bf16[512,1408]{1,0:T(8,128)(2,1)}, u32[]{:S(2)}, u32[]{:S(2)}) collective-permute-start(bf16[512,1408]{1,0:T(8,128)(2,1)} %bitcast.188), channel_id=1, source_target_pairs={{0,1},{1,0},{2,3},{3,2},{4,5},{5,4},{6,7},{7,6},{8,9},{9,8},{10,11... | collective-permute-start | bytes 4325384 | tf_op jit(solution)/shard_map/ppermute | solution.py:99
  419.2 33.9 %collective-permute-start.22 = (bf16[352,512]{1,0:T(8,128)(2,1)}, bf16[352,512]{1,0:T(8,128)(2,1)}, u32[]{:S(2)}, u32[]{:S(2)}) collective-permute-start(bf16[352,512]{1,0:T(8,128)(2,1)} %dynamic-slice_bitcast_fusion.7), channel_id=1, source_target_pairs={{0,16},{1,17},{2,18},{3,19},{4,20},{5,21},{6,22},{7,23},{8,24},{9,... | collective-permute-start | bytes 1081352 | tf_op jit(solution)/shard_map/ppermute | solution.py:99
  421.1 38.8 %collective-permute-start.21 = (bf16[352,512]{1,0:T(8,128)(2,1)}, bf16[352,512]{1,0:T(8,128)(2,1)S(1)}, u32[]{:S(2)}, u32[]{:S(2)}) collective-permute-start(bf16[352,512]{1,0:T(8,128)(2,1)} %bitcast.179), channel_id=1, source_target_pairs={{0,1},{1,0},{2,3},{3,2},{4,5},{5,4},{6,7},{7,6},{8,9},{9,8},{10,11... | collective-permute-start | bytes 1081352 | tf_op jit(solution)/shard_map/ppermute | solution.py:99
  422.9 54.2 %collective-permute-start.27 = (bf16[512,1024]{1,0:T(8,128)(2,1)}, bf16[512,1024]{1,0:T(8,128)(2,1)}, u32[]{:S(2)}, u32[]{:S(2)}) collective-permute-start(bf16[512,1024]{1,0:T(8,128)(2,1)} %convolution_convert_fusion.5), channel_id=1, source_target_pairs={{0,8},{1,9},{2,10},{3,11},{4,12},{5,13},{6,14},{7,15},{8,0},{9,1},... | collective-permute-start | bytes 3145736 | tf_op jit(solution)/shard_map/ppermute | solution.py:99
  470.8 33.3 %collective-permute-start.28 = (bf16[512,3072]{1,0:T(8,128)(2,1)}, bf16[512,3072]{1,0:T(8,128)(2,1)}, u32[]{:S(2)}, u32[]{:S(2)}) collective-permute-start(bf16[512,3072]{1,0:T(8,128)(2,1)} %convolution_convert_fusion), channel_id=1, source_target_pairs={{0,8},{1,9},{2,10},{3,11},{4,12},{5,13},{6,14},{7,15},{8,0},{9,1},... | collective-permute-start | bytes 9437192 | tf_op jit(solution)/shard_map/ppermute | solution.py:99
  516.2 43.9 %collective-permute-start.32 = (bf16[1600,512]{1,0:T(8,128)(2,1)S(1)}, bf16[1600,512]{1,0:T(8,128)(2,1)S(1)}, u32[]{:S(2)}, u32[]{:S(2)}) collective-permute-start(bf16[1600,512]{1,0:T(8,128)(2,1)S(1)} %bitcast.865), channel_id=1, source_target_pairs={{0,1},{1,0},{2,3},{3,2},{4,5},{5,4},{6,7},{7,6},{8,9},{9,8},{10,11... | collective-permute-start | bytes 4915208 | tf_op jit(solution)/shard_map/ppermute | solution.py:99
  516.4 42.1 %collective-permute-start.31 = (bf16[1600,512]{1,0:T(8,128)(2,1)S(1)}, bf16[1600,512]{1,0:T(8,128)(2,1)S(1)}, u32[]{:S(2)}, u32[]{:S(2)}) collective-permute-start(bf16[1600,512]{1,0:T(8,128)(2,1)S(1)} %dynamic-slice_bitcast_fusion), channel_id=1, source_target_pairs={{0,16},{1,17},{2,18},{3,19},{4,20},{5,21},{6,22},{7,23},{8,24},{9,... | collective-permute-start | bytes 4915208 | tf_op jit(solution)/shard_map/ppermute | solution.py:99
  586.9 42.3 %collective-permute-start.40 = (bf16[400,1024]{1,0:T(8,128)(2,1)S(1)}, bf16[400,1024]{1,0:T(8,128)(2,1)S(1)}, u32[]{:S(2)}, u32[]{:S(2)}) collective-permute-start(bf16[400,1024]{1,0:T(8,128)(2,1)S(1)} %bitcast.910), channel_id=1, source_target_pairs={{0,2},{1,3},{2,0},{3,1},{4,6},{5,7},{6,4},{7,5},{8,10},{9,11},{10,... | collective-permute-start | bytes 2457608 | tf_op jit(solution)/shard_map/ppermute | solution.py:99
  587.0 42.2 %collective-permute-start.41 = (bf16[176,1024]{1,0:T(8,128)(2,1)S(1)}, bf16[176,1024]{1,0:T(8,128)(2,1)S(1)}, u32[]{:S(2)}, u32[]{:S(2)}) collective-permute-start(bf16[176,1024]{1,0:T(8,128)(2,1)S(1)} %bitcast.870), channel_id=1, source_target_pairs={{0,2},{1,3},{2,0},{3,1},{4,6},{5,7},{6,4},{7,5},{8,10},{9,11},{10,... | collective-permute-start | bytes 1081352 | tf_op jit(solution)/shard_map/ppermute | solution.py:99
  631.1 42.1 %collective-permute-start.42 = (bf16[200,1024]{1,0:T(8,128)(2,1)S(1)}, bf16[200,1024]{1,0:T(8,128)(2,1)S(1)}, u32[]{:S(2)}, u32[]{:S(2)}) collective-permute-start(bf16[200,1024]{1,0:T(8,128)(2,1)S(1)} %dynamic-slice_bitcast_fusion.5), channel_id=1, source_target_pairs={{0,4},{1,5},{2,6},{3,7},{4,0},{5,1},{6,2},{7,3},{8,12},{9,13},{10,... | collective-permute-start | bytes 1228808 | tf_op jit(solution)/shard_map/ppermute | solution.py:99
  738.0 34.4 %collective-permute-start.54 = (bf16[1536,512]{1,0:T(8,128)(2,1)S(1)}, bf16[1536,512]{1,0:T(8,128)(2,1)S(1)}, u32[]{:S(2)}, u32[]{:S(2)}) collective-permute-start(bf16[1536,512]{1,0:T(8,128)(2,1)S(1)} %bitcast.801), channel_id=1, source_target_pairs={{0,1},{1,0},{2,3},{3,2},{4,5},{5,4},{6,7},{7,6},{8,9},{9,8},{10,11... | collective-permute-start | bytes 4718600 | tf_op jit(solution)/shard_map/ppermute | solution.py:99
  740.5 34.1 %collective-permute-start.53 = (bf16[1536,512]{1,0:T(8,128)(2,1)S(1)}, bf16[1536,512]{1,0:T(8,128)(2,1)S(1)}, u32[]{:S(2)}, u32[]{:S(2)}) collective-permute-start(bf16[1536,512]{1,0:T(8,128)(2,1)S(1)} %bitcast.799), channel_id=1, source_target_pairs={{0,16},{1,17},{2,18},{3,19},{4,20},{5,21},{6,22},{7,23},{8,24},{9,... | collective-permute-start | bytes 4718600 | tf_op jit(solution)/shard_map/ppermute | solution.py:99
  (168 other events, 2069.4 us)
Sparse Core Ops, SparseCore 0:
  11.6 164.6 all-gather.3
  256.4 121.7 all-gather.5
  562.6 132.9 all-gather.7

commit v3 on v2

--- a/solution.py
+++ b/solution.py
@@ -254,35 +254,37 @@
         self.arrays, self.start, self.height, self.columns = arrays, start, height, columns
 
 
-def shampoo(links, matrices, roots):
+def shampoo(links, groups, roots):
     side = roots.shape[0]
+    befores = 1 << len(links.upper)
     big = [roots]
-    for source, *_ in matrices:
-        for array in source.arrays:
-            if not any(array is other for other in big):
-                big.append(array)
+    for sources, *_ in groups:
+        for source in sources:
+            for array in source.arrays:
+                if not any(array is other for other in big):
+                    big.append(array)
     place = {id(array): i for i, array in enumerate(big)}
     small, out_shape, scratch, copies = [], [], [], 0
-    for source, shard, left_stat, right_stat, root, weight, which in matrices:
-        rows, columns = left_stat.shape[1], right_stat.shape[1]
-        small += [shard, left_stat, right_stat, root] + ([] if weight is None else [weight])
+    for sources, shards, left_stats, right_stats, own_roots, weights, which in groups:
+        count, _, rows = left_stats.shape
+        columns = right_stats.shape[2]
+        small += [shards, left_stats, right_stats, own_roots]
+        small += [] if weights is None else [weights]
+        third = (count, right_stats.shape[1], rows) if weights is None else weights.shape
         out_shape += [
-            jax.ShapeDtypeStruct(left_stat.shape, F32),
-            jax.ShapeDtypeStruct(right_stat.shape, F32),
-            jax.ShapeDtypeStruct(
-                (right_stat.shape[0], rows) if weight is None else weight.shape,
-                BF16 if weight is None else F32,
-            ),
+            jax.ShapeDtypeStruct(left_stats.shape, F32),
+            jax.ShapeDtypeStruct(right_stats.shape, F32),
+            jax.ShapeDtypeStruct(third, BF16 if weights is None else F32),
         ]
-        if len(source.arrays) == 1:
-            scratch.append(pltpu.VMEM((1, rows, columns), BF16))
-            copies += 1
-        else:
-            blocks = 2 * source.arrays[0].shape[0]
-            scratch.append(pltpu.VMEM((blocks, rows // blocks, columns), BF16))
-            copies += 4 << len(links.upper)
-        scratch.append(pltpu.VMEM((side, side), BF16))
-        copies += 1
+        for source in sources:
+            if len(source.arrays) == 1:
+                scratch.append(pltpu.VMEM((1, rows, columns), BF16))
+                copies += 2
+            else:
+                blocks = 2 * source.arrays[0].shape[0]
+                scratch.append(pltpu.VMEM((blocks, rows // blocks, columns), BF16))
+                copies += 4 * befores + 1
+            scratch.append(pltpu.VMEM((side, side), BF16))
     bits = jnp.stack([links.index, links.own(links.core)]).astype(jnp.int32)
 
     def kernel(*refs):
@@ -293,69 +295,69 @@
         scratches, done = refs[: len(scratch)], refs[-1]
         index, own = place_ref[0], place_ref[1]
         started, used = [], 0
-        for i, (source, *_, which) in enumerate(matrices):
-            whole, root = scratches[2 * i], scratches[2 * i + 1]
-            mine = []
-            if len(source.arrays) == 1:
-                ref = bigs[place[id(source.arrays[0])]]
-                mine.append((ref.at[:, pl.ds(source.start, source.columns)], whole.at[0]))
-            else:
-                befores = 1 << len(links.upper)
-                deep = source.arrays[0].shape[0] // befores
-                half = source.arrays[0].shape[2]
-                for part in range(4):
-                    ref = bigs[place[id(source.arrays[part])]]
-                    core = own if part < 2 else 1 - own
-                    for before in range(befores):
-                        mine.append(
-                            (
-                                ref.at[
-                                    pl.ds(before * deep, deep), pl.ds(source.start, source.height)
-                                ],
-                                whole.at[
-                                    pl.ds((2 * before + core) * deep, deep),
-                                    :,
-                                    pl.ds((part % 2) * half, half),
-                                ],
-                            )
-                        )
-            mine.append((bigs[0].at[:, pl.ds(which * side, side)], root))
-            group = []
-            for from_ref, to_ref in mine:
-                copy = pltpu.make_async_copy(from_ref, to_ref, done.at[used])
-                copy.start()
-                group.append(copy)
-                used += 1
-            started.append(group)
-        for i, (source, shard, left_stat, right_stat, root, weight, which) in enumerate(matrices):
-            for copy in started[i]:
-                copy.wait()
-            rows, columns = left_stat.shape[1], right_stat.shape[1]
-            high, wide = left_stat.shape[0], right_stat.shape[0]
-            whole = scratches[2 * i][...].reshape(rows, columns)
+        for sources, *_, which in groups:
+            for source, block in zip(sources, which):
+                whole, root = scratches[2 * len(started)], scratches[2 * len(started) + 1]
+                mine = []
+                if len(source.arrays) == 1:
+                    ref = bigs[place[id(source.arrays[0])]]
+                    mine.append((ref.at[:, pl.ds(source.start, source.columns)], whole.at[0]))
+                else:
+                    deep = source.arrays[0].shape[0] // befores
+                    half = source.arrays[0].shape[2]
+                    for part in range(4):
+                        ref = bigs[place[id(source.arrays[part])]]
+                        core = own if part < 2 else 1 - own
+                        for before in range(befores):
+                            from_ref = ref.at[
+                                pl.ds(before * deep, deep), pl.ds(source.start, source.height)
+                            ]
+                            to_ref = whole.at[
+                                pl.ds((2 * before + core) * deep, deep),
+                                :,
+                                pl.ds((part % 2) * half, half),
+                            ]
+                            mine.append((from_ref, to_ref))
+                mine.append((bigs[0].at[:, pl.ds(block * side, side)], root))
+                group = []
+                for from_ref, to_ref in mine:
+                    copy = pltpu.make_async_copy(from_ref, to_ref, done.at[used])
+                    copy.start()
+                    group.append(copy)
+                    used += 1
+                started.append(group)
+        matrix = 0
+        for i, (sources, _, left_stats, right_stats, _, weights, _) in enumerate(groups):
+            rows, columns = left_stats.shape[2], right_stats.shape[2]
+            high, wide = left_stats.shape[1], right_stats.shape[1]
             shard_ref, left_ref, right_ref, root_ref = smalls[:4]
+            weight_ref = None if weights is None else smalls[4]
+            smalls = smalls[4 if weights is None else 5 :]
+            left_out, right_out, third_out = outs[3 * i : 3 * i + 3]
             lane = lax.broadcasted_iota(jnp.int32, (wide, columns), 1)
             row = lax.broadcasted_iota(jnp.int32, (wide, columns), 0)
             pick = (lane == row + index * wide).astype(F32)
-            stacked = [shard_ref[...], pick] + ([root_ref[...]] if weight is None else [])
-            first = against(jnp.concatenate(stacked, axis=0).astype(BF16), whole)
-            outs[3 * i][...] = 0.5 * left_ref[...] + (0.5 / columns) * first[:high]
-            picked = first[high : high + wide]
-            other = scratches[2 * i + 1][...]
-            if weight is None:
-                second = product(picked.astype(BF16), whole)
-                outs[3 * i + 1][...] = 0.5 * right_ref[...] + (0.5 / rows) * second
-                turned = first[high + wide :].astype(BF16)
-                outs[3 * i + 2][...] = product(turned, other).astype(BF16)
-                smalls = smalls[4:]
-            else:
-                second = product(
-                    jnp.concatenate([root_ref[...], picked], axis=0).astype(BF16), whole
-                )
-                outs[3 * i + 1][...] = 0.5 * right_ref[...] + (0.5 / rows) * second[high:]
-                step = product(second[:high].astype(BF16), other)
-                outs[3 * i + 2][...] = smalls[4][...] - step * (1.0 / math.sqrt(rows))
-                smalls = smalls[5:]
+            for j in range(len(sources)):
+                for copy in started[matrix]:
+                    copy.wait()
+                whole = scratches[2 * matrix][...].reshape(rows, columns)
+                other = scratches[2 * matrix + 1][...]
+                matrix += 1
+                stacked = [shard_ref[j], pick] + ([root_ref[j]] if weights is None else [])
+                first = against(jnp.concatenate(stacked, axis=0).astype(BF16), whole)
+                left_out[j] = 0.5 * left_ref[j] + (0.5 / columns) * first[:high]
+                picked = first[high : high + wide]
+                if weights is None:
+                    second = product(picked.astype(BF16), whole)
+                    right_out[j] = 0.5 * right_ref[j] + (0.5 / rows) * second
+                    turned = first[high + wide :].astype(BF16)
+                    third_out[j] = product(turned, other).astype(BF16)
+                else:
+                    stacked = jnp.concatenate([root_ref[j], picked], axis=0).astype(BF16)
+                    second = product(stacked, whole)
+                    right_out[j] = 0.5 * right_ref[j] + (0.5 / rows) * second[high:]
+                    step = product(second[:high].astype(BF16), other)
+                    third_out[j] = weight_ref[j] - step * (1.0 / math.sqrt(rows))
 
     vmem = pl.BlockSpec(memory_space=pltpu.VMEM)
     results = pl.pallas_call(
@@ -368,7 +370,7 @@
         scratch_shapes=scratch + [pltpu.SemaphoreType.DMA((copies,))],
         compiler_params=pltpu.CompilerParams(vmem_limit_bytes=56 << 20),
     )(bits, *big, *small)
-    return [results[3 * i : 3 * i + 3] for i in range(len(matrices))]
+    return [results[3 * i : 3 * i + 3] for i in range(len(groups))]
 
 
 def body(
@@ -407,14 +409,6 @@
     hidden_width = weight_gateup.shape[2]
     by_heads = HEADS % n_seq == 0
 
-    gateup_rows = weight_gateup.astype(BF16)
-    down_rows = weight_down.astype(BF16).reshape(-1, hidden_width)
-    feed_full = lax.all_gather(
-        jnp.concatenate([gateup_rows[0], gateup_rows[1], down_rows], axis=1),
-        AXES,
-        axis=0,
-        tiled=True,
-    )
     gain_share = norm_gains.shape[1]
     small = jnp.concatenate(
         [norm_gains.astype(BF16).reshape(-1), segment_ids.astype(BF16).reshape(-1)]
@@ -423,21 +417,32 @@
     attn_rows = weight_attn.astype(BF16)
     first = Gathering(links, [weight_adapt.astype(BF16), small])
     second = Gathering(links, [attn_rows[i] for i in range(4)])
+    third = Gathering(links, [weight_down.astype(BF16)])
+    gateup_rows = weight_gateup.astype(BF16)
+    gateup_rows = jnp.concatenate([gateup_rows[0], gateup_rows[1]], axis=1)
     inner_steps, cross_steps = range(len(links.inner)), range(links.steps)
     for step in inner_steps:
         first.inside(step)
-    tick([first, second])
+    (gateup_rows,) = tick([first, second], gateup_rows)
+    gateup_full = lax.all_gather(gateup_rows, AXES, axis=0, tiled=True)
     for step in inner_steps:
         second.inside(step)
     for step in cross_steps:
         first.cross(step)
-    tick([first, second])
+    tick([first, second, third])
     first.core()
     adapt_full, small = first.finish()
     for step in cross_steps:
         second.cross(step)
+    for step in inner_steps:
+        third.inside(step)
+    tick([second, third])
     second.core()
     query_full, key_full, value_full, out_full = second.finish()
+    for step in cross_steps:
+        third.cross(step)
+    third.core()
+    (down_full,) = third.finish()
 
     small = small.reshape(links.count, 8, width)[:, 0]
     gain_values = small[:, : 4 * gain_share].reshape(links.count, 4, gain_share)
@@ -487,7 +492,7 @@
 
     scaling = 1.0 / math.sqrt(HEAD_DIM)
 
-    def attention(queries, keys, values, with_feed):
+    def attention(queries, keys, values):
         if by_heads:
             queries, keys, values = to_heads(jnp.stack([queries, keys, values], axis=2))
         else:
@@ -496,8 +501,6 @@
                 lax.all_gather(item, "seq", axis=1, tiled=True).transpose(0, 2, 1, 3)
                 for item in (keys, values)
             )
-        if with_feed:
-            queries, feed[0], feed[1] = tie(queries, feed[0], feed[1])
         scores = jnp.einsum("shqd,shkd->shqk", queries, keys, preferred_element_type=F32)
         scores = jnp.where(allowed[:, None], scores * scaling, -1e30)
         exponent = jnp.exp(scores - jnp.max(scores, axis=-1, keepdims=True))
@@ -542,15 +545,19 @@
 
     embed_flat = embedding.reshape(tokens, width)
     embed_part = product(embed_flat, adapt_full[width:])
-    embed_part, feed_full = tie(embed_part, feed_full)
-    feed = [
-        feed_full[:, : 2 * hidden_width],
-        feed_full[:, 2 * hidden_width :].reshape(hidden_width, width),
-    ]
-
+    root_stack = jnp.concatenate(
+        [
+            right_root_adapt.astype(BF16)[:, None],
+            right_root_attn.astype(BF16).transpose(1, 0, 2),
+            right_root_down.astype(BF16)[:, None],
+            left_root_gateup.astype(BF16).transpose(1, 0, 2),
+        ],
+        axis=1,
+    )
+    root_stack = root_stack.reshape(root_stack.shape[0], 8 * width)
     roots = []
 
-    def forward(latent_low, with_roots=False):
+    def forward(latent_low):
         start_sum = product(latent_low, adapt_full[:width]) + embed_part
         scale_one = norm_scale(start_sum)
         normed_one = (start_sum * scale_one * gain_values[0]).astype(BF16)
@@ -561,26 +568,18 @@
         keys = product(normed_one, key_full).reshape(head_shape)
         keys = rotate(keys, turn_cos, turn_sin).astype(BF16)
         values = product(normed_one, value_full).astype(BF16).reshape(head_shape)
-        mixed_heads, attended = attention(queries, keys, values, with_roots)
-        if with_roots:
-            root_stack = jnp.concatenate(
-                [
-                    right_root_adapt.astype(BF16)[:, None],
-                    right_root_attn.astype(BF16).transpose(1, 0, 2),
-                    right_root_down.astype(BF16)[:, None],
-                    left_root_gateup.astype(BF16).transpose(1, 0, 2),
-                ],
-                axis=1,
-            )
-            share = root_stack.shape[0]
-            root_stack, mixed_heads = tie(root_stack.reshape(share, 8 * width), mixed_heads)
-            roots.append(lax.all_gather(root_stack, AXES, axis=0, tiled=True))
+        tied = len(roots) > 0
+        if not tied:
+            tied_stack, queries = tie(root_stack, queries)
+            roots.append(lax.all_gather(tied_stack, AXES, axis=0, tiled=True))
+        mixed_heads, attended = attention(queries, keys, values)
+        if tied:
+            roots[0], mixed_heads = tie(roots[0], mixed_heads)
         branch = product(mixed_heads, out_full)
         scale_two = norm_scale(branch)
         middle = start_sum + branch * scale_two * gain_values[1]
         scale_three = norm_scale(middle)
         normed_three = (middle * scale_three * gain_values[2]).astype(BF16)
-        gateup_full, down_full = feed
         both = product(normed_three, gateup_full)
         gate_value, upward = both[:, :hidden_width], both[:, hidden_width:]
         hidden = (jax.nn.silu(gate_value) * upward).astype(BF16)
@@ -607,7 +606,7 @@
         return (result, saved_values)
 
     latent_low = latent.reshape(tokens, width)
-    latent_state, unused_saved = forward(latent_low, True)
+    latent_state, unused_saved = forward(latent_low)
     latent_low = latent_state.astype(BF16)
     final_state, saved_values = forward(latent_low)
     (
@@ -633,7 +632,6 @@
     feed_grad = feed_grad.astype(BF16)
     down_sum = Reduction(links, width)
     down_sum.send(hidden, feed_grad)
-    gateup_full, down_full = feed
     hidden_grad = against(feed_grad, down_full)
     gate_grad = (hidden_grad * upward * silu_grad(gate_value)).astype(BF16)
     up_grad = (hidden_grad * jax.nn.silu(gate_value)).astype(BF16)
@@ -658,17 +656,16 @@
         mixed_grad = mixed_grad.transpose(0, 2, 1, 3)
     down_sum.cross(0)
     gateup_sum.add()
-    (mixed_grad,) = tick([down_sum, gateup_sum], mixed_grad)
+    gateup_sum.cross(0)
+    (mixed_grad,) = tick([down_sum], mixed_grad)
     grads = attention_back(mixed_grad, attended)
     for step in cross_steps[1:]:
         down_sum.cross(step)
-    gateup_sum.cross(0)
+        gateup_sum.cross(step)
     if by_heads:
         grads = to_tokens(grads)
     query_pre, key_pre, value_pre = grads.reshape(3, tokens, width)
-    query_pre, key_pre, value_pre = tick([down_sum, gateup_sum], query_pre, key_pre, value_pre)
-    for step in cross_steps[1:]:
-        gateup_sum.cross(step)
+    query_pre, key_pre, value_pre = tick([down_sum], query_pre, key_pre, value_pre)
     rest_sum.send(normed_one, jnp.concatenate([query_pre, key_pre, value_pre], axis=1))
     normed_one_grad = (
         against(query_pre, query_full) + against(key_pre, key_full) + against(value_pre, value_full)
@@ -683,20 +680,12 @@
     gain_sums = jnp.pad(gain_sums, ((0, 0), (0, 7), (0, width - 4 * gain_share)))
     rest_sum.send_rows(gain_sums.reshape(-1, width))
     rest_sum.add()
-    start_grad, root_rows = tick([gateup_sum, down_sum, rest_sum], start_grad, roots[0])
+    root_rows = roots[0]
+    (start_grad,) = tick([gateup_sum, down_sum, rest_sum], start_grad)
     rest_sum.cross(0)
     for step in inner_steps:
-        down_sum.inside(step)
-    for step in inner_steps:
         gateup_sum.inside(step)
-    tick([rest_sum, gateup_sum, down_sum])
-    reduced_down = down_sum.parts[0] * factor
-    first = Gathering(links, [reduced_down.astype(BF16)])
-    left_root_adapt, left_root_attn, left_root_down, right_root_gateup, reduced_down = tie(
-        left_root_adapt, left_root_attn, left_root_down, right_root_gateup, reduced_down
-    )
-    for step in cross_steps[1:]:
-        rest_sum.cross(step)
+    tick([rest_sum, gateup_sum])
     gate_shards = (gateup_sum.parts[0] * factor).reshape(2, -1, hidden_width)
     full_both = lax.all_gather(
         jnp.concatenate([gate_shards[0], gate_shards[1]], axis=1).astype(BF16),
@@ -704,15 +693,22 @@
         axis=0,
         tiled=True,
     )
+    for step in cross_steps[1:]:
+        rest_sum.cross(step)
+    for step in inner_steps:
+        down_sum.inside(step)
+    tick([rest_sum, down_sum])
+    reduced_down = down_sum.parts[0] * factor
+    first = Gathering(links, [reduced_down.astype(BF16)])
+    left_root_adapt, left_root_attn, left_root_down, right_root_gateup, reduced_down = tie(
+        left_root_adapt, left_root_attn, left_root_down, right_root_gateup, reduced_down
+    )
+    rest_sum.inside(0)
     first.inside(0)
-    tick([rest_sum, first])
-    rest_sum.inside(0)
-    for step in inner_steps[1:]:
-        first.inside(step)
     tick([rest_sum, first])
     for step in inner_steps[1:]:
         rest_sum.inside(step)
-    first.cross(0)
+        first.inside(step)
     tick([rest_sum, first])
     reduced_rest = rest_sum.parts[0] * factor
     row_share = width // links.count
@@ -724,23 +720,8 @@
         links, [attn_shards[i].astype(BF16) for i in range(4)] + [reduced_adapt.astype(BF16)]
     )
     third.inside(0)
-    for step in cross_steps[1:]:
-        first.cross(step)
-    tick([third, first])
-    for step in inner_steps[1:]:
-        third.inside(step)
-    first.core()
-    tick([third, first])
-    third.cross(0)
-    tick([third])
-    for step in cross_steps[1:]:
-        third.cross(step)
-    tick([third])
-    third.core()
-    tick([third])
-    grad_embedding = against(start_grad, adapt_full[width:]).reshape(
-        seq_count, group_len, width
-    )
+    first.cross(0)
+    (full_both,) = tick([third, first], full_both)
     def statistics(shard, whole, left_stat, right_stat, left_root):
         rows, columns = whole.shape
         new_left = 0.5 * left_stat + (0.5 / columns) * against(shard.astype(BF16), whole)
@@ -752,29 +733,33 @@
         both = product(jnp.concatenate([left_root.astype(BF16), own], axis=0), whole)
         return (new_left, 0.5 * right_stat + (0.5 / rows) * both[own_count:], both[:own_count])
 
-    def step(part, which, rows):
+    def whole_step(part, which, rows):
         root = root_rows[:, which * width : (which + 1) * width]
         return product(part.astype(BF16), root) * (1.0 / math.sqrt(rows))
 
+    for step in inner_steps[1:]:
+        third.inside(step)
+    for step in cross_steps[1:]:
+        first.cross(step)
     fits = row_share % 16 == 0
     if fits:
-        gateup_parts = shampoo(
+        sources = [Source([full_both], i * hidden_width, width, hidden_width) for i in range(2)]
+        ((new_left_gateup, new_right_gateup, step_columns),) = shampoo(
             links,
             [
                 (
-                    Source([full_both], i * hidden_width, width, hidden_width),
-                    gate_shards[i],
-                    left_gateup[i],
-                    right_gateup[i],
-                    right_root_gateup[i],
+                    sources,
+                    gate_shards,
+                    left_gateup,
+                    right_gateup,
+                    right_root_gateup,
                     None,
-                    6 + i,
+                    [6, 7],
                 )
-                for i in range(2)
             ],
             root_rows,
         )
-        step_columns = jnp.stack([member[2].T for member in gateup_parts])
+        step_columns = step_columns.transpose(0, 2, 1)
     else:
         whole_gates = [full_both[:, :hidden_width], full_both[:, hidden_width:]]
         gateup_parts = [
@@ -787,61 +772,75 @@
             root = root_rows[:, (6 + i) * width : (7 + i) * width]
             step_columns.append(product(root, turned).astype(BF16))
         step_columns = jnp.stack(step_columns)
+        new_left_gateup = jnp.stack([member[0] for member in gateup_parts])
+        new_right_gateup = jnp.stack([member[1] for member in gateup_parts])
     ff_share = step_columns.shape[2]
     step_columns = step_columns.reshape(2, links.count, row_share, ff_share).transpose(1, 0, 2, 3)
+    (step_columns,) = tick([third, first], step_columns)
+    first.core()
     step_rows = lax.all_to_all(step_columns, AXES, 0, 0, tiled=True)
     step_gateup = step_rows.transpose(1, 2, 0, 3).reshape(2, row_share, hidden_width)
     new_gateup = weight_gateup - step_gateup.astype(F32) * (1.0 / math.sqrt(width))
 
+    third.cross(0)
+    (new_gateup,) = tick([third, first], new_gateup)
+    for step in cross_steps[1:]:
+        third.cross(step)
     if fits:
-        ((new_left_down, new_right_down, new_down),) = shampoo(
-            links,
-            [
-                (
-                    first.sources()[0],
-                    reduced_down,
-                    left_down,
-                    right_down,
-                    left_root_down,
-                    weight_down,
-                    5,
-                )
-            ],
-            root_rows,
-        )
-        sources = third.sources()
-        attn_parts = [
-            (
-                sources[i],
-                attn_shards[i],
-                left_attn[i],
-                right_attn[i],
-                left_root_attn[i],
-                weight_attn[i],
-                1 + i,
-            )
-            for i in range(4)
-        ]
-        adapt_part = (
-            sources[4],
-            reduced_adapt,
-            left_adapt,
-            right_adapt,
-            left_root_adapt,
-            weight_adapt,
-            0,
-        )
-        *attn_parts, (new_left_adapt, new_right_adapt, new_adapt) = shampoo(
-            links, attn_parts + [adapt_part], root_rows
-        )
-        new_attn = jnp.stack([member[2] for member in attn_parts])
+        down_group = (
+            first.sources(),
+            reduced_down[None],
+            left_down[None],
+            right_down[None],
+            left_root_down[None],
+            weight_down[None],
+            [5],
+        )
+        ((new_left_down, new_right_down, new_down),) = shampoo(links, [down_group], root_rows)
+        new_left_down, new_right_down, new_down = new_left_down[0], new_right_down[0], new_down[0]
     else:
         (full_down,) = first.finish()
-        *attn_wholes, full_adapt = third.finish()
         new_left_down, new_right_down, down_part = statistics(
             reduced_down, full_down, left_down, right_down, left_root_down
         )
-        new_down = weight_down - step(down_part, 5, hidden_width)
+        new_down = weight_down - whole_step(down_part, 5, hidden_width)
+    (new_down,) = tick([third], new_down)
+    third.core()
+    tick([third])
+    grad_embedding = against(start_grad, adapt_full[width:]).reshape(
+        seq_count, group_len, width
+    )
+    if fits:
+        sources = third.sources()
+        attn_group = (
+            sources[:4],
+            attn_shards,
+            left_attn,
+            right_attn,
+            left_root_attn,
+            weight_attn,
+            [1, 2, 3, 4],
+        )
+        adapt_group = (
+            sources[4:],
+            reduced_adapt[None],
+            left_adapt[None],
+            right_adapt[None],
+            left_root_adapt[None],
+            weight_adapt[None],
+            [0],
+        )
+        (
+            (new_left_attn, new_right_attn, new_attn),
+            (new_left_adapt, new_right_adapt, new_adapt),
+        ) = shampoo(links, [attn_group, adapt_group], root_rows)
+        new_left_adapt, new_right_adapt, new_adapt = (
+            new_left_adapt[0],
+            new_right_adapt[0],
+            new_adapt[0],
+        )
+    else:
+        *attn_wholes, full_adapt = third.finish()
         attn_parts = [
             statistics(
                 attn_shards[i], attn_wholes[i], left_attn[i], right_attn[i], left_root_attn[i]
@@ -849,12 +848,14 @@
             for i in range(4)
         ]
         new_attn = weight_attn - jnp.stack(
-            [step(attn_parts[i][2], 1 + i, width) for i in range(4)]
-        )
+            [whole_step(attn_parts[i][2], 1 + i, width) for i in range(4)]
+        )
+        new_left_attn = jnp.stack([member[0] for member in attn_parts])
+        new_right_attn = jnp.stack([member[1] for member in attn_parts])
         new_left_adapt, new_right_adapt, adapt_part = statistics(
             reduced_adapt, full_adapt, left_adapt, right_adapt, left_root_adapt
         )
-        new_adapt = weight_adapt - step(adapt_part, 0, 2 * width)
+        new_adapt = weight_adapt - whole_step(adapt_part, 0, 2 * width)
     new_gain_moment = 0.5 * gain_moment + 0.5 * reduced_gains * reduced_gains
     new_norm_gains = norm_gains - 0.5 * reduced_gains / (jnp.sqrt(new_gain_moment) + 1e-08)
     latent_out = final_state.reshape(seq_count, group_len, width).astype(BF16)
@@ -868,10 +869,10 @@
         reduced_gains,
         new_left_adapt,
         new_right_adapt,
-        jnp.stack([member[0] for member in attn_parts]),
-        jnp.stack([member[1] for member in attn_parts]),
-        jnp.stack([member[0] for member in gateup_parts]),
-        jnp.stack([member[1] for member in gateup_parts]),
+        new_left_attn,
+        new_right_attn,
+        new_left_gateup,
+        new_right_gateup,
         new_left_down,
         new_right_down,
         new_adapt,

time: 870 us -> 814 us (0.936)
  waiting for transfers between devices: 429 us -> 317 us
  blocking collectives: 0 us -> 35.7 us
  local copies, waits for them, and re-layouts: 144 us -> 156 us
  matrix products: 81.1 us -> 90.4 us
    ppermute x57 -> x65, waiting for transfers between devices: 367 us -> 296 us  [swap(): return lax.ppermute(values, AXES, self.pairs[bit])]
    all_to_all x0 -> x1, blocking collectives: none -> 35.7 us  [to_heads(): came = lax.all_to_all(values, 'seq', 0, 0, tiled=True)]
    all_to_all x3 -> x2, waiting for transfers between devices: 36.6 us -> 1.97 us  [to_heads(): came = lax.all_to_all(values, 'seq', 0, 0, tiled=True)]
    slice x3 -> x0, local copies, waits for them, and re-layouts: 16.3 us -> none  [the longest x1 9.91 us: body(): feed_full[:, :2 * hidden_width]]
    dynamic_update_slice x24 -> x31, local copies, waits for them, and re-layouts: 7.65 us -> 23.4 us  [widen(): lax.dynamic_update_slice(both, came.reshape(mine.shape), (0, 1 - links.ow...]
    dynamic_update_slice x24 -> x29, local copies, waits for them, and re-layouts: 6.65 us -> 22.1 us  [widen(): both = lax.dynamic_update_slice(both, mine, (0, links.own(bit), 0, 0))]
    ppermute x57 -> x65, starting transfers between devices: 61.5 us -> 74.3 us  [swap(): return lax.ppermute(values, AXES, self.pairs[bit])]
    reshape x3 -> x1, local copies, waits for them, and re-layouts: 12.8 us -> 0.83 us  [body(): root_stack = root_stack.reshape(root_stack.shape[0], 8 * width)]
  transfers between devices with their start and end apart: 67 -> 74, of which waited for: 30 -> 36; matrix products, arithmetic and copies ran while one was open for 28% -> 31% of each run, Pallas kernels for 3% -> 3%
where the time goes in v3:
time: 814 us; the launch traced here: 802 us
  waiting for transfers between devices  317 us (39%)
  local copies, waits for them, and re-layouts  156 us (19%)
  starting transfers between devices  100 us (12%)
  matrix products  90.4 us (11%)
  other arithmetic  48.8 us (6%)
  Pallas kernels  36.4 us (4%)
  blocking collectives  35.7 us (4%)
  between operations  17.2 us (2%)
    ppermute x65, waiting for transfers between devices, swap(): return lax.ppermute(values, AXES, self.pairs[bit])  296 us
    ppermute x65, starting transfers between devices, swap(): return lax.ppermute(values, AXES, self.pairs[bit])  74.3 us
    pallas_call x3, Pallas kernels, shampoo(): pl.pallas_call(kernel, out_shape=out_shape, in_specs=[pl.BlockSpec(memory...  36.4 us
    all_to_all x1, blocking collectives, to_heads(): came = lax.all_to_all(values, 'seq', 0, 0, tiled=True)  35.7 us
    dot_general x12, matrix products, across(): lax.dot_general(left_side, right_side, (((0,), (0,)), ((), ())), preferre...  29.5 us
    dot_general x15, matrix products, product(): return jnp.dot(left_side, right_side, preferred_element_type=F32)  28.3 us
    dynamic_update_slice x31, local copies, waits for them, and re-layouts, widen(): lax.dynamic_update_slice(both, came.reshape(mine.shape), (0, 1 - links.ow...  23.4 us
    dynamic_update_slice x19, local copies, waits for them, and re-layouts, finish(): lax.dynamic_update_slice(whole, piece[i][:, None], (0, place, 0, 0, i % 2...  23.4 us
  transfers between devices with their start and end apart: 74, of which 36 were waited for; matrix products, arithmetic and copies ran while one was open for 31% of the time, Pallas kernels for 3%

profile of v3, /device:TPU:0, one launch (start us, length us, event | category | flops | bytes accessed | tf_op | source)
XLA Modules:
  0.0 801.7 jit_solution(12899319075812837426)
XLA Ops:
  21.9 7.3 collective-permute-done.1
  37.0 11.7 %collective-permute-done.6 = bf16[128,1024]{1,0:T(8,128)(2,1)S(1)} collective-permute-done((bf16[128,1024]{1,0:T(8,128)(2,1)S(1)}, bf16[128,1024]{1,0:T(8,128)(2,1)S(1)}, u32[]{:S(2)}, u32[]{:S(2)}) %collective-permute-start.6) | collective-permute-done | bytes 262176 | tf_op jit(solution)/shard_map/ppermute | solution.py:99
  55.5 15.1 %collective-permute-done.7 = bf16[256,1024]{1,0:T(8,128)(2,1)S(1)} collective-permute-done((bf16[256,1024]{1,0:T(8,128)(2,1)S(1)}, bf16[256,1024]{1,0:T(8,128)(2,1)S(1)}, u32[]{:S(2)}, u32[]{:S(2)}) %collective-permute-start.7) | collective-permute-done | bytes 524320 | tf_op jit(solution)/shard_map/ppermute | solution.py:99
  99.8 7.3 collective-permute-done.15
  116.9 16.6 %collective-permute-done.13 = bf16[1024,512]{1,0:T(8,128)(2,1)} collective-permute-done((bf16[1024,512]{1,0:T(8,128)(2,1)S(1)}, bf16[1024,512]{1,0:T(8,128)(2,1)}, u32[]{:S(2)}, u32[]{:S(2)}) %collective-permute-start.13) | collective-permute-done | bytes 1048608 | tf_op jit(solution)/shard_map/ppermute | solution.py:99
  174.9 8.3 %collective-permute-done.18 = bf16[352,512]{1,0:T(8,128)(2,1)S(1)} collective-permute-done((bf16[352,512]{1,0:T(8,128)(2,1)S(1)}, bf16[352,512]{1,0:T(8,128)(2,1)S(1)}, u32[]{:S(2)}, u32[]{:S(2)}) %collective-permute-start.18) | collective-permute-done | bytes 360480 | tf_op jit(solution)/shard_map/ppermute | solution.py:99
  206.1 25.6 %collective-permute-done.21 = bf16[704,512]{1,0:T(8,128)(2,1)S(1)} collective-permute-done((bf16[704,512]{1,0:T(8,128)(2,1)S(1)}, bf16[704,512]{1,0:T(8,128)(2,1)S(1)}, u32[]{:S(2)}, u32[]{:S(2)}) %collective-permute-start.21) | collective-permute-done | bytes 720928 | tf_op jit(solution)/shard_map/ppermute | solution.py:99
  282.3 35.7 %all_to_all.35 = bf16[8,3,2,64,128]{4,3,2,1,0:T(8,128)(2,1)S(1)} all-to-all(bf16[8,3,2,64,128]{4,3,2,1,0:T(8,128)(2,1)S(1)} %copy.292), channel_id=1, replica_groups=mesh['dp'=4,'seq'=8] {'seq'}, dimensions={0} | all-to-all | bytes 1572864 | tf_op jit(solution)/shard_map/all_to_all | solution.py:479
  331.0 8.9 %all-to-all-done.3 = bf16[8,1,1,2,64,128]{5,4,3,2,1,0:T(8,128)(2,1)S(1)} async-done(((bf16[8,1,1,2,64,128]{5,4,3,2,1,0:T(8,128)(2,1)}), bf16[8,1,1,2,64,128]{5,4,3,2,1,0:T(8,128)(2,1)S(1)}, u32[]{:S(2)}, u32[]{:S(2)}) %all-to-all-start.3) | async-done | bytes 262176 | tf_op jit(solution)/shard_map/all_to_all | solution.py:489
  447.0 12.1 %collective-permute-done.33 = bf16[352,512]{1,0:T(8,128)(2,1)S(1)} collective-permute-done((bf16[352,512]{1,0:T(8,128)(2,1)S(1)}, bf16[352,512]{1,0:T(8,128)(2,1)S(1)}, u32[]{:S(2)}, u32[]{:S(2)}) %collective-permute-start.33) | collective-permute-done | bytes 360480 | tf_op jit(solution)/shard_map/ppermute | solution.py:99
  482.7 7.7 collective-permute-done.29
  507.4 12.4 %collective-permute-done.41 = bf16[128,2816]{1,0:T(8,128)(2,1)S(1)} collective-permute-done((bf16[128,2816]{1,0:T(8,128)(2,1)S(1)}, bf16[128,2816]{1,0:T(8,128)(2,1)S(1)}, u32[]{:S(2)}, u32[]{:S(2)}) %collective-permute-start.41) | collective-permute-done | bytes 720928 | tf_op jit(solution)/shard_map/ppermute | solution.py:99
  520.1 15.4 %collective-permute-done.42 = bf16[64,2816]{1,0:T(8,128)(2,1)S(1)} collective-permute-done((bf16[64,2816]{1,0:T(8,128)(2,1)S(1)}, bf16[64,2816]{1,0:T(8,128)(2,1)S(1)}, u32[]{:S(2)}, u32[]{:S(2)}) %collective-permute-start.42) | collective-permute-done | bytes 360480 | tf_op jit(solution)/shard_map/ppermute | solution.py:99
  548.4 8.3 %collective-permute-done.45 = bf16[176,1024]{1,0:T(8,128)(2,1)S(1)} collective-permute-done((bf16[176,1024]{1,0:T(8,128)(2,1)S(1)}, bf16[176,1024]{1,0:T(8,128)(2,1)S(1)}, u32[]{:S(2)}, u32[]{:S(2)}) %collective-permute-start.45) | collective-permute-done | bytes 360480 | tf_op jit(solution)/shard_map/ppermute | solution.py:99
  557.0 12.6 %collective-permute-done.46 = bf16[88,1024]{1,0:T(8,128)(2,1)S(1)} collective-permute-done((bf16[88,1024]{1,0:T(8,128)(2,1)S(1)}, bf16[88,1024]{1,0:T(8,128)(2,1)S(1)}, u32[]{:S(2)}, u32[]{:S(2)}) %collective-permute-start.46) | collective-permute-done | bytes 180256 | tf_op jit(solution)/shard_map/ppermute | solution.py:99
  573.5 31.3 %collective-permute-done.48 = bf16[88,1024]{1,0:T(8,128)(2,1)S(1)} collective-permute-done((bf16[88,1024]{1,0:T(8,128)(2,1)S(1)}, bf16[88,1024]{1,0:T(8,128)(2,1)S(1)}, u32[]{:S(2)}, u32[]{:S(2)}) %collective-permute-start.48) | collective-permute-done | bytes 180256 | tf_op jit(solution)/shard_map/ppermute | solution.py:99
  604.9 6.5 collective-permute-done.47
  613.5 21.4 %collective-permute-done.50 = bf16[176,1024]{1,0:T(8,128)(2,1)S(1)} collective-permute-done((bf16[176,1024]{1,0:T(8,128)(2,1)S(1)}, bf16[176,1024]{1,0:T(8,128)(2,1)S(1)}, u32[]{:S(2)}, u32[]{:S(2)}) %collective-permute-start.50) | collective-permute-done | bytes 360480 | tf_op jit(solution)/shard_map/ppermute | solution.py:99
  635.0 17.3 %collective-permute-done.49 = bf16[200,1024]{1,0:T(8,128)(2,1)S(1)} collective-permute-done((bf16[200,1024]{1,0:T(8,128)(2,1)S(1)}, bf16[200,1024]{1,0:T(8,128)(2,1)S(1)}, u32[]{:S(2)}, u32[]{:S(2)}) %collective-permute-start.49) | collective-permute-done | bytes 409632 | tf_op jit(solution)/shard_map/ppermute | solution.py:99
  661.9 8.1 %collective-permute-done.51 = bf16[192,1024]{1,0:T(8,128)(2,1)S(1)} collective-permute-done((bf16[192,1024]{1,0:T(8,128)(2,1)S(1)}, bf16[192,1024]{1,0:T(8,128)(2,1)S(1)}, u32[]{:S(2)}, u32[]{:S(2)}) %collective-permute-start.51) | collective-permute-done | bytes 393248 | tf_op jit(solution)/shard_map/ppermute | solution.py:99
  675.3 13.4 %shard_map.409 = (f32[2,32,1024]{2,1,0:T(8,128)}, f32[2,88,2816]{2,1,0:T(8,128)}, bf16[2,88,1024]{2,1,0:T(8,128)(2,1)}) custom-call(s32[2]{0:T(128)} %pad_add_fusion.refs_0_, bf16[1024,8192]{1,0:T(8,128)(2,1)} %all-gather.6.cloned.1.call-done.refs_1_, bf16[1024,5632]{1,0:T(8,128)(2,1)} %all-gather.8.cloned.1.call-done.refs_2_, f32[2,32,2816]{2,1,0:T(8,128)} %bitcast.803, ...), custom_call_target="tpu_custom_call" | custom-call | tf_op jit(solution)/shard_map/pallas_call | solution.py:363
  735.1 9.2 %shard_map.410 = (f32[1,88,2816]{2,1,0:T(8,128)}, f32[1,32,1024]{2,1,0:T(8,128)}, f32[1,88,1024]{2,1,0:T(8,128)}) custom-call(s32[2]{0:T(128)} %pad_add_fusion.refs_0_, bf16[1024,8192]{1,0:T(8,128)(2,1)} %all-gather.6.cloned.1.call-done.refs_1_, bf16[2,704,512]{2,1,0:T(8,128)(2,1)} %bitcast.770, bf16[2,704,512]{2,1,0:T(8,128)(2,1)} %bitcast.768, ...), custom_call_target="tpu_custom_call" | custom-call | tf_op jit(solution)/shard_map/pallas_call | solution.py:363
  750.8 18.0 %collective-permute-done.62 = bf16[1536,512]{1,0:T(8,128)(2,1)S(1)} collective-permute-done((bf16[1536,512]{1,0:T(8,128)(2,1)}, bf16[1536,512]{1,0:T(8,128)(2,1)S(1)}, u32[]{:S(2)}, u32[]{:S(2)}) %collective-permute-start.62) | collective-permute-done | bytes 1572896 | tf_op jit(solution)/shard_map/ppermute | solution.py:99
  780.8 13.9 %shard_map.411 = (f32[4,32,1024]{2,1,0:T(8,128)}, f32[4,32,1024]{2,1,0:T(8,128)}, f32[4,32,1024]{2,1,0:T(8,128)}, f32[1,64,2048]{2,1,0:T(8,128)}, f32[1,32,1024]{2,1,0:T(8,128)}, /*index=5*/f32[1,64,1024]{2,1,0:T(8,128)}) custom-call(s32[2]{0:T(128)} %pad_add_fusion.refs_0_, bf16[1024,8192]{1,0:T(8,128)(2,1)} %all-gather.6.cloned.1.call-done.refs_1_, ...), custom_call_target="tpu_custom_call" | custom-call | tf_op jit(solution)/shard_map/pallas_call | solution.py:363
  (707 shorter events, 440.3 us)
Async XLA Ops:
  7.2 259.4 %all-gather.4.cloned.1.call-start = ((), (), s32[]{:S(2)}) async-start(), calls=%async_computation.7 | async-start | bytes 11894784 | tf_op jit(solution)/shard_map/all_gather | solution.py:427
  29.3 310.9 %all-gather.6.cloned.1.call-start = ((), (), s32[]{:S(2)}) async-start(), calls=%async_computation.8 | async-start | bytes 17301504 | tf_op jit(solution)/shard_map/all_gather | solution.py:574
  90.2 43.3 %collective-permute-start.13 = (bf16[1024,512]{1,0:T(8,128)(2,1)S(1)}, bf16[1024,512]{1,0:T(8,128)(2,1)}, u32[]{:S(2)}, u32[]{:S(2)}) collective-permute-start(bf16[1024,512]{1,0:T(8,128)(2,1)S(1)} %bitcast.782), channel_id=1, source_target_pairs={{0,1},{1,0},{2,3},{3,2},{4,5},{5,4},{6,7},{7,6},{8,9},{9,8},{10,11... | collective-permute-start | bytes 3145736 | tf_op jit(solution)/shard_map/ppermute | solution.py:99
  91.8 45.2 %collective-permute-start.11 = (bf16[1024,512]{1,0:T(8,128)(2,1)}, bf16[1024,512]{1,0:T(8,128)(2,1)}, u32[]{:S(2)}, u32[]{:S(2)}) collective-permute-start(bf16[1024,512]{1,0:T(8,128)(2,1)} %bitcast.70), channel_id=1, source_target_pairs={{0,16},{1,17},{2,18},{3,19},{4,20},{5,21},{6,22},{7,23},{8,24},{9,... | collective-permute-start | bytes 3145736 | tf_op jit(solution)/shard_map/ppermute | solution.py:99
  189.4 44.2 %all-to-all-start = ((bf16[8,3,2,64,128]{4,3,2,1,0:T(8,128)(2,1)}), bf16[8,3,2,64,128]{4,3,2,1,0:T(8,128)(2,1)}, u32[]{:S(2)}, u32[]{:S(2)}) async-start(bf16[8,3,2,64,128]{4,3,2,1,0:T(8,128)(2,1)} %copy.276), calls=%async_computation | async-start | bytes 1572864 | tf_op jit(solution)/shard_map/all_to_all | solution.py:479
  196.1 35.6 %collective-permute-start.21 = (bf16[704,512]{1,0:T(8,128)(2,1)S(1)}, bf16[704,512]{1,0:T(8,128)(2,1)S(1)}, u32[]{:S(2)}, u32[]{:S(2)}) collective-permute-start(bf16[704,512]{1,0:T(8,128)(2,1)S(1)} %bitcast.801), channel_id=1, source_target_pairs={{0,1},{1,0},{2,3},{3,2},{4,5},{5,4},{6,7},{7,6},{8,9},{9,8},{10,11... | collective-permute-start | bytes 2162696 | tf_op jit(solution)/shard_map/ppermute | solution.py:99
  203.9 53.3 %collective-permute-start.22 = (bf16[1408,512]{1,0:T(8,128)(2,1)}, bf16[1408,512]{1,0:T(8,128)(2,1)}, u32[]{:S(2)}, u32[]{:S(2)}) collective-permute-start(bf16[1408,512]{1,0:T(8,128)(2,1)} %bitcast.156), channel_id=1, source_target_pairs={{0,8},{1,9},{2,10},{3,11},{4,12},{5,13},{6,14},{7,15},{8,0},{9,1},... | collective-permute-start | bytes 4325384 | tf_op jit(solution)/shard_map/ppermute | solution.py:99
  232.6 27.2 %collective-permute-start.23 = (bf16[1408,512]{1,0:T(8,128)(2,1)}, bf16[1408,512]{1,0:T(8,128)(2,1)}, u32[]{:S(2)}, u32[]{:S(2)}) collective-permute-start(bf16[1408,512]{1,0:T(8,128)(2,1)} %bitcast.158), channel_id=1, source_target_pairs={{0,8},{1,9},{2,10},{3,11},{4,12},{5,13},{6,14},{7,15},{8,0},{9,1},... | collective-permute-start | bytes 4325384 | tf_op jit(solution)/shard_map/ppermute | solution.py:99
  376.7 25.1 %collective-permute-start.25 = (bf16[512,2816]{1,0:T(8,128)(2,1)}, bf16[512,2816]{1,0:T(8,128)(2,1)}, u32[]{:S(2)}, u32[]{:S(2)}) collective-permute-start(bf16[512,2816]{1,0:T(8,128)(2,1)} %convolution_convert_fusion.1), channel_id=1, source_target_pairs={{0,8},{1,9},{2,10},{3,11},{4,12},{5,13},{6,14},{7,15},{8,0},{9,1},... | collective-permute-start | bytes 8650760 | tf_op jit(solution)/shard_map/ppermute | solution.py:99
  408.9 51.0 %collective-permute-start.28 = (bf16[512,1408]{1,0:T(8,128)(2,1)}, bf16[512,1408]{1,0:T(8,128)(2,1)}, u32[]{:S(2)}, u32[]{:S(2)}) collective-permute-start(bf16[512,1408]{1,0:T(8,128)(2,1)} %bitcast.196), channel_id=1, source_target_pairs={{0,1},{1,0},{2,3},{3,2},{4,5},{5,4},{6,7},{7,6},{8,9},{9,8},{10,11... | collective-permute-start | bytes 4325384 | tf_op jit(solution)/shard_map/ppermute | solution.py:99
  430.3 33.6 %all-to-all-start.5 = ((bf16[8,1,3,2,64,128]{5,4,3,2,1,0:T(8,128)(2,1)}), bf16[8,1,3,2,64,128]{5,4,3,2,1,0:T(8,128)(2,1)}, u32[]{:S(2)}, u32[]{:S(2)}) async-start(bf16[8,1,3,2,64,128]{5,4,3,2,1,0:T(8,128)(2,1)} %maximum_bitcast_fusion.2), calls=%async_computation.5 | async-start | bytes 1572864 | tf_op jit(solution)/shard_map/all_to_all | solution.py:489
  434.6 236.2 %all-gather.8.cloned.1.call-start = ((), (), s32[]{:S(2)}) async-start(), calls=%async_computation.9 | async-start | bytes 11894784 | tf_op jit(solution)/shard_map/all_gather | solution.py:690
  441.4 35.7 %collective-permute-start.26 = (bf16[512,1408]{1,0:T(8,128)(2,1)}, bf16[512,1408]{1,0:T(8,128)(2,1)}, u32[]{:S(2)}, u32[]{:S(2)}) collective-permute-start(bf16[512,1408]{1,0:T(8,128)(2,1)} %dynamic-slice_bitcast_fusion.1), channel_id=1, source_target_pairs={{0,16},{1,17},{2,18},{3,19},{4,20},{5,21},{6,22},{7,23},{8,24},{9,... | collective-permute-start | bytes 4325384 | tf_op jit(solution)/shard_map/ppermute | solution.py:99
  462.5 27.9 %collective-permute-start.29 = (bf16[256,1408]{1,0:T(8,128)(2,1)}, bf16[256,1408]{1,0:T(8,128)(2,1)}, u32[]{:S(2)}, u32[]{:S(2)}) collective-permute-start(bf16[256,1408]{1,0:T(8,128)(2,1)} %dynamic-slice_bitcast_fusion.4), channel_id=1, source_target_pairs={{0,16},{1,17},{2,18},{3,19},{4,20},{5,21},{6,22},{7,23},{8,24},{9,... | collective-permute-start | bytes 2162696 | tf_op jit(solution)/shard_map/ppermute | solution.py:99
  470.4 29.4 %collective-permute-start.36 = (bf16[512,3072]{1,0:T(8,128)(2,1)}, bf16[512,3072]{1,0:T(8,128)(2,1)}, u32[]{:S(2)}, u32[]{:S(2)}) collective-permute-start(bf16[512,3072]{1,0:T(8,128)(2,1)} %convolution_convert_fusion), channel_id=1, source_target_pairs={{0,8},{1,9},{2,10},{3,11},{4,12},{5,13},{6,14},{7,15},{8,0},{9,1},... | collective-permute-start | bytes 9437192 | tf_op jit(solution)/shard_map/ppermute | solution.py:99
  505.4 35.7 %collective-permute-start.40 = (bf16[1600,512]{1,0:T(8,128)(2,1)S(1)}, bf16[1600,512]{1,0:T(8,128)(2,1)S(1)}, u32[]{:S(2)}, u32[]{:S(2)}) collective-permute-start(bf16[1600,512]{1,0:T(8,128)(2,1)S(1)} %bitcast.821), channel_id=1, source_target_pairs={{0,1},{1,0},{2,3},{3,2},{4,5},{5,4},{6,7},{7,6},{8,9},{9,8},{10,11... | collective-permute-start | bytes 4915208 | tf_op jit(solution)/shard_map/ppermute | solution.py:99
  506.0 34.6 %collective-permute-start.39 = (bf16[1600,512]{1,0:T(8,128)(2,1)S(1)}, bf16[1600,512]{1,0:T(8,128)(2,1)S(1)}, u32[]{:S(2)}, u32[]{:S(2)}) collective-permute-start(bf16[1600,512]{1,0:T(8,128)(2,1)S(1)} %dynamic-slice_bitcast_fusion), channel_id=1, source_target_pairs={{0,16},{1,17},{2,18},{3,19},{4,20},{5,21},{6,22},{7,23},{8,24},{9,... | collective-permute-start | bytes 4915208 | tf_op jit(solution)/shard_map/ppermute | solution.py:99
  570.6 40.8 %collective-permute-start.47 = (bf16[400,1024]{1,0:T(8,128)(2,1)S(1)}, bf16[400,1024]{1,0:T(8,128)(2,1)S(1)}, u32[]{:S(2)}, u32[]{:S(2)}) collective-permute-start(bf16[400,1024]{1,0:T(8,128)(2,1)S(1)} %bitcast.866), channel_id=1, source_target_pairs={{0,2},{1,3},{2,0},{3,1},{4,6},{5,7},{6,4},{7,5},{8,10},{9,11},{10,... | collective-permute-start | bytes 2457608 | tf_op jit(solution)/shard_map/ppermute | solution.py:99
  571.1 33.8 %collective-permute-start.48 = (bf16[88,1024]{1,0:T(8,128)(2,1)S(1)}, bf16[88,1024]{1,0:T(8,128)(2,1)S(1)}, u32[]{:S(2)}, u32[]{:S(2)}) collective-permute-start(bf16[88,1024]{1,0:T(8,128)(2,1)S(1)} %get-tuple-element.200), channel_id=1, source_target_pairs={{0,4},{1,5},{2,6},{3,7},{4,0},{5,1},{6,2},{7,3},{8,12},{9,13},{10,... | collective-permute-start | bytes 540680 | tf_op jit(solution)/shard_map/ppermute | solution.py:99
  611.9 40.4 %collective-permute-start.49 = (bf16[200,1024]{1,0:T(8,128)(2,1)S(1)}, bf16[200,1024]{1,0:T(8,128)(2,1)S(1)}, u32[]{:S(2)}, u32[]{:S(2)}) collective-permute-start(bf16[200,1024]{1,0:T(8,128)(2,1)S(1)} %dynamic-slice_bitcast_fusion.5), channel_id=1, source_target_pairs={{0,4},{1,5},{2,6},{3,7},{4,0},{5,1},{6,2},{7,3},{8,12},{9,13},{10,... | collective-permute-start | bytes 1228808 | tf_op jit(solution)/shard_map/ppermute | solution.py:99
  702.8 29.7 %collective-permute-start.59 = (bf16[1408,512]{1,0:T(8,128)(2,1)}, bf16[1408,512]{1,0:T(8,128)(2,1)}, u32[]{:S(2)}, u32[]{:S(2)}) collective-permute-start(bf16[1408,512]{1,0:T(8,128)(2,1)} %bitcast.769), channel_id=1, source_target_pairs={{0,8},{1,9},{2,10},{3,11},{4,12},{5,13},{6,14},{7,15},{8,0},{9,1},... | collective-permute-start | bytes 4325384 | tf_op jit(solution)/shard_map/ppermute | solution.py:99
  703.0 29.4 %collective-permute-start.60 = (bf16[1408,512]{1,0:T(8,128)(2,1)S(1)}, bf16[1408,512]{1,0:T(8,128)(2,1)}, u32[]{:S(2)}, u32[]{:S(2)}) collective-permute-start(bf16[1408,512]{1,0:T(8,128)(2,1)S(1)} %bitcast.767), channel_id=1, source_target_pairs={{0,8},{1,9},{2,10},{3,11},{4,12},{5,13},{6,14},{7,15},{8,0},{9,1},... | collective-permute-start | bytes 4325384 | tf_op jit(solution)/shard_map/ppermute | solution.py:99
  732.4 36.4 %collective-permute-start.62 = (bf16[1536,512]{1,0:T(8,128)(2,1)}, bf16[1536,512]{1,0:T(8,128)(2,1)S(1)}, u32[]{:S(2)}, u32[]{:S(2)}) collective-permute-start(bf16[1536,512]{1,0:T(8,128)(2,1)} %bitcast.304), channel_id=1, source_target_pairs={{0,1},{1,0},{2,3},{3,2},{4,5},{5,4},{6,7},{7,6},{8,9},{9,8},{10,11... | collective-permute-start | bytes 4718600 | tf_op jit(solution)/shard_map/ppermute | solution.py:99
  733.6 36.5 %collective-permute-start.61 = (bf16[1536,512]{1,0:T(8,128)(2,1)}, bf16[1536,512]{1,0:T(8,128)(2,1)S(1)}, u32[]{:S(2)}, u32[]{:S(2)}) collective-permute-start(bf16[1536,512]{1,0:T(8,128)(2,1)} %bitcast.301), channel_id=1, source_target_pairs={{0,16},{1,17},{2,18},{3,19},{4,20},{5,21},{6,22},{7,23},{8,24},{9,... | collective-permute-start | bytes 4718600 | tf_op jit(solution)/shard_map/ppermute | solution.py:99
  (154 other events, 1743.4 us)
Sparse Core Ops, SparseCore 0:
  29.4 121.7 all-gather.3
  168.8 150.1 all-gather.5
  543.7 120.6 all-gather.7

commit v4 on v3

--- a/solution.py
+++ b/solution.py
@@ -173,7 +173,7 @@
 class Reduction:
     def __init__(self, links, wide):
         self.links, self.wide = links, wide
-        self.terms, self.came = [], []
+        self.terms = []
 
     def sides(self, left_side, which):
         blocks = 2 << len(self.links.upper)
@@ -185,12 +185,16 @@
             chosen.append(jnp.where(which == 0, first, second))
         return jnp.concatenate(chosen, axis=1)
 
-    def send(self, left_side, right_side):
+    def early(self, left_side):
         links = self.links
-        away = across(self.sides(left_side, 1 - links.own(links.core)), right_side)
+        away = self.sides(left_side, 1 - links.own(links.core))
         kept = self.sides(left_side, links.own(links.core))
-        self.terms.append(lambda: across(kept, right_side))
-        self.came.append(links.swap(away.astype(BF16), links.core))
+        return (kept, links.swap(away, links.core))
+
+    def send(self, left_pair, right_side):
+        other = self.links.swap(right_side, self.links.core)
+        left_both = jnp.concatenate(left_pair, axis=0)
+        self.terms.append(lambda: across(left_both, jnp.concatenate([right_side, other], axis=0)))
 
     def send_rows(self, values):
         links = self.links
@@ -198,15 +202,15 @@
         own = links.own(links.core)
         away = lax.dynamic_index_in_dim(halves, 1 - own, 1, False).reshape(-1, values.shape[1])
         kept = lax.dynamic_index_in_dim(halves, own, 1, False).reshape(-1, values.shape[1])
-        self.terms.append(lambda: kept)
-        self.came.append(links.swap(away.astype(BF16), links.core))
+        came = links.swap(away.astype(BF16), links.core)
+        self.terms.append(lambda: kept + came.astype(F32))
 
     def add(self):
         links = self.links
         owners = links.count // 2
         total = []
-        for term, came in zip(self.terms, self.came):
-            item = (term() + came.astype(F32)).astype(BF16)
+        for term in self.terms:
+            item = term().astype(BF16)
             item = item.reshape(owners, -1, item.shape[1])
             for start in range(0, item.shape[2], self.wide):
                 total.append(item[:, :, start : start + self.wide])
@@ -631,13 +635,18 @@
     feed_grad, gain_four = norm_back(feed_out, scale_four, gain_values[3], incoming)
     feed_grad = feed_grad.astype(BF16)
     down_sum = Reduction(links, width)
-    down_sum.send(hidden, feed_grad)
+    hidden_pair = down_sum.early(hidden)
+    normed_three_pair = down_sum.early(normed_three)
+    mixed_pair = down_sum.early(mixed_heads)
+    normed_one_pair = down_sum.early(normed_one)
+    joined_pair = down_sum.early(jnp.concatenate([latent_low, embed_flat], axis=1))
+    down_sum.send(hidden_pair, feed_grad)
     hidden_grad = against(feed_grad, down_full)
     gate_grad = (hidden_grad * upward * silu_grad(gate_value)).astype(BF16)
     up_grad = (hidden_grad * jax.nn.silu(gate_value)).astype(BF16)
     gateup_sum = Reduction(links, hidden_width)
-    gateup_sum.send(normed_three, gate_grad)
-    gateup_sum.send(normed_three, up_grad)
+    gateup_sum.send(normed_three_pair, gate_grad)
+    gateup_sum.send(normed_three_pair, up_grad)
     both_grad = jnp.concatenate([gate_grad, up_grad], axis=1)
     normed_three_grad = against(both_grad, gateup_full)
     middle_grad, gain_three = norm_back(middle, scale_three, gain_values[2], normed_three_grad)
@@ -646,7 +655,7 @@
     branch_grad = branch_grad.astype(BF16)
     mixed_grad = against(branch_grad, out_full).astype(BF16)
     rest_sum = Reduction(links, width)
-    rest_sum.send(mixed_heads, branch_grad)
+    rest_sum.send(mixed_pair, branch_grad)
     down_sum.add()
     (mixed_grad,) = tick([down_sum], mixed_grad)
     mixed_grad = mixed_grad.reshape(seq_count, group_len, HEADS, HEAD_DIM)
@@ -666,14 +675,13 @@
         grads = to_tokens(grads)
     query_pre, key_pre, value_pre = grads.reshape(3, tokens, width)
     query_pre, key_pre, value_pre = tick([down_sum], query_pre, key_pre, value_pre)
-    rest_sum.send(normed_one, jnp.concatenate([query_pre, key_pre, value_pre], axis=1))
+    rest_sum.send(normed_one_pair, jnp.concatenate([query_pre, key_pre, value_pre], axis=1))
     normed_one_grad = (
         against(query_pre, query_full) + against(key_pre, key_full) + against(value_pre, value_full)
     )
     start_grad, gain_one = norm_back(start_sum, scale_one, gain_values[0], normed_one_grad)
     start_grad = (start_grad + middle_grad).astype(BF16)
-    joined = jnp.concatenate([latent_low, embed_flat], axis=1)
-    rest_sum.send(joined, start_grad)
+    rest_sum.send(joined_pair, start_grad)
     gain_sums = jnp.stack([gain_one, gain_two, gain_three, gain_four])
     gain_sums = gain_sums.reshape(4, links.count, gain_share).transpose(1, 0, 2)
     gain_sums = gain_sums.reshape(links.count, 1, 4 * gain_share)
@@ -681,7 +689,7 @@
     rest_sum.send_rows(gain_sums.reshape(-1, width))
     rest_sum.add()
     root_rows = roots[0]
-    (start_grad,) = tick([gateup_sum, down_sum, rest_sum], start_grad)
+    (start_grad,) = tick([down_sum, rest_sum], start_grad)
     rest_sum.cross(0)
     for step in inner_steps:
         gateup_sum.inside(step)

time: 814 us -> 802 us (0.985)
  blocking collectives: 35.7 us -> 0 us
  starting transfers between devices: 100 us -> 118 us
  waiting for transfers between devices: 317 us -> 334 us
  matrix products: 90.4 us -> 74.5 us
    all_to_all x1 -> x0, blocking collectives: 35.7 us -> none  [to_heads(): came = lax.all_to_all(values, 'seq', 0, 0, tiled=True)]
    all_to_all x2 -> x3, waiting for transfers between devices: 1.97 us -> 31.9 us  [to_heads(): came = lax.all_to_all(values, 'seq', 0, 0, tiled=True)]
    dot_general x12 -> x6, matrix products: 29.5 us -> 10.8 us  [across(): lax.dot_general(left_side, right_side, (((0,), (0,)), ((), ())), preferre...]
    ppermute x65 -> x70, starting transfers between devices: 74.3 us -> 87 us  [swap(): return lax.ppermute(values, AXES, self.pairs[bit])]
    ppermute x65 -> x70, waiting for transfers between devices: 296 us -> 286 us  [swap(): return lax.ppermute(values, AXES, self.pairs[bit])]
  transfers between devices with their start and end apart: 74 -> 80, of which waited for: 36 -> 38; matrix products, arithmetic and copies ran while one was open for 31% -> 34% of each run, Pallas kernels for 3% -> 3%
where the time goes in v4:
time: 802 us; the launch traced here: 789 us
  waiting for transfers between devices  334 us (42%)
  local copies, waits for them, and re-layouts  155 us (19%)
  starting transfers between devices  118 us (15%)
  matrix products  74.5 us (9%)
  other arithmetic  55.3 us (7%)
  Pallas kernels  36.4 us (5%)
  between operations  16.7 us (2%)
    ppermute x70, waiting for transfers between devices, swap(): return lax.ppermute(values, AXES, self.pairs[bit])  286 us
    ppermute x70, starting transfers between devices, swap(): return lax.ppermute(values, AXES, self.pairs[bit])  87 us
    pallas_call x3, Pallas kernels, shampoo(): pl.pallas_call(kernel, out_shape=out_shape, in_specs=[pl.BlockSpec(memory...  36.4 us
    all_to_all x3, waiting for transfers between devices, to_heads(): came = lax.all_to_all(values, 'seq', 0, 0, tiled=True)  31.9 us
    dot_general x15, matrix products, product(): return jnp.dot(left_side, right_side, preferred_element_type=F32)  28.3 us
    dynamic_update_slice x19, local copies, waits for them, and re-layouts, finish(): lax.dynamic_update_slice(whole, piece[i][:, None], (0, place, 0, 0, i % 2...  23.5 us
    dynamic_update_slice x31, local copies, waits for them, and re-layouts, widen(): lax.dynamic_update_slice(both, came.reshape(mine.shape), (0, 1 - links.ow...  23.4 us
    dynamic_update_slice x29, local copies, waits for them, and re-layouts, widen(): both = lax.dynamic_update_slice(both, mine, (0, links.own(bit), 0, 0))  21.9 us
  transfers between devices with their start and end apart: 80, of which 38 were waited for; matrix products, arithmetic and copies ran while one was open for 34% of the time, Pallas kernels for 3%

profile of v4, /device:TPU:0, one launch (start us, length us, event | category | flops | bytes accessed | tf_op | source)
XLA Modules:
  0.0 789.0 jit_solution(1361782168709475004)
XLA Ops:
  21.9 7.3 collective-permute-done.1
  37.0 11.7 %collective-permute-done.6 = bf16[128,1024]{1,0:T(8,128)(2,1)S(1)} collective-permute-done((bf16[128,1024]{1,0:T(8,128)(2,1)S(1)}, bf16[128,1024]{1,0:T(8,128)(2,1)S(1)}, u32[]{:S(2)}, u32[]{:S(2)}) %collective-permute-start.6) | collective-permute-done | bytes 262176 | tf_op jit(solution)/shard_map/ppermute | solution.py:99
  55.5 15.1 %collective-permute-done.7 = bf16[256,1024]{1,0:T(8,128)(2,1)S(1)} collective-permute-done((bf16[256,1024]{1,0:T(8,128)(2,1)S(1)}, bf16[256,1024]{1,0:T(8,128)(2,1)S(1)}, u32[]{:S(2)}, u32[]{:S(2)}) %collective-permute-start.7) | collective-permute-done | bytes 524320 | tf_op jit(solution)/shard_map/ppermute | solution.py:99
  99.6 7.6 collective-permute-done.15
  116.9 16.6 %collective-permute-done.13 = bf16[1024,512]{1,0:T(8,128)(2,1)} collective-permute-done((bf16[1024,512]{1,0:T(8,128)(2,1)S(1)}, bf16[1024,512]{1,0:T(8,128)(2,1)}, u32[]{:S(2)}, u32[]{:S(2)}) %collective-permute-start.13) | collective-permute-done | bytes 1048608 | tf_op jit(solution)/shard_map/ppermute | solution.py:99
  174.7 8.6 %collective-permute-done.18 = bf16[352,512]{1,0:T(8,128)(2,1)S(1)} collective-permute-done((bf16[352,512]{1,0:T(8,128)(2,1)S(1)}, bf16[352,512]{1,0:T(8,128)(2,1)S(1)}, u32[]{:S(2)}, u32[]{:S(2)}) %collective-permute-start.18) | collective-permute-done | bytes 360480 | tf_op jit(solution)/shard_map/ppermute | solution.py:99
  206.2 25.8 %collective-permute-done.21 = bf16[704,512]{1,0:T(8,128)(2,1)S(1)} collective-permute-done((bf16[704,512]{1,0:T(8,128)(2,1)S(1)}, bf16[704,512]{1,0:T(8,128)(2,1)S(1)}, u32[]{:S(2)}, u32[]{:S(2)}) %collective-permute-start.21) | collective-permute-done | bytes 720928 | tf_op jit(solution)/shard_map/ppermute | solution.py:99
  266.3 6.1 fusion.107
  288.4 29.4 %all-to-all-done.2 = bf16[8,3,2,64,128]{4,3,2,1,0:T(8,128)(2,1)} async-done(((bf16[8,3,2,64,128]{4,3,2,1,0:T(8,128)(2,1)}), bf16[8,3,2,64,128]{4,3,2,1,0:T(8,128)(2,1)}, u32[]{:S(2)}, u32[]{:S(2)}) %all-to-all-start.2) | async-done | bytes 786464 | tf_op jit(solution)/shard_map/all_to_all | solution.py:483
  335.5 6.0 all-to-all-done.3
  434.2 11.0 %collective-permute-done.29 = bf16[352,512]{1,0:T(8,128)(2,1)} collective-permute-done((bf16[352,512]{1,0:T(8,128)(2,1)}, bf16[352,512]{1,0:T(8,128)(2,1)}, u32[]{:S(2)}, u32[]{:S(2)}) %collective-permute-start.29) | collective-permute-done | bytes 360480 | tf_op jit(solution)/shard_map/ppermute | solution.py:99
  483.3 9.7 %collective-permute-done.46 = bf16[128,2816]{1,0:T(8,128)(2,1)S(1)} collective-permute-done((bf16[128,2816]{1,0:T(8,128)(2,1)S(1)}, bf16[128,2816]{1,0:T(8,128)(2,1)S(1)}, u32[]{:S(2)}, u32[]{:S(2)}) %collective-permute-start.46) | collective-permute-done | bytes 720928 | tf_op jit(solution)/shard_map/ppermute | solution.py:99
  495.8 14.6 %collective-permute-done.47 = bf16[64,2816]{1,0:T(8,128)(2,1)S(1)} collective-permute-done((bf16[64,2816]{1,0:T(8,128)(2,1)S(1)}, bf16[64,2816]{1,0:T(8,128)(2,1)S(1)}, u32[]{:S(2)}, u32[]{:S(2)}) %collective-permute-start.47) | collective-permute-done | bytes 360480 | tf_op jit(solution)/shard_map/ppermute | solution.py:99
  510.5 7.9 %collective-permute-done.37 = bf16[1600,512]{1,0:T(8,128)(2,1)S(1)} collective-permute-done((bf16[1600,512]{1,0:T(8,128)(2,1)S(1)}, bf16[1600,512]{1,0:T(8,128)(2,1)S(1)}, u32[]{:S(2)}, u32[]{:S(2)}) %collective-permute-start.37) | collective-permute-done | bytes 1638432 | tf_op jit(solution)/shard_map/ppermute | solution.py:99
  533.9 11.8 %collective-permute-done.51 = bf16[88,1024]{1,0:T(8,128)(2,1)S(1)} collective-permute-done((bf16[88,1024]{1,0:T(8,128)(2,1)S(1)}, bf16[88,1024]{1,0:T(8,128)(2,1)S(1)}, u32[]{:S(2)}, u32[]{:S(2)}) %collective-permute-start.51) | collective-permute-done | bytes 180256 | tf_op jit(solution)/shard_map/ppermute | solution.py:99
  552.3 32.4 %collective-permute-done.53 = bf16[88,1024]{1,0:T(8,128)(2,1)S(1)} collective-permute-done((bf16[88,1024]{1,0:T(8,128)(2,1)S(1)}, bf16[88,1024]{1,0:T(8,128)(2,1)S(1)}, u32[]{:S(2)}, u32[]{:S(2)}) %collective-permute-start.53) | collective-permute-done | bytes 180256 | tf_op jit(solution)/shard_map/ppermute | solution.py:99
  592.5 22.9 %collective-permute-done.55 = bf16[176,1024]{1,0:T(8,128)(2,1)S(1)} collective-permute-done((bf16[176,1024]{1,0:T(8,128)(2,1)S(1)}, bf16[176,1024]{1,0:T(8,128)(2,1)S(1)}, u32[]{:S(2)}, u32[]{:S(2)}) %collective-permute-start.55) | collective-permute-done | bytes 360480 | tf_op jit(solution)/shard_map/ppermute | solution.py:99
  615.5 21.4 %collective-permute-done.54 = bf16[200,1024]{1,0:T(8,128)(2,1)S(1)} collective-permute-done((bf16[200,1024]{1,0:T(8,128)(2,1)S(1)}, bf16[200,1024]{1,0:T(8,128)(2,1)S(1)}, u32[]{:S(2)}, u32[]{:S(2)}) %collective-permute-start.54) | collective-permute-done | bytes 409632 | tf_op jit(solution)/shard_map/ppermute | solution.py:99
  648.1 9.9 %collective-permute-done.56 = bf16[192,1024]{1,0:T(8,128)(2,1)S(1)} collective-permute-done((bf16[192,1024]{1,0:T(8,128)(2,1)S(1)}, bf16[192,1024]{1,0:T(8,128)(2,1)S(1)}, u32[]{:S(2)}, u32[]{:S(2)}) %collective-permute-start.56) | collective-permute-done | bytes 393248 | tf_op jit(solution)/shard_map/ppermute | solution.py:99
  662.4 13.4 %shard_map.409 = (f32[2,32,1024]{2,1,0:T(8,128)}, f32[2,88,2816]{2,1,0:T(8,128)}, bf16[2,88,1024]{2,1,0:T(8,128)(2,1)}) custom-call(s32[2]{0:T(128)} %pad_add_fusion.refs_0_, bf16[1024,8192]{1,0:T(8,128)(2,1)} %all-gather.6.cloned.1.call-done.refs_1_, bf16[1024,5632]{1,0:T(8,128)(2,1)} %all-gather.8.cloned.1.call-done.refs_2_, f32[2,32,2816]{2,1,0:T(8,128)} %bitcast.787, ...), custom_call_target="tpu_custom_call" | custom-call | tf_op jit(solution)/shard_map/pallas_call | solution.py:367
  700.1 6.3 all-to-all-done.6
  722.5 9.2 %shard_map.410 = (f32[1,88,2816]{2,1,0:T(8,128)}, f32[1,32,1024]{2,1,0:T(8,128)}, f32[1,88,1024]{2,1,0:T(8,128)}) custom-call(s32[2]{0:T(128)} %pad_add_fusion.refs_0_, bf16[1024,8192]{1,0:T(8,128)(2,1)} %all-gather.6.cloned.1.call-done.refs_1_, bf16[2,704,512]{2,1,0:T(8,128)(2,1)} %bitcast.752, bf16[2,704,512]{2,1,0:T(8,128)(2,1)} %bitcast.750, ...), custom_call_target="tpu_custom_call" | custom-call | tf_op jit(solution)/shard_map/pallas_call | solution.py:367
  738.2 18.1 %collective-permute-done.67 = bf16[1536,512]{1,0:T(8,128)(2,1)S(1)} collective-permute-done((bf16[1536,512]{1,0:T(8,128)(2,1)}, bf16[1536,512]{1,0:T(8,128)(2,1)S(1)}, u32[]{:S(2)}, u32[]{:S(2)}) %collective-permute-start.67) | collective-permute-done | bytes 1572896 | tf_op jit(solution)/shard_map/ppermute | solution.py:99
  768.3 13.9 %shard_map.411 = (f32[4,32,1024]{2,1,0:T(8,128)}, f32[4,32,1024]{2,1,0:T(8,128)}, f32[4,32,1024]{2,1,0:T(8,128)}, f32[1,64,2048]{2,1,0:T(8,128)}, f32[1,32,1024]{2,1,0:T(8,128)}, /*index=5*/f32[1,64,1024]{2,1,0:T(8,128)}) custom-call(s32[2]{0:T(128)} %pad_add_fusion.refs_0_, bf16[1024,8192]{1,0:T(8,128)(2,1)} %all-gather.6.cloned.1.call-done.refs_1_, ...), custom_call_target="tpu_custom_call" | custom-call | tf_op jit(solution)/shard_map/pallas_call | solution.py:367
  (697 shorter events, 435.7 us)
Async XLA Ops:
  7.2 259.1 %all-gather.4.cloned.1.call-start = ((), (), s32[]{:S(2)}) async-start(), calls=%async_computation.7 | async-start | bytes 11894784 | tf_op jit(solution)/shard_map/all_gather | solution.py:431
  29.3 312.5 %all-gather.6.cloned.1.call-start = ((), (), s32[]{:S(2)}) async-start(), calls=%async_computation.8 | async-start | bytes 17301504 | tf_op jit(solution)/shard_map/all_gather | solution.py:578
  90.2 43.3 %collective-permute-start.13 = (bf16[1024,512]{1,0:T(8,128)(2,1)S(1)}, bf16[1024,512]{1,0:T(8,128)(2,1)}, u32[]{:S(2)}, u32[]{:S(2)}) collective-permute-start(bf16[1024,512]{1,0:T(8,128)(2,1)S(1)} %bitcast.764), channel_id=1, source_target_pairs={{0,1},{1,0},{2,3},{3,2},{4,5},{5,4},{6,7},{7,6},{8,9},{9,8},{10,11... | collective-permute-start | bytes 3145736 | tf_op jit(solution)/shard_map/ppermute | solution.py:99
  91.7 45.2 %collective-permute-start.11 = (bf16[1024,512]{1,0:T(8,128)(2,1)}, bf16[1024,512]{1,0:T(8,128)(2,1)}, u32[]{:S(2)}, u32[]{:S(2)}) collective-permute-start(bf16[1024,512]{1,0:T(8,128)(2,1)} %bitcast.70), channel_id=1, source_target_pairs={{0,16},{1,17},{2,18},{3,19},{4,20},{5,21},{6,22},{7,23},{8,24},{9,... | collective-permute-start | bytes 3145736 | tf_op jit(solution)/shard_map/ppermute | solution.py:99
  189.3 44.6 %all-to-all-start = ((bf16[8,3,2,64,128]{4,3,2,1,0:T(8,128)(2,1)}), bf16[8,3,2,64,128]{4,3,2,1,0:T(8,128)(2,1)}, u32[]{:S(2)}, u32[]{:S(2)}) async-start(bf16[8,3,2,64,128]{4,3,2,1,0:T(8,128)(2,1)} %copy.276), calls=%async_computation | async-start | bytes 1572864 | tf_op jit(solution)/shard_map/all_to_all | solution.py:483
  196.0 36.0 %collective-permute-start.21 = (bf16[704,512]{1,0:T(8,128)(2,1)S(1)}, bf16[704,512]{1,0:T(8,128)(2,1)S(1)}, u32[]{:S(2)}, u32[]{:S(2)}) collective-permute-start(bf16[704,512]{1,0:T(8,128)(2,1)S(1)} %bitcast.783), channel_id=1, source_target_pairs={{0,1},{1,0},{2,3},{3,2},{4,5},{5,4},{6,7},{7,6},{8,9},{9,8},{10,11... | collective-permute-start | bytes 2162696 | tf_op jit(solution)/shard_map/ppermute | solution.py:99
  204.0 52.9 %collective-permute-start.22 = (bf16[1408,512]{1,0:T(8,128)(2,1)}, bf16[1408,512]{1,0:T(8,128)(2,1)}, u32[]{:S(2)}, u32[]{:S(2)}) collective-permute-start(bf16[1408,512]{1,0:T(8,128)(2,1)} %bitcast.156), channel_id=1, source_target_pairs={{0,8},{1,9},{2,10},{3,11},{4,12},{5,13},{6,14},{7,15},{8,0},{9,1},... | collective-permute-start | bytes 4325384 | tf_op jit(solution)/shard_map/ppermute | solution.py:99
  282.8 35.0 %all-to-all-start.2 = ((bf16[8,3,2,64,128]{4,3,2,1,0:T(8,128)(2,1)}), bf16[8,3,2,64,128]{4,3,2,1,0:T(8,128)(2,1)}, u32[]{:S(2)}, u32[]{:S(2)}) async-start(bf16[8,3,2,64,128]{4,3,2,1,0:T(8,128)(2,1)} %copy.292), calls=%async_computation.2 | async-start | bytes 1572864 | tf_op jit(solution)/shard_map/all_to_all | solution.py:483
  334.2 131.4 %collective-permute-start.34 = (bf16[128,1024]{1,0:T(8,128)(2,1)}, bf16[128,1024]{1,0:T(8,128)(2,1)}, u32[]{:S(2)}, u32[]{:S(2)}) collective-permute-start(bf16[128,1024]{1,0:T(8,128)(2,1)} %pad_maximum_fusion.12), channel_id=1, source_target_pairs={{0,8},{1,9},{2,10},{3,11},{4,12},{5,13},{6,14},{7,15},{8,0},{9,1},... | collective-permute-start | bytes 786440 | tf_op jit(solution)/shard_map/ppermute | solution.py:99
  381.4 28.3 %collective-permute-start.27 = (bf16[704,512]{1,0:T(8,128)(2,1)}, bf16[704,512]{1,0:T(8,128)(2,1)}, u32[]{:S(2)}, u32[]{:S(2)}) collective-permute-start(bf16[704,512]{1,0:T(8,128)(2,1)} %bitcast.191), channel_id=1, source_target_pairs={{0,1},{1,0},{2,3},{3,2},{4,5},{5,4},{6,7},{7,6},{8,9},{9,8},{10,11... | collective-permute-start | bytes 2162696 | tf_op jit(solution)/shard_map/ppermute | solution.py:99
  396.5 52.7 %collective-permute-start.42 = (bf16[512,1408]{1,0:T(8,128)(2,1)}, bf16[512,1408]{1,0:T(8,128)(2,1)}, u32[]{:S(2)}, u32[]{:S(2)}) collective-permute-start(bf16[512,1408]{1,0:T(8,128)(2,1)} %dynamic-slice_bitcast_fusion.1), channel_id=1, source_target_pairs={{0,16},{1,17},{2,18},{3,19},{4,20},{5,21},{6,22},{7,23},{8,24},{9,... | collective-permute-start | bytes 4325384 | tf_op jit(solution)/shard_map/ppermute | solution.py:99
  398.9 54.0 %collective-permute-start.44 = (bf16[512,1408]{1,0:T(8,128)(2,1)}, bf16[512,1408]{1,0:T(8,128)(2,1)}, u32[]{:S(2)}, u32[]{:S(2)}) collective-permute-start(bf16[512,1408]{1,0:T(8,128)(2,1)} %bitcast.238), channel_id=1, source_target_pairs={{0,1},{1,0},{2,3},{3,2},{4,5},{5,4},{6,7},{7,6},{8,9},{9,8},{10,11... | collective-permute-start | bytes 4325384 | tf_op jit(solution)/shard_map/ppermute | solution.py:99
  433.7 225.1 %all-gather.8.cloned.1.call-start = ((), (), s32[]{:S(2)}) async-start(), calls=%async_computation.9 | async-start | bytes 11894784 | tf_op jit(solution)/shard_map/all_gather | solution.py:698
  445.2 32.2 %collective-permute-start.32 = (bf16[128,512]{1,0:T(8,128)(2,1)S(1)}, bf16[128,512]{1,0:T(8,128)(2,1)}, u32[]{:S(2)}, u32[]{:S(2)}) collective-permute-start(bf16[128,512]{1,0:T(8,128)(2,1)S(1)} %copy-done.61), channel_id=1, source_target_pairs={{0,8},{1,9},{2,10},{3,11},{4,12},{5,13},{6,14},{7,15},{8,0},{9,1},... | collective-permute-start | bytes 393224 | tf_op jit(solution)/shard_map/ppermute | solution.py:99
  480.7 38.2 %collective-permute-start.38 = (bf16[1600,512]{1,0:T(8,128)(2,1)S(1)}, bf16[1600,512]{1,0:T(8,128)(2,1)S(1)}, u32[]{:S(2)}, u32[]{:S(2)}) collective-permute-start(bf16[1600,512]{1,0:T(8,128)(2,1)S(1)} %bitcast.806), channel_id=1, source_target_pairs={{0,1},{1,0},{2,3},{3,2},{4,5},{5,4},{6,7},{7,6},{8,9},{9,8},{10,11... | collective-permute-start | bytes 4915208 | tf_op jit(solution)/shard_map/ppermute | solution.py:99
  481.8 36.6 %collective-permute-start.37 = (bf16[1600,512]{1,0:T(8,128)(2,1)S(1)}, bf16[1600,512]{1,0:T(8,128)(2,1)S(1)}, u32[]{:S(2)}, u32[]{:S(2)}) collective-permute-start(bf16[1600,512]{1,0:T(8,128)(2,1)S(1)} %dynamic-slice_bitcast_fusion), channel_id=1, source_target_pairs={{0,16},{1,17},{2,18},{3,19},{4,20},{5,21},{6,22},{7,23},{8,24},{9,... | collective-permute-start | bytes 4915208 | tf_op jit(solution)/shard_map/ppermute | solution.py:99
  546.7 38.7 %collective-permute-start.52 = (bf16[400,1024]{1,0:T(8,128)(2,1)S(1)}, bf16[400,1024]{1,0:T(8,128)(2,1)S(1)}, u32[]{:S(2)}, u32[]{:S(2)}) collective-permute-start(bf16[400,1024]{1,0:T(8,128)(2,1)S(1)} %bitcast.853), channel_id=1, source_target_pairs={{0,2},{1,3},{2,0},{3,1},{4,6},{5,7},{6,4},{7,5},{8,10},{9,11},{10,... | collective-permute-start | bytes 2457608 | tf_op jit(solution)/shard_map/ppermute | solution.py:99
  548.8 35.8 %collective-permute-start.53 = (bf16[88,1024]{1,0:T(8,128)(2,1)S(1)}, bf16[88,1024]{1,0:T(8,128)(2,1)S(1)}, u32[]{:S(2)}, u32[]{:S(2)}) collective-permute-start(bf16[88,1024]{1,0:T(8,128)(2,1)S(1)} %get-tuple-element.196), channel_id=1, source_target_pairs={{0,4},{1,5},{2,6},{3,7},{4,0},{5,1},{6,2},{7,3},{8,12},{9,13},{10,... | collective-permute-start | bytes 540680 | tf_op jit(solution)/shard_map/ppermute | solution.py:99
  585.8 29.7 %collective-permute-start.55 = (bf16[176,1024]{1,0:T(8,128)(2,1)S(1)}, bf16[176,1024]{1,0:T(8,128)(2,1)S(1)}, u32[]{:S(2)}, u32[]{:S(2)}) collective-permute-start(bf16[176,1024]{1,0:T(8,128)(2,1)S(1)} %bitcast.811), channel_id=1, source_target_pairs={{0,2},{1,3},{2,0},{3,1},{4,6},{5,7},{6,4},{7,5},{8,10},{9,11},{10,... | collective-permute-start | bytes 1081352 | tf_op jit(solution)/shard_map/ppermute | solution.py:99
  590.0 46.8 %collective-permute-start.54 = (bf16[200,1024]{1,0:T(8,128)(2,1)S(1)}, bf16[200,1024]{1,0:T(8,128)(2,1)S(1)}, u32[]{:S(2)}, u32[]{:S(2)}) collective-permute-start(bf16[200,1024]{1,0:T(8,128)(2,1)S(1)} %dynamic-slice_bitcast_fusion.5), channel_id=1, source_target_pairs={{0,4},{1,5},{2,6},{3,7},{4,0},{5,1},{6,2},{7,3},{8,12},{9,13},{10,... | collective-permute-start | bytes 1228808 | tf_op jit(solution)/shard_map/ppermute | solution.py:99
  690.2 29.7 %collective-permute-start.64 = (bf16[1408,512]{1,0:T(8,128)(2,1)}, bf16[1408,512]{1,0:T(8,128)(2,1)}, u32[]{:S(2)}, u32[]{:S(2)}) collective-permute-start(bf16[1408,512]{1,0:T(8,128)(2,1)} %bitcast.751), channel_id=1, source_target_pairs={{0,8},{1,9},{2,10},{3,11},{4,12},{5,13},{6,14},{7,15},{8,0},{9,1},... | collective-permute-start | bytes 4325384 | tf_op jit(solution)/shard_map/ppermute | solution.py:99
  690.4 29.4 %collective-permute-start.65 = (bf16[1408,512]{1,0:T(8,128)(2,1)S(1)}, bf16[1408,512]{1,0:T(8,128)(2,1)}, u32[]{:S(2)}, u32[]{:S(2)}) collective-permute-start(bf16[1408,512]{1,0:T(8,128)(2,1)S(1)} %bitcast.749), channel_id=1, source_target_pairs={{0,8},{1,9},{2,10},{3,11},{4,12},{5,13},{6,14},{7,15},{8,0},{9,1},... | collective-permute-start | bytes 4325384 | tf_op jit(solution)/shard_map/ppermute | solution.py:99
  719.9 36.4 %collective-permute-start.67 = (bf16[1536,512]{1,0:T(8,128)(2,1)}, bf16[1536,512]{1,0:T(8,128)(2,1)S(1)}, u32[]{:S(2)}, u32[]{:S(2)}) collective-permute-start(bf16[1536,512]{1,0:T(8,128)(2,1)} %bitcast.304), channel_id=1, source_target_pairs={{0,1},{1,0},{2,3},{3,2},{4,5},{5,4},{6,7},{7,6},{8,9},{9,8},{10,11... | collective-permute-start | bytes 4718600 | tf_op jit(solution)/shard_map/ppermute | solution.py:99
  721.0 36.5 %collective-permute-start.66 = (bf16[1536,512]{1,0:T(8,128)(2,1)}, bf16[1536,512]{1,0:T(8,128)(2,1)S(1)}, u32[]{:S(2)}, u32[]{:S(2)}) collective-permute-start(bf16[1536,512]{1,0:T(8,128)(2,1)} %bitcast.301), channel_id=1, source_target_pairs={{0,16},{1,17},{2,18},{3,19},{4,20},{5,21},{6,22},{7,23},{8,24},{9,... | collective-permute-start | bytes 4718600 | tf_op jit(solution)/shard_map/ppermute | solution.py:99
  (150 other events, 1688.2 us)
Sparse Core Ops, SparseCore 0:
  29.4 121.6 all-gather.3
  168.7 148.5 all-gather.5
  521.4 136.8 all-gather.7

commit v5 on v4

--- a/solution.py
+++ b/solution.py
@@ -695,12 +695,7 @@
         gateup_sum.inside(step)
     tick([rest_sum, gateup_sum])
     gate_shards = (gateup_sum.parts[0] * factor).reshape(2, -1, hidden_width)
-    full_both = lax.all_gather(
-        jnp.concatenate([gate_shards[0], gate_shards[1]], axis=1).astype(BF16),
-        AXES,
-        axis=0,
-        tiled=True,
-    )
+    gate_low = jnp.concatenate([gate_shards[0], gate_shards[1]], axis=1).astype(BF16)
     for step in cross_steps[1:]:
         rest_sum.cross(step)
     for step in inner_steps:
@@ -717,7 +712,8 @@
     for step in inner_steps[1:]:
         rest_sum.inside(step)
         first.inside(step)
-    tick([rest_sum, first])
+    (gate_low,) = tick([rest_sum, first], gate_low)
+    full_both = lax.all_gather(gate_low, AXES, axis=0, tiled=True)
     reduced_rest = rest_sum.parts[0] * factor
     row_share = width // links.count
     attn_shards = reduced_rest[: 4 * row_share].reshape(4, row_share, width)
@@ -729,7 +725,7 @@
     )
     third.inside(0)
     first.cross(0)
-    (full_both,) = tick([third, first], full_both)
+    tick([third, first])
     def statistics(shard, whole, left_stat, right_stat, left_root):
         rows, columns = whole.shape
         new_left = 0.5 * left_stat + (0.5 / columns) * against(shard.astype(BF16), whole)
@@ -749,7 +745,32 @@
         third.inside(step)
     for step in cross_steps[1:]:
         first.cross(step)
+    tick([third, first])
+    first.core()
     fits = row_share % 16 == 0
+    third.cross(0)
+    tick([third, first])
+    for step in cross_steps[1:]:
+        third.cross(step)
+    if fits:
+        down_group = (
+            first.sources(),
+            reduced_down[None],
+            left_down[None],
+            right_down[None],
+            left_root_down[None],
+            weight_down[None],
+            [5],
+        )
+        ((new_left_down, new_right_down, new_down),) = shampoo(links, [down_group], root_rows)
+        new_left_down, new_right_down, new_down = new_left_down[0], new_right_down[0], new_down[0]
+    else:
+        (full_down,) = first.finish()
+        new_left_down, new_right_down, down_part = statistics(
+            reduced_down, full_down, left_down, right_down, left_root_down
+        )
+        new_down = weight_down - whole_step(down_part, 5, hidden_width)
+    full_both, new_down = tie(full_both, new_down)
     if fits:
         sources = [Source([full_both], i * hidden_width, width, hidden_width) for i in range(2)]
         ((new_left_gateup, new_right_gateup, step_columns),) = shampoo(
@@ -784,37 +805,11 @@
         new_right_gateup = jnp.stack([member[1] for member in gateup_parts])
     ff_share = step_columns.shape[2]
     step_columns = step_columns.reshape(2, links.count, row_share, ff_share).transpose(1, 0, 2, 3)
-    (step_columns,) = tick([third, first], step_columns)
-    first.core()
-    step_rows = lax.all_to_all(step_columns, AXES, 0, 0, tiled=True)
-    step_gateup = step_rows.transpose(1, 2, 0, 3).reshape(2, row_share, hidden_width)
-    new_gateup = weight_gateup - step_gateup.astype(F32) * (1.0 / math.sqrt(width))
-
-    third.cross(0)
-    (new_gateup,) = tick([third, first], new_gateup)
-    for step in cross_steps[1:]:
-        third.cross(step)
-    if fits:
-        down_group = (
-            first.sources(),
-            reduced_down[None],
-            left_down[None],
-            right_down[None],
-            left_root_down[None],
-            weight_down[None],
-            [5],
-        )
-        ((new_left_down, new_right_down, new_down),) = shampoo(links, [down_group], root_rows)
-        new_left_down, new_right_down, new_down = new_left_down[0], new_right_down[0], new_down[0]
-    else:
-        (full_down,) = first.finish()
-        new_left_down, new_right_down, down_part = statistics(
-            reduced_down, full_down, left_down, right_down, left_root_down
-        )
-        new_down = weight_down - whole_step(down_part, 5, hidden_width)
-    (new_down,) = tick([third], new_down)
+    new_down, step_columns = tick([third], new_down, step_columns)
     third.core()
     tick([third])
+    step_rows = lax.all_to_all(step_columns, AXES, 0, 0, tiled=True)
+
     grad_embedding = against(start_grad, adapt_full[width:]).reshape(
         seq_count, group_len, width
     )
@@ -864,6 +859,9 @@
             reduced_adapt, full_adapt, left_adapt, right_adapt, left_root_adapt
         )
         new_adapt = weight_adapt - whole_step(adapt_part, 0, 2 * width)
+    step_rows, new_adapt = tie(step_rows, new_adapt)
+    step_gateup = step_rows.transpose(1, 2, 0, 3).reshape(2, row_share, hidden_width)
+    new_gateup = weight_gateup - step_gateup.astype(F32) * (1.0 / math.sqrt(width))
     new_gain_moment = 0.5 * gain_moment + 0.5 * reduced_gains * reduced_gains
     new_norm_gains = norm_gains - 0.5 * reduced_gains / (jnp.sqrt(new_gain_moment) + 1e-08)
     latent_out = final_state.reshape(seq_count, group_len, width).astype(BF16)

time: 802 us -> 802 us (level)
  waiting for transfers between devices: 334 us -> 363 us
  local copies, waits for them, and re-layouts: 155 us -> 131 us
    ppermute x70, waiting for transfers between devices: 286 us -> 321 us  [swap(): return lax.ppermute(values, AXES, self.pairs[bit])]
    dynamic_update_slice x29, local copies, waits for them, and re-layouts: 21.9 us -> 13.2 us  [widen(): both = lax.dynamic_update_slice(both, mine, (0, links.own(bit), 0, 0))]
    dynamic_update_slice x31, local copies, waits for them, and re-layouts: 23.4 us -> 14.7 us  [widen(): lax.dynamic_update_slice(both, came.reshape(mine.shape), (0, 1 - links.ow...]
  transfers between devices with their start and end apart: 80 -> 80, of which waited for: 38 -> 40; matrix products, arithmetic and copies ran while one was open for 34% -> 30% of each run, Pallas kernels for 3% -> 3%
where the time goes in v5:
time: 802 us; the launch traced here: 790 us
  waiting for transfers between devices  363 us (45%)
  local copies, waits for them, and re-layouts  131 us (16%)
  starting transfers between devices  115 us (14%)
  matrix products  74.5 us (9%)
  other arithmetic  53.2 us (7%)
  Pallas kernels  36.8 us (5%)
  between operations  16.9 us (2%)
    ppermute x70, waiting for transfers between devices, swap(): return lax.ppermute(values, AXES, self.pairs[bit])  321 us
    ppermute x70, starting transfers between devices, swap(): return lax.ppermute(values, AXES, self.pairs[bit])  84.7 us
    pallas_call x3, Pallas kernels, shampoo(): pl.pallas_call(kernel, out_shape=out_shape, in_specs=[pl.BlockSpec(memory...  36.8 us
    all_to_all x3, waiting for transfers between devices, to_heads(): came = lax.all_to_all(values, 'seq', 0, 0, tiled=True)  32.1 us
    dot_general x15, matrix products, product(): return jnp.dot(left_side, right_side, preferred_element_type=F32)  28.3 us
    dynamic_update_slice x19, local copies, waits for them, and re-layouts, finish(): lax.dynamic_update_slice(whole, piece[i][:, None], (0, place, 0, 0, i % 2...  23.4 us
    dot_general x7, matrix products, against(): lax.dot_general(left_side, right_side, (((1,), (1,)), ((), ())), preferre...  17.9 us
  transfers between devices with their start and end apart: 80, of which 40 were waited for; matrix products, arithmetic and copies ran while one was open for 30% of the time, Pallas kernels for 3%

profile of v5, /device:TPU:0, one launch (start us, length us, event | category | flops | bytes accessed | tf_op | source)
XLA Modules:
  0.0 790.0 jit_solution(5652486180736119198)
XLA Ops:
  21.9 7.3 collective-permute-done.1
  37.0 11.7 %collective-permute-done.6 = bf16[128,1024]{1,0:T(8,128)(2,1)S(1)} collective-permute-done((bf16[128,1024]{1,0:T(8,128)(2,1)S(1)}, bf16[128,1024]{1,0:T(8,128)(2,1)S(1)}, u32[]{:S(2)}, u32[]{:S(2)}) %collective-permute-start.6) | collective-permute-done | bytes 262176 | tf_op jit(solution)/shard_map/ppermute | solution.py:99
  55.5 15.1 %collective-permute-done.7 = bf16[256,1024]{1,0:T(8,128)(2,1)S(1)} collective-permute-done((bf16[256,1024]{1,0:T(8,128)(2,1)S(1)}, bf16[256,1024]{1,0:T(8,128)(2,1)S(1)}, u32[]{:S(2)}, u32[]{:S(2)}) %collective-permute-start.7) | collective-permute-done | bytes 524320 | tf_op jit(solution)/shard_map/ppermute | solution.py:99
  99.9 7.3 collective-permute-done.15
  116.9 16.6 %collective-permute-done.13 = bf16[1024,512]{1,0:T(8,128)(2,1)} collective-permute-done((bf16[1024,512]{1,0:T(8,128)(2,1)S(1)}, bf16[1024,512]{1,0:T(8,128)(2,1)}, u32[]{:S(2)}, u32[]{:S(2)}) %collective-permute-start.13) | collective-permute-done | bytes 1048608 | tf_op jit(solution)/shard_map/ppermute | solution.py:99
  175.0 8.2 %collective-permute-done.18 = bf16[352,512]{1,0:T(8,128)(2,1)S(1)} collective-permute-done((bf16[352,512]{1,0:T(8,128)(2,1)S(1)}, bf16[352,512]{1,0:T(8,128)(2,1)S(1)}, u32[]{:S(2)}, u32[]{:S(2)}) %collective-permute-start.18) | collective-permute-done | bytes 360480 | tf_op jit(solution)/shard_map/ppermute | solution.py:99
  206.4 25.6 %collective-permute-done.21 = bf16[704,512]{1,0:T(8,128)(2,1)S(1)} collective-permute-done((bf16[704,512]{1,0:T(8,128)(2,1)S(1)}, bf16[704,512]{1,0:T(8,128)(2,1)S(1)}, u32[]{:S(2)}, u32[]{:S(2)}) %collective-permute-start.21) | collective-permute-done | bytes 720928 | tf_op jit(solution)/shard_map/ppermute | solution.py:99
  288.8 29.5 %all-to-all-done.2 = bf16[8,3,2,64,128]{4,3,2,1,0:T(8,128)(2,1)} async-done(((bf16[8,3,2,64,128]{4,3,2,1,0:T(8,128)(2,1)}), bf16[8,3,2,64,128]{4,3,2,1,0:T(8,128)(2,1)}, u32[]{:S(2)}, u32[]{:S(2)}) %all-to-all-start.2) | async-done | bytes 786464 | tf_op jit(solution)/shard_map/all_to_all | solution.py:483
  434.7 10.9 %collective-permute-done.29 = bf16[352,512]{1,0:T(8,128)(2,1)} collective-permute-done((bf16[352,512]{1,0:T(8,128)(2,1)}, bf16[352,512]{1,0:T(8,128)(2,1)}, u32[]{:S(2)}, u32[]{:S(2)}) %collective-permute-start.29) | collective-permute-done | bytes 360480 | tf_op jit(solution)/shard_map/ppermute | solution.py:99
  485.2 15.9 %collective-permute-done.50 = bf16[176,1024]{1,0:T(8,128)(2,1)S(1)} collective-permute-done((bf16[176,1024]{1,0:T(8,128)(2,1)S(1)}, bf16[176,1024]{1,0:T(8,128)(2,1)S(1)}, u32[]{:S(2)}, u32[]{:S(2)}) %collective-permute-start.50) | collective-permute-done | bytes 360480 | tf_op jit(solution)/shard_map/ppermute | solution.py:99
  504.6 15.4 %collective-permute-done.51 = bf16[88,1024]{1,0:T(8,128)(2,1)S(1)} collective-permute-done((bf16[88,1024]{1,0:T(8,128)(2,1)S(1)}, bf16[88,1024]{1,0:T(8,128)(2,1)S(1)}, u32[]{:S(2)}, u32[]{:S(2)}) %collective-permute-start.51) | collective-permute-done | bytes 180256 | tf_op jit(solution)/shard_map/ppermute | solution.py:99
  520.0 6.4 collective-permute-done.47
  532.0 14.7 %collective-permute-done.49 = bf16[800,512]{1,0:T(8,128)(2,1)S(1)} collective-permute-done((bf16[800,512]{1,0:T(8,128)(2,1)S(1)}, bf16[800,512]{1,0:T(8,128)(2,1)S(1)}, u32[]{:S(2)}, u32[]{:S(2)}) %collective-permute-start.49) | collective-permute-done | bytes 819232 | tf_op jit(solution)/shard_map/ppermute | solution.py:99
  559.0 14.4 %collective-permute-done.52 = bf16[400,1024]{1,0:T(8,128)(2,1)S(1)} collective-permute-done((bf16[400,1024]{1,0:T(8,128)(2,1)S(1)}, bf16[400,1024]{1,0:T(8,128)(2,1)S(1)}, u32[]{:S(2)}, u32[]{:S(2)}) %collective-permute-start.52) | collective-permute-done | bytes 819232 | tf_op jit(solution)/shard_map/ppermute | solution.py:99
  578.8 11.1 %collective-permute-done.55 = bf16[176,1024]{1,0:T(8,128)(2,1)} collective-permute-done((bf16[176,1024]{1,0:T(8,128)(2,1)S(1)}, bf16[176,1024]{1,0:T(8,128)(2,1)}, u32[]{:S(2)}, u32[]{:S(2)}) %collective-permute-start.55) | collective-permute-done | bytes 360480 | tf_op jit(solution)/shard_map/ppermute | solution.py:99
  601.7 7.8 collective-permute-done.57
  609.6 17.9 %collective-permute-done.56 = bf16[192,1024]{1,0:T(8,128)(2,1)S(1)} collective-permute-done((bf16[192,1024]{1,0:T(8,128)(2,1)S(1)}, bf16[192,1024]{1,0:T(8,128)(2,1)S(1)}, u32[]{:S(2)}, u32[]{:S(2)}) %collective-permute-start.56) | collective-permute-done | bytes 393248 | tf_op jit(solution)/shard_map/ppermute | solution.py:99
  629.3 26.6 %collective-permute-done.61 = bf16[704,512]{1,0:T(8,128)(2,1)S(1)} collective-permute-done((bf16[704,512]{1,0:T(8,128)(2,1)S(1)}, bf16[704,512]{1,0:T(8,128)(2,1)S(1)}, u32[]{:S(2)}, u32[]{:S(2)}) %collective-permute-start.61) | collective-permute-done | bytes 720928 | tf_op jit(solution)/shard_map/ppermute | solution.py:99
  656.1 6.6 collective-permute-done.59
  667.4 30.8 %collective-permute-done.62 = bf16[768,512]{1,0:T(8,128)(2,1)S(1)} collective-permute-done((bf16[768,512]{1,0:T(8,128)(2,1)S(1)}, bf16[768,512]{1,0:T(8,128)(2,1)S(1)}, u32[]{:S(2)}, u32[]{:S(2)}) %collective-permute-start.62) | collective-permute-done | bytes 786464 | tf_op jit(solution)/shard_map/ppermute | solution.py:99
  704.9 9.4 %shard_map.409 = (f32[1,88,2816]{2,1,0:T(8,128)}, f32[1,32,1024]{2,1,0:T(8,128)}, f32[1,88,1024]{2,1,0:T(8,128)}) custom-call(s32[2]{0:T(128)} %pad_add_fusion.refs_0_, bf16[1024,8192]{1,0:T(8,128)(2,1)} %all-gather.6.cloned.1.call-done.refs_1_, bf16[2,704,512]{2,1,0:T(8,128)(2,1)} %bitcast.754, bf16[2,704,512]{2,1,0:T(8,128)(2,1)} %bitcast.752, ...), custom_call_target="tpu_custom_call" | custom-call | tf_op jit(solution)/shard_map/pallas_call | solution.py:367
  720.6 16.7 %collective-permute-done.67 = bf16[1536,512]{1,0:T(8,128)(2,1)S(1)} collective-permute-done((bf16[1536,512]{1,0:T(8,128)(2,1)S(1)}, bf16[1536,512]{1,0:T(8,128)(2,1)S(1)}, u32[]{:S(2)}, u32[]{:S(2)}) %collective-permute-start.67) | collective-permute-done | bytes 1572896 | tf_op jit(solution)/shard_map/ppermute | solution.py:99
  739.8 13.5 %shard_map.410 = (f32[2,32,1024]{2,1,0:T(8,128)}, f32[2,88,2816]{2,1,0:T(8,128)}, bf16[2,88,1024]{2,1,0:T(8,128)(2,1)}) custom-call(s32[2]{0:T(128)} %pad_add_fusion.refs_0_, bf16[1024,8192]{1,0:T(8,128)(2,1)} %all-gather.6.cloned.1.call-done.refs_1_, bf16[1024,5632]{1,0:T(8,128)(2,1)} %all-gather.8.cloned.1.call-done.refs_2_, f32[2,32,2816]{2,1,0:T(8,128)} %bitcast.796, ...), custom_call_target="tpu_custom_call" | custom-call | tf_op jit(solution)/shard_map/pallas_call | solution.py:367
  766.0 13.9 %shard_map.411 = (f32[4,32,1024]{2,1,0:T(8,128)}, f32[4,32,1024]{2,1,0:T(8,128)}, f32[4,32,1024]{2,1,0:T(8,128)}, f32[1,64,2048]{2,1,0:T(8,128)}, f32[1,32,1024]{2,1,0:T(8,128)}, /*index=5*/f32[1,64,1024]{2,1,0:T(8,128)}) custom-call(s32[2]{0:T(128)} %pad_add_fusion.refs_0_, bf16[1024,8192]{1,0:T(8,128)(2,1)} %all-gather.6.cloned.1.call-done.refs_1_, ...), custom_call_target="tpu_custom_call" | custom-call | tf_op jit(solution)/shard_map/pallas_call | solution.py:367
  (701 shorter events, 420.1 us)
Async XLA Ops:
  7.2 259.4 %all-gather.4.cloned.1.call-start = ((), (), s32[]{:S(2)}) async-start(), calls=%async_computation.7 | async-start | bytes 11894784 | tf_op jit(solution)/shard_map/all_gather | solution.py:431
  29.3 313.0 %all-gather.6.cloned.1.call-start = ((), (), s32[]{:S(2)}) async-start(), calls=%async_computation.8 | async-start | bytes 17301504 | tf_op jit(solution)/shard_map/all_gather | solution.py:578
  90.2 43.3 %collective-permute-start.13 = (bf16[1024,512]{1,0:T(8,128)(2,1)S(1)}, bf16[1024,512]{1,0:T(8,128)(2,1)}, u32[]{:S(2)}, u32[]{:S(2)}) collective-permute-start(bf16[1024,512]{1,0:T(8,128)(2,1)S(1)} %bitcast.766), channel_id=1, source_target_pairs={{0,1},{1,0},{2,3},{3,2},{4,5},{5,4},{6,7},{7,6},{8,9},{9,8},{10,11... | collective-permute-start | bytes 3145736 | tf_op jit(solution)/shard_map/ppermute | solution.py:99
  91.8 45.2 %collective-permute-start.11 = (bf16[1024,512]{1,0:T(8,128)(2,1)}, bf16[1024,512]{1,0:T(8,128)(2,1)}, u32[]{:S(2)}, u32[]{:S(2)}) collective-permute-start(bf16[1024,512]{1,0:T(8,128)(2,1)} %bitcast.70), channel_id=1, source_target_pairs={{0,16},{1,17},{2,18},{3,19},{4,20},{5,21},{6,22},{7,23},{8,24},{9,... | collective-permute-start | bytes 3145736 | tf_op jit(solution)/shard_map/ppermute | solution.py:99
  189.5 44.4 %all-to-all-start = ((bf16[8,3,2,64,128]{4,3,2,1,0:T(8,128)(2,1)}), bf16[8,3,2,64,128]{4,3,2,1,0:T(8,128)(2,1)}, u32[]{:S(2)}, u32[]{:S(2)}) async-start(bf16[8,3,2,64,128]{4,3,2,1,0:T(8,128)(2,1)} %copy.276), calls=%async_computation | async-start | bytes 1572864 | tf_op jit(solution)/shard_map/all_to_all | solution.py:483
  196.2 35.7 %collective-permute-start.21 = (bf16[704,512]{1,0:T(8,128)(2,1)S(1)}, bf16[704,512]{1,0:T(8,128)(2,1)S(1)}, u32[]{:S(2)}, u32[]{:S(2)}) collective-permute-start(bf16[704,512]{1,0:T(8,128)(2,1)S(1)} %bitcast.790), channel_id=1, source_target_pairs={{0,1},{1,0},{2,3},{3,2},{4,5},{5,4},{6,7},{7,6},{8,9},{9,8},{10,11... | collective-permute-start | bytes 2162696 | tf_op jit(solution)/shard_map/ppermute | solution.py:99
  204.2 53.0 %collective-permute-start.22 = (bf16[1408,512]{1,0:T(8,128)(2,1)}, bf16[1408,512]{1,0:T(8,128)(2,1)}, u32[]{:S(2)}, u32[]{:S(2)}) collective-permute-start(bf16[1408,512]{1,0:T(8,128)(2,1)} %bitcast.156), channel_id=1, source_target_pairs={{0,8},{1,9},{2,10},{3,11},{4,12},{5,13},{6,14},{7,15},{8,0},{9,1},... | collective-permute-start | bytes 4325384 | tf_op jit(solution)/shard_map/ppermute | solution.py:99
  283.1 35.1 %all-to-all-start.2 = ((bf16[8,3,2,64,128]{4,3,2,1,0:T(8,128)(2,1)}), bf16[8,3,2,64,128]{4,3,2,1,0:T(8,128)(2,1)}, u32[]{:S(2)}, u32[]{:S(2)}) async-start(bf16[8,3,2,64,128]{4,3,2,1,0:T(8,128)(2,1)} %copy.292), calls=%async_computation.2 | async-start | bytes 1572864 | tf_op jit(solution)/shard_map/all_to_all | solution.py:483
  334.6 131.5 %collective-permute-start.34 = (bf16[128,1024]{1,0:T(8,128)(2,1)}, bf16[128,1024]{1,0:T(8,128)(2,1)}, u32[]{:S(2)}, u32[]{:S(2)}) collective-permute-start(bf16[128,1024]{1,0:T(8,128)(2,1)} %pad_maximum_fusion.12), channel_id=1, source_target_pairs={{0,8},{1,9},{2,10},{3,11},{4,12},{5,13},{6,14},{7,15},{8,0},{9,1},... | collective-permute-start | bytes 786440 | tf_op jit(solution)/shard_map/ppermute | solution.py:99
  381.8 28.3 %collective-permute-start.27 = (bf16[704,512]{1,0:T(8,128)(2,1)}, bf16[704,512]{1,0:T(8,128)(2,1)}, u32[]{:S(2)}, u32[]{:S(2)}) collective-permute-start(bf16[704,512]{1,0:T(8,128)(2,1)} %bitcast.191), channel_id=1, source_target_pairs={{0,1},{1,0},{2,3},{3,2},{4,5},{5,4},{6,7},{7,6},{8,9},{9,8},{10,11... | collective-permute-start | bytes 2162696 | tf_op jit(solution)/shard_map/ppermute | solution.py:99
  397.0 52.6 %collective-permute-start.42 = (bf16[512,1408]{1,0:T(8,128)(2,1)}, bf16[512,1408]{1,0:T(8,128)(2,1)}, u32[]{:S(2)}, u32[]{:S(2)}) collective-permute-start(bf16[512,1408]{1,0:T(8,128)(2,1)} %dynamic-slice_bitcast_fusion.1), channel_id=1, source_target_pairs={{0,16},{1,17},{2,18},{3,19},{4,20},{5,21},{6,22},{7,23},{8,24},{9,... | collective-permute-start | bytes 4325384 | tf_op jit(solution)/shard_map/ppermute | solution.py:99
  399.2 54.1 %collective-permute-start.44 = (bf16[512,1408]{1,0:T(8,128)(2,1)}, bf16[512,1408]{1,0:T(8,128)(2,1)}, u32[]{:S(2)}, u32[]{:S(2)}) collective-permute-start(bf16[512,1408]{1,0:T(8,128)(2,1)} %bitcast.238), channel_id=1, source_target_pairs={{0,1},{1,0},{2,3},{3,2},{4,5},{5,4},{6,7},{7,6},{8,9},{9,8},{10,11... | collective-permute-start | bytes 4325384 | tf_op jit(solution)/shard_map/ppermute | solution.py:99
  434.2 305.6 %all-gather.8.cloned.1.call-start = ((), (), s32[]{:S(2)}) async-start(), calls=%async_computation.9 | async-start | bytes 11894784 | tf_op jit(solution)/shard_map/all_gather | solution.py:716
  445.5 32.2 %collective-permute-start.32 = (bf16[128,512]{1,0:T(8,128)(2,1)S(1)}, bf16[128,512]{1,0:T(8,128)(2,1)}, u32[]{:S(2)}, u32[]{:S(2)}) collective-permute-start(bf16[128,512]{1,0:T(8,128)(2,1)S(1)} %copy-done.63), channel_id=1, source_target_pairs={{0,8},{1,9},{2,10},{3,11},{4,12},{5,13},{6,14},{7,15},{8,0},{9,1},... | collective-permute-start | bytes 393224 | tf_op jit(solution)/shard_map/ppermute | solution.py:99
  482.4 44.6 %collective-permute-start.38 = (bf16[1600,512]{1,0:T(8,128)(2,1)S(1)}, bf16[1600,512]{1,0:T(8,128)(2,1)S(1)}, u32[]{:S(2)}, u32[]{:S(2)}) collective-permute-start(bf16[1600,512]{1,0:T(8,128)(2,1)S(1)} %bitcast.815), channel_id=1, source_target_pairs={{0,1},{1,0},{2,3},{3,2},{4,5},{5,4},{6,7},{7,6},{8,9},{9,8},{10,11... | collective-permute-start | bytes 4915208 | tf_op jit(solution)/shard_map/ppermute | solution.py:99
  483.5 43.0 %collective-permute-start.37 = (bf16[1600,512]{1,0:T(8,128)(2,1)S(1)}, bf16[1600,512]{1,0:T(8,128)(2,1)S(1)}, u32[]{:S(2)}, u32[]{:S(2)}) collective-permute-start(bf16[1600,512]{1,0:T(8,128)(2,1)S(1)} %dynamic-slice_bitcast_fusion), channel_id=1, source_target_pairs={{0,16},{1,17},{2,18},{3,19},{4,20},{5,21},{6,22},{7,23},{8,24},{9,... | collective-permute-start | bytes 4915208 | tf_op jit(solution)/shard_map/ppermute | solution.py:99
  627.5 28.4 %collective-permute-start.61 = (bf16[704,512]{1,0:T(8,128)(2,1)S(1)}, bf16[704,512]{1,0:T(8,128)(2,1)S(1)}, u32[]{:S(2)}, u32[]{:S(2)}) collective-permute-start(bf16[704,512]{1,0:T(8,128)(2,1)S(1)} %bitcast.792), channel_id=1, source_target_pairs={{0,1},{1,0},{2,3},{3,2},{4,5},{5,4},{6,7},{7,6},{8,9},{9,8},{10,11... | collective-permute-start | bytes 2162696 | tf_op jit(solution)/shard_map/ppermute | solution.py:99
  628.6 34.0 %collective-permute-start.59 = (bf16[384,1024]{1,0:T(8,128)(2,1)S(1)}, bf16[384,1024]{1,0:T(8,128)(2,1)S(1)}, u32[]{:S(2)}, u32[]{:S(2)}) collective-permute-start(bf16[384,1024]{1,0:T(8,128)(2,1)S(1)} %bitcast.776), channel_id=1, source_target_pairs={{0,2},{1,3},{2,0},{3,1},{4,6},{5,7},{6,4},{7,5},{8,10},{9,11},{10,... | collective-permute-start | bytes 2359304 | tf_op jit(solution)/shard_map/ppermute | solution.py:99
  662.7 38.0 %collective-permute-start.64 = (bf16[1408,512]{1,0:T(8,128)(2,1)S(1)}, bf16[1408,512]{1,0:T(8,128)(2,1)S(1)}, u32[]{:S(2)}, u32[]{:S(2)}) collective-permute-start(bf16[1408,512]{1,0:T(8,128)(2,1)S(1)} %bitcast.753), channel_id=1, source_target_pairs={{0,8},{1,9},{2,10},{3,11},{4,12},{5,13},{6,14},{7,15},{8,0},{9,1},... | collective-permute-start | bytes 4325384 | tf_op jit(solution)/shard_map/ppermute | solution.py:99
  662.8 38.0 %collective-permute-start.65 = (bf16[1408,512]{1,0:T(8,128)(2,1)S(1)}, bf16[1408,512]{1,0:T(8,128)(2,1)S(1)}, u32[]{:S(2)}, u32[]{:S(2)}) collective-permute-start(bf16[1408,512]{1,0:T(8,128)(2,1)S(1)} %bitcast.751), channel_id=1, source_target_pairs={{0,8},{1,9},{2,10},{3,11},{4,12},{5,13},{6,14},{7,15},{8,0},{9,1},... | collective-permute-start | bytes 4325384 | tf_op jit(solution)/shard_map/ppermute | solution.py:99
  663.5 34.7 %collective-permute-start.62 = (bf16[768,512]{1,0:T(8,128)(2,1)S(1)}, bf16[768,512]{1,0:T(8,128)(2,1)S(1)}, u32[]{:S(2)}, u32[]{:S(2)}) collective-permute-start(bf16[768,512]{1,0:T(8,128)(2,1)S(1)} %get-tuple-element.239), channel_id=1, source_target_pairs={{0,1},{1,0},{2,3},{3,2},{4,5},{5,4},{6,7},{7,6},{8,9},{9,8},{10,11... | collective-permute-start | bytes 2359304 | tf_op jit(solution)/shard_map/ppermute | solution.py:99
  665.1 35.6 %collective-permute-start.63 = (bf16[768,512]{1,0:T(8,128)(2,1)S(1)}, bf16[768,512]{1,0:T(8,128)(2,1)S(1)}, u32[]{:S(2)}, u32[]{:S(2)}) collective-permute-start(bf16[768,512]{1,0:T(8,128)(2,1)S(1)} %get-tuple-element.238), channel_id=1, source_target_pairs={{0,16},{1,17},{2,18},{3,19},{4,20},{5,21},{6,22},{7,23},{8,24},{9,... | collective-permute-start | bytes 2359304 | tf_op jit(solution)/shard_map/ppermute | solution.py:99
  700.8 36.5 %collective-permute-start.67 = (bf16[1536,512]{1,0:T(8,128)(2,1)S(1)}, bf16[1536,512]{1,0:T(8,128)(2,1)S(1)}, u32[]{:S(2)}, u32[]{:S(2)}) collective-permute-start(bf16[1536,512]{1,0:T(8,128)(2,1)S(1)} %bitcast.743), channel_id=1, source_target_pairs={{0,1},{1,0},{2,3},{3,2},{4,5},{5,4},{6,7},{7,6},{8,9},{9,8},{10,11... | collective-permute-start | bytes 4718600 | tf_op jit(solution)/shard_map/ppermute | solution.py:99
  700.9 37.7 %collective-permute-start.66 = (bf16[1536,512]{1,0:T(8,128)(2,1)S(1)}, bf16[1536,512]{1,0:T(8,128)(2,1)S(1)}, u32[]{:S(2)}, u32[]{:S(2)}) collective-permute-start(bf16[1536,512]{1,0:T(8,128)(2,1)S(1)} %bitcast.741), channel_id=1, source_target_pairs={{0,16},{1,17},{2,18},{3,19},{4,20},{5,21},{6,22},{7,23},{8,24},{9,... | collective-permute-start | bytes 4718600 | tf_op jit(solution)/shard_map/ppermute | solution.py:99
  (152 other events, 1703.5 us)
Sparse Core Ops, SparseCore 0:
  29.4 121.6 all-gather.3
  168.9 148.8 all-gather.5
  596.8 126.9 all-gather.7
